TPU v7x, 32 devices: a whole 2x2x4 slice. The times are simulated.
32 devices in a mesh: tile: 8 (over y, x, core), comp: 4 (over z).
Axes of the slice: x: 2, y: 2, z: 4, core: 2. Of those that a mesh axis runs over, the one named last changes fastest.
Arguments:
- spectrum: bfloat16 [768, 64, 1024], P('comp', 'tile'), may hold values from 0.049804688 to 2
- sea_mask: int32 [64, 1024], P('tile'), may hold values 0 or 1
- depth_class: int32 [64, 1024], P('tile'), may hold values from 0 to 15
- group_speed: float32 [16, 32], replicated, may hold values from 0.2 to 0.45
- wind_speed: float32 [64, 1024], P('tile'), may hold values from 2 to 20
- wind_dir: float32 [64, 1024], P('tile'), may hold values from -3.140625 to 3.140625
- coupling: bfloat16 [768, 768], replicated, may hold values from -0.21875 to 0.21875
Outputs:
- spectrum_next: bfloat16 [768, 64, 1024], P('comp', 'tile')
All inputs are finite; a program needn't handle non-finite values. No bound on the sum of `sea_mask` on one device may be relied on, other than what follows from the above.
Results may differ from a plain program's by a relative error of at most 0.002.
The roundings to bfloat16 on the way count: a program that leaves them out, or rounds other values in their place, can miss the bound.
Values may be sent and summed in bfloat16 or wider, within the bound.
No kernel may reach another device: no remote copies, remote signals or barrier semaphores. Data moves between devices by JAX's collectives and lax.ppermute only.
A program may use at most 64 MiB of HBM per device.

v0:
```python
import math

import jax
import jax.numpy as jnp
from jax import lax
from jax.sharding import PartitionSpec as P

K = 24
F = 32
DEPTHS = 16
PSTEPS = 4
SRC_STEPS = 4


def padded_2(block, sides, width):
    for axis, dim in sides:
        count = lax.axis_size(axis)
        forward = [(i, i + 1) for i in range(count - 1)]
        forward.append((count - 1, 0))
        backward = [(target, source) for source, target in forward]
        low = lax.ppermute(
            lax.slice_in_dim(block, block.shape[dim] - width, None, axis=dim), axis, forward
        )
        high = lax.ppermute(lax.slice_in_dim(block, 0, width, axis=dim), axis, backward)
        block = jnp.concatenate([low, block, high], axis=dim)
    return block


def sources(spectra, speed, direction, coupling, freq_index, theta):
    state = spectra.astype(jnp.float32)
    weight = (0.1 * jnp.power(1.1, freq_index))[:, None]
    align = jnp.maximum(jnp.cos(theta[:, None] - direction[None, :]), 0.0)
    grow = (0.004 * jnp.power(1.1, freq_index - 16.0))[:, None] * speed[None, :] * align
    freq_rate = ((freq_index + 1.0) / F)[:, None]
    for step in range(SRC_STEPS):
        total = jnp.sum(weight * state, axis=0)
        sat = total / (total + 100.0)
        nonlin = jnp.dot(coupling, state.astype(jnp.bfloat16), preferred_element_type=jnp.float32)
        state = jnp.maximum(
            state + 0.5 * ((grow - 0.3 * sat[None, :] * freq_rate) * state + 0.25 * nonlin), 0.0
        )
    return state.astype(jnp.bfloat16)


def point_update(block, speed, direction, coupling):
    whole = block.shape[0]
    comp_index = jnp.arange(whole)
    freq_index = (comp_index // K).astype(jnp.float32)
    theta = (comp_index % K).astype(jnp.float32) * (2.0 * math.pi / K)
    flat = block.reshape(whole, -1)
    result = sources(flat, speed.reshape(-1), direction.reshape(-1), coupling, freq_index, theta)
    return result.reshape(block.shape)


def courants(depth_field, table, theta):
    depth_onehot = (depth_field[None] == jnp.arange(DEPTHS)[:, None, None]).astype(jnp.float32)
    speed = jnp.einsum("cd,dxy->cxy", table, depth_onehot, precision=lax.Precision.HIGHEST)
    return (speed * jnp.cos(theta)[:, None, None], speed * jnp.sin(theta)[:, None, None])


def upwind(energy, west_side, east_side, courant_x, courant_y, sea):
    ypad = jnp.pad(energy, ((0, 0), (0, 0), (1, 1)))
    south_side = ypad[:, :, :-2]
    north_side = ypad[:, :, 2:]
    return (
        energy
        - jnp.maximum(courant_x, 0.0) * (energy - west_side)
        - jnp.minimum(courant_x, 0.0) * (east_side - energy)
        - jnp.maximum(courant_y, 0.0) * (energy - south_side)
        - jnp.minimum(courant_y, 0.0) * (north_side - energy)
    ) * sea


def on_device(spectrum, sea_mask, depth_class, group_speed, wind_speed, wind_dir, coupling):
    local_comps, columns, rows = spectrum.shape
    comp_devices = lax.axis_size("comp")
    base = lax.axis_index("comp") * local_comps
    comp_index = base + jnp.arange(local_comps)
    freq_index = comp_index // K
    theta = (comp_index % K).astype(jnp.float32) * (2.0 * math.pi / K)
    freq_select = (freq_index[:, None] == jnp.arange(F)[None, :]).astype(jnp.float32)
    table = jnp.dot(freq_select, group_speed.T, precision=lax.Precision.HIGHEST)
    courant_x, courant_y = courants(depth_class, table, theta)
    sea = sea_mask.astype(jnp.float32)[None]
    energy = spectrum.astype(jnp.float32)
    for step in range(PSTEPS):
        padded = padded_2(energy, (("tile", 1),), 1)
        energy = upwind(energy, padded[:, :-2], padded[:, 2:], courant_x, courant_y, sea)
    propagated = energy.astype(jnp.bfloat16)
    point_rows = rows // comp_devices
    start = lax.axis_index("comp") * point_rows
    speed_part = lax.dynamic_slice_in_dim(wind_speed, start, point_rows, 1)
    dir_part = lax.dynamic_slice_in_dim(wind_dir, start, point_rows, 1)
    at_points = lax.all_to_all(propagated, "comp", split_axis=2, concat_axis=0, tiled=True)
    updated = point_update(at_points, speed_part, dir_part, coupling)
    return lax.all_to_all(updated, "comp", split_axis=0, concat_axis=2, tiled=True)


def solution(mesh):
    placed = (
        P("comp", "tile", None),
        P("tile", None),
        P("tile", None),
        P(),
        P("tile", None),
        P("tile", None),
        P(),
    )
    return jax.shard_map(
        on_device, mesh=mesh, in_specs=placed, out_specs=P("comp", "tile", None), check_vma=False
    )
```

profile of v0, /device:TPU:8, one launch (start us, length us, event | category | flops | bytes accessed | tf_op | source)
XLA Modules:
  0.0 439.9 jit_solution(8980960000333486228)
XLA Ops:
  0.0 0.0 copy-start
  0.0 0.0 copy-start.2
  0.0 0.0 copy-start.4
  0.0 0.0 copy-start.3
  0.0 3.8 copy_convert_fusion
  3.8 0.0 copy-start.1
  3.8 2.6 copy-done.1
  6.5 0.1 fusion.91
  6.6 0.1 collective-permute-start
  6.7 2.6 collective-permute-start.1
  9.3 0.0 copy-done.2
  9.3 0.1 fusion.86
  9.4 0.0 copy-done.4
  9.4 0.2 convolution_bitcast_fusion
  9.6 16.0 %collective-permute-done = f32[192,1,1024]{2,0,1:T(8,128)} collective-permute-done((f32[192,1,1024]{2,0,1:T(8,128)S(1)}, f32[192,1,1024]{2,0,1:T(8,128)}, u32[]{:S(2)}, u32[]{:S(2)}) %collective-permute-start) | collective-permute-done | bytes 786464 | tf_op jit(solution)/shard_map/ppermute | solution.py:21
  25.6 0.0 collective-permute-done.1
  25.6 0.0 copy-done.3
  25.6 15.9 %fusion.26 = (f32[192,8,1024]{2,0,1:T(8,128)}, f32[192,8,1024]{2,0,1:T(8,128)S(1)}) fusion(f32[192,8,1024]{2,0,1:T(8,128)} %copy-done.1, f32[192,1,1024]{2,0,1:T(8,128)} %collective-permute-done.1, f32[192,1,1024]{2,0,1:T(8,128)} %collective-permute-done, f32[8,1024]{1,0:T(8,128)S(1)} %convert_element_type.84, f32[192]{0:T(256)S(1)} %get-tuple-element.21, ...), kind=kOutput, calls=%fused_computation.41 | convolution fusion | flops 336723968 | bytes 23672320 | tf_op jit(solution)/shard_map/cd,dxy->cxy/dot_general | solution.py:57
  41.5 1.5 fusion.90
  42.9 1.8 collective-permute-start.2
  44.8 1.1 collective-permute-start.3
  45.9 16.8 %collective-permute-done.2 = f32[192,1,1024]{2,0,1:T(8,128)S(1)} collective-permute-done((f32[192,1,1024]{2,0,1:T(8,128)S(1)}, f32[192,1,1024]{2,0,1:T(8,128)S(1)}, u32[]{:S(2)}, u32[]{:S(2)}) %collective-permute-start.2) | collective-permute-done | bytes 786464 | tf_op jit(solution)/shard_map/ppermute | solution.py:21
  62.7 0.0 collective-permute-done.3
  62.7 12.8 %fusion.4 = f32[192,8,1024]{2,0,1:T(8,128)S(1)} fusion(f32[192,8,1024]{2,0,1:T(8,128)} %get-tuple-element.13, f32[192,1,1024]{2,0,1:T(8,128)S(1)} %collective-permute-done.3, f32[192,1,1024]{2,0,1:T(8,128)S(1)} %collective-permute-done.2, f32[192,8,1024]{2,0,1:T(8,128)S(1)} %get-tuple-element.14, f32[8,1024]{1,0:T(8,128)S(1)} %convert_element_type.84, ...), kind=kLoop, calls=%fused_computation.19 | loop fusion | flops 33030144 | bytes 20481536 | tf_op jit(solution)/shard_map/mul | solution.py:65
  75.5 0.2 fusion.89
  75.7 2.0 collective-permute-start.4
  77.7 0.7 collective-permute-start.5
  78.4 17.5 %collective-permute-done.4 = f32[192,1,1024]{2,0,1:T(8,128)S(1)} collective-permute-done((f32[192,1,1024]{2,0,1:T(8,128)S(1)}, f32[192,1,1024]{2,0,1:T(8,128)S(1)}, u32[]{:S(2)}, u32[]{:S(2)}) %collective-permute-start.4) | collective-permute-done | bytes 786464 | tf_op jit(solution)/shard_map/ppermute | solution.py:21
  95.9 0.0 collective-permute-done.5
  95.9 6.2 %fusion.11 = f32[192,8,1024]{2,0,1:T(8,128)S(1)} fusion(f32[192,8,1024]{2,0,1:T(8,128)S(1)} %fusion.4, f32[192,1,1024]{2,0,1:T(8,128)S(1)} %collective-permute-done.5, f32[192,1,1024]{2,0,1:T(8,128)S(1)} %collective-permute-done.4, f32[192,8,1024]{2,0,1:T(8,128)S(1)} %get-tuple-element.14, f32[8,1024]{1,0:T(8,128)S(1)} %convert_element_type.84, ...), kind=kLoop, calls=%fused_computation.26 | loop fusion | flops 33030144 | bytes 20481536 | tf_op jit(solution)/shard_map/mul | solution.py:65
  102.1 0.2 fusion.88
  102.3 0.9 collective-permute-start.6
  103.2 1.8 collective-permute-start.7
  105.0 17.8 %collective-permute-done.6 = f32[192,1,1024]{2,0,1:T(8,128)S(1)} collective-permute-done((f32[192,1,1024]{2,0,1:T(8,128)S(1)}, f32[192,1,1024]{2,0,1:T(8,128)S(1)}, u32[]{:S(2)}, u32[]{:S(2)}) %collective-permute-start.6) | collective-permute-done | bytes 786464 | tf_op jit(solution)/shard_map/ppermute | solution.py:21
  122.8 0.0 collective-permute-done.7
  122.8 7.6 %fusion.19 = bf16[192,8,1024]{2,0,1:T(8,128)(2,1)} fusion(f32[192,8,1024]{2,0,1:T(8,128)S(1)} %fusion.11, f32[192,1,1024]{2,0,1:T(8,128)S(1)} %collective-permute-done.7, f32[192,1,1024]{2,0,1:T(8,128)S(1)} %collective-permute-done.6, f32[192,8,1024]{2,0,1:T(8,128)S(1)} %get-tuple-element.14, f32[8,1024]{1,0:T(8,128)S(1)} %convert_element_type.84, ...), kind=kLoop, calls=%fused_computation.34 | loop fusion | flops 34603008 | bytes 17335808 | tf_op jit(solution)/shard_map/convert_element_type | solution.py:89
  130.3 6.9 %copy.21 = bf16[192,8,1024]{0,1,2:T(8,128)(2,1)} copy(bf16[192,8,1024]{2,0,1:T(8,128)(2,1)} %fusion.19) | data formatting | bytes 6291456 | tf_op jit(solution)/shard_map/convert_element_type | solution.py:89
  137.2 6.1 %all-to-all-start = ((bf16[192,8,1024]{0,1,2:T(8,128)(2,1)}), bf16[192,8,1024]{0,1,2:T(8,128)(2,1)}, u32[]{:S(2)}, u32[]{:S(2)}) async-start(bf16[192,8,1024]{0,1,2:T(8,128)(2,1)} %copy.21), calls=%async_computation | async-start | bytes 8388608 | tf_op jit(solution)/shard_map/all_to_all | solution.py:94
  143.4 0.7 dynamic-slice_bitcast_fusion
  144.2 87.8 %all-to-all-done = bf16[192,8,1024]{0,1,2:T(8,128)(2,1)} async-done(((bf16[192,8,1024]{0,1,2:T(8,128)(2,1)}), bf16[192,8,1024]{0,1,2:T(8,128)(2,1)}, u32[]{:S(2)}, u32[]{:S(2)}) %all-to-all-start) | async-done | bytes 3145760 | tf_op jit(solution)/shard_map/all_to_all | solution.py:94
  232.0 8.2 %copy.22 = bf16[192,8,4,256]{3,1,0,2:T(8,128)(2,1)} copy(bf16[192,8,4,256]{0,1,3,2:T(8,128)(2,1)} %bitcast.1) | data formatting | bytes 6291456 | tf_op jit(solution)/shard_map/all_to_all | solution.py:94
  240.2 4.6 %copy.27 = bf16[96,8,8,256]{3,1,2,0:T(8,128)(2,1)} copy(bf16[96,8,8,256]{3,2,1,0:T(8,128)(2,1)} %bitcast.57) | data formatting | bytes 6291456
  244.8 4.7 %copy.23 = bf16[768,2048]{0,1:T(8,128)(2,1)} copy(bf16[768,2048]{1,0:T(8,128)(2,1)} %bitcast.58) | data formatting | bytes 6291456 | tf_op jit(solution)/shard_map/reshape | solution.py:50
  249.5 2.4 multiply_reduce_fusion.3
  251.9 0.0 copy-done
  251.9 29.2 %multiply_reduce_fusion.2 = (f32[2048]{0:T(1024)S(1)}, f32[768,2048]{0,1:T(8,128)S(1)}) fusion(f32[768]{0:T(1024)S(1)} %get-tuple-element.26, bf16[768,2048]{1,0:T(8,128)(2,1)} %bitcast.59, bf16[768,768]{1,0:T(8,128)(2,1)S(1)} %copy-done, f32[768]{0:T(1024)S(1)} %get-tuple-element.27, f32[2048]{0:T(1024)S(1)} %fusion.67, f32[2048]{0:T(1024)S(1)} %bitcast.68, ...), kind=kOutput, calls=%fused_computation.89 | convolution fusion | flops 2439510016 | bytes 13807616 | tf_op jit(solution)/shard_map/dot_general | solution.py:38
  281.1 25.0 %multiply_reduce_fusion.1 = (f32[2048]{0:T(1024)S(1)}, f32[768,2048]{0,1:T(8,128)S(1)}) fusion(f32[768]{0:T(1024)S(1)} %get-tuple-element.26, f32[768,2048]{0,1:T(8,128)S(1)} %get-tuple-element.16, bf16[768,768]{1,0:T(8,128)(2,1)S(1)} %copy-done, f32[768]{0:T(1024)S(1)} %get-tuple-element.27, f32[2048]{0:T(1024)S(1)} %fusion.68, f32[2048]{0:T(1024)S(1)} %bitcast.69, ...), kind=kOutput, calls=%fused_computation.88 | convolution fusion | flops 2439510016 | bytes 13807616 | tf_op jit(solution)/shard_map/dot_general | solution.py:38
  306.1 25.2 %multiply_reduce_fusion = (f32[2048]{0:T(1024)S(1)}, f32[768,2048]{0,1:T(8,128)S(1)}) fusion(f32[768]{0:T(1024)S(1)} %get-tuple-element.26, f32[768,2048]{0,1:T(8,128)S(1)} %get-tuple-element.18, bf16[768,768]{1,0:T(8,128)(2,1)S(1)} %copy-done, f32[768]{0:T(1024)S(1)} %get-tuple-element.27, f32[2048]{0:T(1024)S(1)} %fusion.69, f32[2048]{0:T(1024)S(1)} %bitcast.70, ...), kind=kOutput, calls=%fused_computation.87 | convolution fusion | flops 2439510016 | bytes 13807616 | tf_op jit(solution)/shard_map/dot_general | solution.py:38
  331.3 26.0 %fusion.54 = bf16[768,2048]{0,1:T(8,128)(2,1)} fusion(f32[768,2048]{0,1:T(8,128)S(1)} %get-tuple-element.20, bf16[768,768]{1,0:T(8,128)(2,1)S(1)} %copy-done, f32[2048]{0:T(1024)S(1)} %fusion.70, f32[768]{0:T(1024)S(1)} %get-tuple-element.27, f32[2048]{0:T(1024)S(1)} %bitcast.71, f32[768]{0:T(1024)S(1)} %get-tuple-element.25, f32[2048]{0:T(1024)S(1)} %bitcast.67, ...), kind=kOutput, calls=%fused_computation.78 | convolution fusion | flops 2437939200 | bytes 10650624 | tf_op jit(solution)/shard_map/dot_general | solution.py:38
  357.3 5.1 %copy.24 = bf16[768,8,256]{2,1,0:T(8,128)(2,1)} copy(bf16[768,8,256]{0,2,1:T(8,128)(2,1)} %bitcast.61) | data formatting | bytes 6291456 | tf_op jit(solution)/shard_map/reshape | solution.py:52
  362.4 75.4 %all_to_all.33 = bf16[768,8,256]{2,1,0:T(8,128)(2,1)S(1)} all-to-all(bf16[768,8,256]{2,1,0:T(8,128)(2,1)} %copy.24), channel_id=1, replica_groups=mesh['tile'=8,'comp'=4] {'comp'}, dimensions={0} | all-to-all | bytes 6291456 | tf_op jit(solution)/shard_map/all_to_all | solution.py:96
  437.8 2.1 copy.26
  (12 shorter events, 0.1 us)
Async XLA Ops:
  0.0 251.9 %copy-start = (bf16[768,768]{1,0:T(8,128)(2,1)S(1)}, bf16[768,768]{1,0:T(8,128)(2,1)}, u32[]{:S(2)}) copy-start(bf16[768,768]{1,0:T(8,128)(2,1)} %param.13) | copy-start | bytes 3538948
  0.0 9.3 %copy-start.2 = (s32[8,1024]{1,0:T(8,128)S(1)}, s32[8,1024]{1,0:T(8,128)}, u32[]{:S(2)}) copy-start(s32[8,1024]{1,0:T(8,128)} %param.8) | copy-start | bytes 98308
  0.0 9.4 %copy-start.4 = (f32[16,32]{1,0:T(8,128)S(1)}, f32[16,32]{1,0:T(8,128)}, u32[]{:S(2)}) copy-start(f32[16,32]{1,0:T(8,128)} %param.10) | copy-start | bytes 6148
  0.0 25.6 %copy-start.3 = (s32[8,1024]{1,0:T(8,128)S(1)}, s32[8,1024]{1,0:T(8,128)}, u32[]{:S(2)}) copy-start(s32[8,1024]{1,0:T(8,128)} %param.9) | copy-start | bytes 98308
  3.8 2.7 copy-start.1
  6.6 19.0 %collective-permute-start = (f32[192,1,1024]{2,0,1:T(8,128)S(1)}, f32[192,1,1024]{2,0,1:T(8,128)}, u32[]{:S(2)}, u32[]{:S(2)}) collective-permute-start(f32[192,1,1024]{2,0,1:T(8,128)S(1)} %get-tuple-element.11), channel_id=1, source_target_pairs={{0,4},{4,8},{8,12},{12,16},{16,20},{20,24},{24,28},{28,0},{1,5},{5... | collective-permute-start | bytes 2359304 | tf_op jit(solution)/shard_map/ppermute | solution.py:21
  6.7 18.9 %collective-permute-start.1 = (f32[192,1,1024]{2,0,1:T(8,128)S(1)}, f32[192,1,1024]{2,0,1:T(8,128)}, u32[]{:S(2)}, u32[]{:S(2)}) collective-permute-start(f32[192,1,1024]{2,0,1:T(8,128)S(1)} %get-tuple-element.12), channel_id=1, source_target_pairs={{4,0},{8,4},{12,8},{16,12},{20,16},{24,20},{28,24},{0,28},{5,1},{9... | collective-permute-start | bytes 2359304 | tf_op jit(solution)/shard_map/ppermute | solution.py:24
  42.9 19.8 %collective-permute-start.2 = (f32[192,1,1024]{2,0,1:T(8,128)S(1)}, f32[192,1,1024]{2,0,1:T(8,128)S(1)}, u32[]{:S(2)}, u32[]{:S(2)}) collective-permute-start(f32[192,1,1024]{2,0,1:T(8,128)S(1)} %get-tuple-element.9), channel_id=1, source_target_pairs={{0,4},{4,8},{8,12},{12,16},{16,20},{20,24},{24,28},{28,0},{1,5},{5... | collective-permute-start | bytes 2359304 | tf_op jit(solution)/shard_map/ppermute | solution.py:21
  44.8 17.9 %collective-permute-start.3 = (f32[192,1,1024]{2,0,1:T(8,128)S(1)}, f32[192,1,1024]{2,0,1:T(8,128)S(1)}, u32[]{:S(2)}, u32[]{:S(2)}) collective-permute-start(f32[192,1,1024]{2,0,1:T(8,128)S(1)} %get-tuple-element.10), channel_id=1, source_target_pairs={{4,0},{8,4},{12,8},{16,12},{20,16},{24,20},{28,24},{0,28},{5,1},{9... | collective-permute-start | bytes 2359304 | tf_op jit(solution)/shard_map/ppermute | solution.py:24
  75.7 20.2 %collective-permute-start.4 = (f32[192,1,1024]{2,0,1:T(8,128)S(1)}, f32[192,1,1024]{2,0,1:T(8,128)S(1)}, u32[]{:S(2)}, u32[]{:S(2)}) collective-permute-start(f32[192,1,1024]{2,0,1:T(8,128)S(1)} %get-tuple-element.7), channel_id=1, source_target_pairs={{0,4},{4,8},{8,12},{12,16},{16,20},{20,24},{24,28},{28,0},{1,5},{5... | collective-permute-start | bytes 2359304 | tf_op jit(solution)/shard_map/ppermute | solution.py:21
  77.7 18.2 %collective-permute-start.5 = (f32[192,1,1024]{2,0,1:T(8,128)S(1)}, f32[192,1,1024]{2,0,1:T(8,128)S(1)}, u32[]{:S(2)}, u32[]{:S(2)}) collective-permute-start(f32[192,1,1024]{2,0,1:T(8,128)S(1)} %get-tuple-element.8), channel_id=1, source_target_pairs={{4,0},{8,4},{12,8},{16,12},{20,16},{24,20},{28,24},{0,28},{5,1},{9... | collective-permute-start | bytes 2359304 | tf_op jit(solution)/shard_map/ppermute | solution.py:24
  102.3 20.5 %collective-permute-start.6 = (f32[192,1,1024]{2,0,1:T(8,128)S(1)}, f32[192,1,1024]{2,0,1:T(8,128)S(1)}, u32[]{:S(2)}, u32[]{:S(2)}) collective-permute-start(f32[192,1,1024]{2,0,1:T(8,128)S(1)} %get-tuple-element.5), channel_id=1, source_target_pairs={{0,4},{4,8},{8,12},{12,16},{16,20},{20,24},{24,28},{28,0},{1,5},{5... | collective-permute-start | bytes 2359304 | tf_op jit(solution)/shard_map/ppermute | solution.py:21
  103.2 19.6 %collective-permute-start.7 = (f32[192,1,1024]{2,0,1:T(8,128)S(1)}, f32[192,1,1024]{2,0,1:T(8,128)S(1)}, u32[]{:S(2)}, u32[]{:S(2)}) collective-permute-start(f32[192,1,1024]{2,0,1:T(8,128)S(1)} %get-tuple-element.6), channel_id=1, source_target_pairs={{4,0},{8,4},{12,8},{16,12},{20,16},{24,20},{28,24},{0,28},{5,1},{9... | collective-permute-start | bytes 2359304 | tf_op jit(solution)/shard_map/ppermute | solution.py:24
  137.2 94.8 %all-to-all-start = ((bf16[192,8,1024]{0,1,2:T(8,128)(2,1)}), bf16[192,8,1024]{0,1,2:T(8,128)(2,1)}, u32[]{:S(2)}, u32[]{:S(2)}) async-start(bf16[192,8,1024]{0,1,2:T(8,128)(2,1)} %copy.21), calls=%async_computation | async-start | bytes 8388608 | tf_op jit(solution)/shard_map/all_to_all | solution.py:94
where the time goes:
time: 444 us; the launch traced here: 440 us
  waiting for transfers between devices  156 us (35%)
  matrix products  121 us (27%)
  blocking collectives  75.4 us (17%)
  local copies, waits for them, and re-layouts  36.8 us (8%)
  other arithmetic  32.9 us (7%)
  starting transfers between devices  17.2 us (4%)
    dot_general x4, matrix products, sources(): jnp.dot(coupling, state.astype(jnp.bfloat16), preferred_element_type=jnp....  105 us
    all_to_all x1, waiting for transfers between devices, on_device(): lax.all_to_all(propagated, 'comp', split_axis=2, concat_axis=0, tiled=True)  87.8 us
    all_to_all x1, blocking collectives, on_device(): lax.all_to_all(updated, 'comp', split_axis=0, concat_axis=2, tiled=True)  75.4 us
    ppermute x4, waiting for transfers between devices, padded_2(): lax.ppermute(lax.slice_in_dim(block, block.shape[dim] - width, None, axis...  68.1 us
    mul x2, other arithmetic, upwind(): (energy - jnp.maximum(courant_x, 0.0) * (energy - west_side) - jnp.minimu...  19 us
    dot_general x1, matrix products, courants(): jnp.einsum('cd,dxy->cxy', table, depth_onehot, precision=lax.Precision.HI...  15.9 us
  transfers between devices with their start and end apart: 9, of which 5 were waited for; matrix products, arithmetic and copies ran while one was open for 0% of the time, Pallas kernels for 0%

commit v1 on v0

v1 whole, which is shorter than its diff:
```python
import functools
import math

import jax
import jax.numpy as jnp
import numpy as np
from jax import lax
from jax.experimental import pallas as pl
from jax.experimental.pallas import tpu as pltpu
from jax.sharding import PartitionSpec as P

K = 24
F = 32
PSTEPS = 4
SRC_STEPS = 4
PAIR = 2 * K
LANES = 128
VMEM_LIMIT = 48 * 1024 * 1024

THETA = np.arange(K).astype(np.float32) * np.float32(2.0 * math.pi / K)
COS = np.cos(THETA)
SIN = np.sin(THETA)


def eastward_rows(start, count):
    k = lax.rem(start + lax.broadcasted_iota(jnp.int32, (count, 1), 0), K)
    return (k < 6) | (k >= 18)


def pack_kernel(raw, to_east, to_west):
    for out, runs, low in ((to_east, ((0, 6), (18, 24)), 4), (to_west, ((6, 18),), 0)):
        at = 0
        for first, last in runs:
            one = raw[first:last].astype(jnp.float32)
            two = raw[K + first : K + last].astype(jnp.float32)
            row = lax.broadcasted_iota(jnp.int32, one.shape, 1)
            if low:
                both = jnp.where(row < 4, pltpu.roll(one, 4, 1), two)
            else:
                both = jnp.where(row < 4, one, pltpu.roll(two, 4, 1))
            out[at : at + last - first] = both.astype(jnp.bfloat16)
            at += last - first


def pack_halo(spectrum):
    comps, columns, rows = spectrum.shape
    half = jax.ShapeDtypeStruct((comps // 4, columns, rows), jnp.bfloat16)
    block = pl.BlockSpec((K // 2, columns, rows), lambda i: (i, 0, 0))
    return pl.pallas_call(
        pack_kernel,
        grid=(comps // PAIR,),
        in_specs=[pl.BlockSpec((PAIR, columns, rows), lambda i: (i, 0, 0))],
        out_specs=[block, block],
        out_shape=[half, half],
        compiler_params=pltpu.CompilerParams(vmem_limit_bytes=VMEM_LIMIT),
        name="pack_halo",
    )(spectrum)


def propagate_kernel(with_halo, parts, pos, *refs):
    if with_halo:
        raw, west, east, code, code_west, code_east, table, trig = refs[:8]
        refs = refs[8:]
    else:
        raw, code, table, trig = refs[:4]
        refs = refs[4:]
    outs, (cols, speed, result) = refs[: len(parts)], refs[len(parts) :]
    columns, rows = code.shape
    tiles = rows // LANES
    nfreq = table.shape[0]
    step = pl.program_id(0)
    row8 = lax.broadcasted_iota(jnp.int32, (columns, rows), 0)

    for f in range(2):
        for first, last, eastward in ((0, 6, True), (6, 18, False), (18, 24, True)):
            a, b = f * K + first, f * K + last
            own = raw[a:b].astype(jnp.float32)
            if with_halo:
                at = {0: 0, 6: 0, 18: 6}[first]
                side = (west if eastward else east)[at : at + last - first].astype(jnp.float32)
                row = lax.broadcasted_iota(jnp.int32, own.shape, 1)
                own = pltpu.roll(own, 4, 1)
                if eastward:
                    side = pltpu.roll(side, 4, 1) if f else side
                    own = jnp.where(row < 4, side, own)
                else:
                    side = side if f else pltpu.roll(side, 4, 1)
                    own = jnp.where(row < 4, own, side)
            own = own.reshape(-1, rows)
            for t in range(tiles):
                cols[t, a * 8 : b * 8, :] = own[:, t * LANES : (t + 1) * LANES]

    if with_halo:
        turned = pltpu.roll(code[...], 4, 0)
        codes = (
            jnp.where(row8 < 4, pltpu.roll(code_west[...], 4, 0), turned),
            jnp.where(row8 < 4, turned, pltpu.roll(code_east[...], 4, 0)),
        )
    else:
        codes = (code[...],)
    lane = lax.broadcasted_iota(jnp.int32, (8, rows), 1)
    freq0 = step * 2
    for f in range(2):
        line = jnp.broadcast_to(table[freq0 + f], (8, LANES))
        for n, c in enumerate(codes):
            sea = (c >= 16).astype(jnp.float32)
            depth = jnp.bitwise_and(c, 15)
            looked = [
                jnp.take_along_axis(line, depth[:, t * LANES : (t + 1) * LANES], axis=1)
                for t in range(tiles)
            ]
            speed[2 * n] = jnp.concatenate(looked, axis=1) * sea
            speed[2 * n + 1] = sea
        last_n = len(codes) - 1
        for g in range(3):
            base = (f * K + g * 8) * 8

            def column(p):
                return jnp.concatenate(
                    [cols[t, pl.ds(base + p, 8, stride=8), :] for t in range(tiles)], axis=1
                )

            east_rows = eastward_rows(g * 8, 8)

            def upwind_order(get, p):
                if g == 1:
                    return get(1, 7 - p)
                return jnp.where(east_rows, get(0, p), get(1, 7 - p))

            def spread(which):
                def get(side, p):
                    n = side if last_n else 0
                    return jnp.broadcast_to(speed[2 * n + which, p : p + 1, :], (8, rows))

                return get

            k = g * 8 + lax.broadcasted_iota(jnp.int32, (8, rows), 0)
            south = k < 12
            cos = jnp.concatenate([trig[0, g * 8 : g * 8 + 8, :]] * tiles, axis=1)
            sin = jnp.concatenate([trig[1, g * 8 : g * 8 + 8, :]] * tiles, axis=1)
            edge = (south & (lane == 0)) | (~south & (lane == rows - 1))
            inner_sin = jnp.where(edge, 0.0, sin)

            def behind(e):
                if g == 0:
                    return pltpu.roll(e, 1, 1)
                if g == 2:
                    return pltpu.roll(e, rows - 1, 1)
                return jnp.where(south, pltpu.roll(e, 1, 1), pltpu.roll(e, rows - 1, 1))

            before = None
            for p in range(8):
                now = [upwind_order(lambda side, q: column(q), p)]
                if p:
                    rate = upwind_order(spread(0), p)
                    sea = upwind_order(spread(1), p)
                    keep = sea - rate * (cos + sin)
                    from_x = rate * cos
                    from_y = rate * inner_sin
                    for t in range(1, min(p, PSTEPS) + 1):
                        e = now[t - 1]
                        now.append(keep * e + from_x * before[t - 1] + from_y * behind(e))
                if p >= PSTEPS:
                    result[p - PSTEPS, f * K + g * 8 : f * K + g * 8 + 8, :] = now[PSTEPS]
                before = now

    z = pos[0]
    width = rows // pos_count(parts)
    for out, (s, lo, size) in zip(outs, parts):
        at = pl.multiple_of(jnp.bitwise_xor(z, s) * width + lo, LANES)
        out[...] = result[:, :, pl.ds(at, size)].astype(jnp.bfloat16)


def pos_count(parts):
    return max(s for s, _, _ in parts) + 1


def propagate(z, spectrum, code, table, trig, parts, halo=None):
    comps, columns, rows = spectrum.shape
    whole = lambda a: pl.BlockSpec(a.shape, lambda i, z: (0,) * a.ndim)
    blocked = lambda a, n: pl.BlockSpec((n,) + a.shape[1:], lambda i, z: (i, 0, 0))
    args, specs = [spectrum], [blocked(spectrum, PAIR)]
    if halo is not None:
        west, east, code_west, code_east = halo
        args += [west, east, code, code_west, code_east]
        specs += [blocked(west, K // 2), blocked(east, K // 2), whole(code), whole(code), whole(code)]
    else:
        args += [code]
        specs += [whole(code)]
    args += [table, trig]
    specs += [whole(table), whole(trig)]
    return pl.pallas_call(
        functools.partial(propagate_kernel, halo is not None, parts),
        grid_spec=pltpu.PrefetchScalarGridSpec(
            num_scalar_prefetch=1,
            grid=(comps // PAIR,),
            in_specs=specs,
            out_specs=[pl.BlockSpec((4, PAIR, size), lambda i, z: (0, i, 0)) for _, _, size in parts],
            scratch_shapes=[
                pltpu.VMEM((rows // LANES, PAIR * columns, LANES), jnp.float32),
                pltpu.VMEM((4, columns, rows), jnp.float32),
                pltpu.VMEM((4, PAIR, rows), jnp.float32),
            ],
        ),
        out_shape=[jax.ShapeDtypeStruct((4, comps, size), jnp.bfloat16) for _, _, size in parts],
        compiler_params=pltpu.CompilerParams(vmem_limit_bytes=VMEM_LIMIT),
        cost_estimate=pl.CostEstimate(flops=comps * columns * rows * 30, bytes_accessed=6 * comps * rows * 8, transcendentals=0),
        name="propagate_downwind" if halo is None else "propagate_upwind",
    )(z, *args)


def sources_kernel(count, lane0, pos, *refs):
    first, second = refs[:count], refs[count : 2 * count]
    wind_c, wind_s, coupling, trig, rates = refs[2 * count : 2 * count + 5]
    outs = refs[2 * count + 5 : 3 * count + 5]
    state, rounded, nonlin, wind = refs[3 * count + 5 :]
    comps = first[0].shape[1]
    width = outs[0].shape[3]
    whole = comps * count
    z = pos[0]
    mask = eastward_rows(0, comps)
    for s in range(count):
        at = pl.multiple_of(jnp.bitwise_xor(z, s) * comps, comps)
        down = first[s][0, :, lane0 : lane0 + width].astype(jnp.float32)
        up = second[s][0].astype(jnp.float32)
        state[pl.ds(at, comps), 0:width] = jnp.where(mask, up, down)
        state[pl.ds(at, comps), width : 2 * width] = jnp.where(mask, down, up)
    pair = pl.program_id(0)
    for n, x in enumerate((pair, 7 - pair)):
        c = wind_c[x, :, lane0 : lane0 + width]
        d = wind_s[x, :, lane0 : lane0 + width]
        wind[:, n * width : (n + 1) * width] = jnp.maximum(trig[0, :, 0:1] * c + trig[1, :, 0:1] * d, 0.0)

    for step in range(SRC_STEPS):
        total = jnp.zeros((8, 2 * width), jnp.float32)
        for f in range(F):
            here = state[f * K : (f + 1) * K, :]
            rounded[f * K : (f + 1) * K, :] = here.astype(jnp.bfloat16)
            total += float(0.1 * 1.1**f) * (here[0:8] + here[8:16] + here[16:24])
        total = jnp.sum(total, axis=0, keepdims=True)
        sat = total / (total + 100.0)
        nonlin[...] = jnp.dot(coupling[...], rounded[...], preferred_element_type=jnp.float32)
        for f in range(F):
            at = slice(f * K, (f + 1) * K)
            here = state[at, :]
            damp = 1.0 - sat * float(0.15 * (f + 1) / F)
            gain = damp + wind[...] * float(1.1 ** (f - 16))
            state[at, :] = jnp.maximum(gain * here + 0.125 * nonlin[at, :], 0.0)

    for s in range(count):
        at = pl.multiple_of(jnp.bitwise_xor(z, s) * comps, comps)
        for n in range(2):
            outs[s][n, 0] = state[pl.ds(at, comps), n * width : (n + 1) * width].astype(jnp.bfloat16)


def sources(z, first, second, wind_c, wind_s, coupling, trig, lane0):
    count = len(first)
    comps, width = second[0].shape[1], second[0].shape[2]
    whole = lambda a: pl.BlockSpec(a.shape, lambda i, z: (0,) * a.ndim)
    return pl.pallas_call(
        functools.partial(sources_kernel, count, lane0),
        grid_spec=pltpu.PrefetchScalarGridSpec(
            num_scalar_prefetch=1,
            grid=(4,),
            in_specs=[pl.BlockSpec((1,) + a.shape[1:], lambda i, z: (3 - i, 0, 0)) for a in first]
            + [pl.BlockSpec((1,) + a.shape[1:], lambda i, z: (i, 0, 0)) for a in second]
            + [whole(wind_c), whole(wind_s), whole(coupling), whole(trig), whole(trig)],
            out_specs=[pl.BlockSpec((2, 1, comps, width), lambda i, z: (0, i, 0, 0))] * count,
            scratch_shapes=[
                pltpu.VMEM((comps * count, 2 * width), jnp.float32),
                pltpu.VMEM((comps * count, 2 * width), jnp.bfloat16),
                pltpu.VMEM((comps * count, 2 * width), jnp.float32),
                pltpu.VMEM((K, 2 * width), jnp.float32),
            ],
        ),
        out_shape=[jax.ShapeDtypeStruct((2, 4, comps, width), jnp.bfloat16)] * count,
        compiler_params=pltpu.CompilerParams(vmem_limit_bytes=VMEM_LIMIT),
        cost_estimate=pl.CostEstimate(
            flops=SRC_STEPS * 2 * (comps * count) ** 2 * 8 * width, bytes_accessed=4 * comps * count * 8 * width, transcendentals=0
        ),
        name="source_terms",
    )(z, *first, *second, wind_c, wind_s, coupling, trig, trig)


def assemble_kernel(count, pos, *refs):
    blocks, out, turned = refs[:count], refs[-2], refs[-1]
    for s in range(count):

        @pl.when(pl.program_id(0) == s)
        def _():
            comps = blocks[s].shape[2]
            for n in range(2):
                for i in range(4):
                    x = i if n == 0 else 7 - i
                    turned[pl.ds(x, comps, stride=8), :] = blocks[s][n, i].astype(jnp.float32)
            out[...] = turned[...].reshape(out.shape).astype(jnp.bfloat16)


def assemble(z, blocks, rows, chunk, chunks, into):
    count = len(blocks)
    comps, width = blocks[0].shape[2], blocks[0].shape[3]
    extra = [] if into is None else [into]
    return pl.pallas_call(
        functools.partial(assemble_kernel, count),
        grid_spec=pltpu.PrefetchScalarGridSpec(
            num_scalar_prefetch=1,
            grid=(count,),
            in_specs=[pl.BlockSpec(b.shape, lambda i, z: (0, 0, 0, 0)) for b in blocks]
            + [pl.BlockSpec(memory_space=pl.ANY)] * len(extra),
            out_specs=pl.BlockSpec((comps, 8, width), lambda i, z: (0, 0, jnp.bitwise_xor(z[0], i) * chunks + chunk)),
            scratch_shapes=[pltpu.VMEM((comps * 8, width), jnp.float32)],
        ),
        out_shape=jax.ShapeDtypeStruct((comps, 8, rows), jnp.bfloat16),
        input_output_aliases={count + 1: 0} if extra else {},
        compiler_params=pltpu.CompilerParams(vmem_limit_bytes=VMEM_LIMIT),
        name="assemble",
    )(z, *blocks, *extra)


def exchange(blocks, axis):
    count = len(blocks)
    return [blocks[0]] + [
        lax.ppermute(blocks[s], axis, [(i, i ^ s) for i in range(count)]) for s in range(1, count)
    ]


def on_device(spectrum, sea_mask, depth_class, group_speed, wind_speed, wind_dir, coupling):
    comps, columns, rows = spectrum.shape
    count = lax.axis_size("comp")
    tiles = lax.axis_size("tile")
    place = lax.axis_index("comp")
    z = place.astype(jnp.int32).reshape(1)
    width = rows // count
    chunks = max(1, width // LANES)
    east = [(i, (i + 1) % tiles) for i in range(tiles)]
    west = [(j, i) for i, j in east]

    code = depth_class + 16 * sea_mask
    freqs = comps // K
    table = lax.dynamic_slice_in_dim(group_speed, place * freqs, freqs, 1).T
    table = jnp.pad(table, ((0, 0), (0, LANES - table.shape[1])))[:, None]
    trig = jnp.broadcast_to(jnp.asarray(np.stack([np.abs(COS), np.abs(SIN)]))[:, :, None], (2, K, LANES))
    signed = jnp.broadcast_to(jnp.asarray(np.stack([COS, SIN]))[:, :, None], (2, K, LANES))
    start = place * width
    speed_part = 0.002 * lax.dynamic_slice_in_dim(wind_speed, start, width, 1)
    dir_part = lax.dynamic_slice_in_dim(wind_dir, start, width, 1)
    wind_c, wind_s = (speed_part * jnp.cos(dir_part))[:, None], (speed_part * jnp.sin(dir_part))[:, None]

    to_east, to_west = pack_halo(spectrum)
    halo = (
        lax.ppermute(to_east, "tile", east),
        lax.ppermute(to_west, "tile", west),
        lax.ppermute(code, "tile", east),
        lax.ppermute(code, "tile", west),
    )
    first = propagate(z, spectrum, code, table, trig, [(s, 0, width) for s in range(count)])
    first = exchange(first, "comp")
    size = width // chunks
    parts = [(s, c * size, size) for c in range(chunks) for s in range(count)]
    second = propagate(z, spectrum, code, table, trig, parts, halo)
    out = None
    for c in range(chunks):
        arrived = exchange(second[c * count : (c + 1) * count], "comp")
        updated = sources(z, first, arrived, wind_c, wind_s, coupling, signed, c * size)
        out = assemble(z, exchange(updated, "comp"), rows, c, chunks, out)
    return out


def solution(mesh):
    placed = (
        P("comp", "tile", None),
        P("tile", None),
        P("tile", None),
        P(),
        P("tile", None),
        P("tile", None),
        P(),
    )
    return jax.shard_map(
        on_device, mesh=mesh, in_specs=placed, out_specs=P("comp", "tile", None), check_vma=False
    )
```

time: 444 us -> 187 us (0.42)
  matrix products: 121 us -> 0 us
  waiting for transfers between devices: 156 us -> 73.9 us
  Pallas kernels: 0 us -> 80.8 us
  blocking collectives: 75.4 us -> 0 us
  other arithmetic: 32.9 us -> 1.53 us
  local copies, waits for them, and re-layouts: 36.8 us -> 7.74 us
  starting transfers between devices: 17.2 us -> 22.5 us
    dot_general x6 -> x0, matrix products: 121 us -> none  [the longest x4 105 us: sources(): jnp.dot(coupling, state.astype(jnp.bfloat16), preferred_element_type=jnp....]
    all_to_all x1 -> x0, waiting for transfers between devices: 87.8 us -> none  [on_device(): lax.all_to_all(propagated, 'comp', split_axis=2, concat_axis=0, tiled=True)]
    pallas_call x0 -> x7, Pallas kernels: none -> 80.8 us  [the longest x2 51.2 us: propagate(): pl.pallas_call(functools.partial(propagate_kernel, halo is not None, part...]
    all_to_all x1 -> x0, blocking collectives: 75.4 us -> none  [on_device(): lax.all_to_all(updated, 'comp', split_axis=0, concat_axis=2, tiled=True)]
    mul x8 -> x1, other arithmetic: 19.1 us -> 0.76 us  [on_device(): speed_part * jnp.sin(dir_part)]
    ppermute x8 -> x19, starting transfers between devices: 11 us -> 22.5 us  [the longest x15 19.3 us: exchange(): lax.ppermute(blocks[s], axis, [(i, i ^ s) for i in range(count)])]
    convert_element_type x3 -> x0, other arithmetic: 11.4 us -> none  [the longest x1 7.55 us: on_device(): propagated = energy.astype(jnp.bfloat16)]
    all_to_all x2 -> x0, local copies, waits for them, and re-layouts: 10.3 us -> none  [the longest x1 8.19 us: on_device(): lax.all_to_all(propagated, 'comp', split_axis=2, concat_axis=0, tiled=True)]
  transfers between devices with their start and end apart: 9 -> 19, of which waited for: 5 -> 8; matrix products, arithmetic and copies ran while one was open for 0% -> 1% of each run, Pallas kernels for 0% -> 41%
where the time goes in v1:
time: 187 us
  Pallas kernels  80.8 us (43%)
  waiting for transfers between devices  73.9 us (40%)
  starting transfers between devices  22.5 us (12%)
  local copies, waits for them, and re-layouts  7.74 us (4%)
    ppermute x15, waiting for transfers between devices, exchange(): lax.ppermute(blocks[s], axis, [(i, i ^ s) for i in range(count)])  72.8 us
    pallas_call x2, Pallas kernels, propagate(): pl.pallas_call(functools.partial(propagate_kernel, halo is not None, part...  51.2 us
    pallas_call x2, Pallas kernels, sources(): pl.pallas_call(functools.partial(sources_kernel, count, lane0), grid_spec...  23.3 us
    ppermute x15, starting transfers between devices, exchange(): lax.ppermute(blocks[s], axis, [(i, i ^ s) for i in range(count)])  19.3 us
    unnamed x31, local copies, waits for them, and re-layouts  7.5 us
    pallas_call x2, Pallas kernels, assemble(): pl.pallas_call(functools.partial(assemble_kernel, count), grid_spec=pltpu...  4.53 us
  transfers between devices with their start and end apart: 19, of which 8 were waited for; matrix products, arithmetic and copies ran while one was open for 1% of the time, Pallas kernels for 41%

profile of v1, /device:TPU:8, one launch (start us, length us, event | category | flops | bytes accessed | tf_op | source)
XLA Modules:
  0.0 186.6 jit_solution(18049725301605713357)
XLA Ops:
  0.0 0.0 copy-start
  0.0 1.9 %copy-done.1 = bf16[192,8,1024]{2,1,0:T(8,128)(2,1)S(1)} copy-done((bf16[192,8,1024]{2,1,0:T(8,128)(2,1)S(1)}, bf16[192,8,1024]{2,1,0:T(8,128)(2,1)}, u32[]{:S(2)}) %copy-start.1) | copy-done | bytes 3145752
  1.9 1.7 pack_halo.1
  3.7 0.0 collective-permute-start.3
  3.7 2.6 %collective-permute-start.4 = (bf16[48,8,1024]{2,1,0:T(8,128)(2,1)}, bf16[48,8,1024]{2,1,0:T(8,128)(2,1)}, u32[]{:S(2)}, u32[]{:S(2)}) collective-permute-start(bf16[48,8,1024]{2,1,0:T(8,128)(2,1)} %get-tuple-element.32), channel_id=1, source_target_pairs={{4,0},{8,4},{12,8},{16,12},{20,16},{24,20},{28,24},{0,28},{5,1},{9... | collective-permute-start | bytes 2359304 | tf_op jit(solution)/shard_map/ppermute | solution.py:352
  6.3 0.0 copy-done
  6.3 0.1 constant_dynamic-slice_fusion
  6.4 0.1 copy.14
  6.5 0.0 copy-done.12
  6.5 0.8 multiply_add_fusion.refs_1_.refs_3_
  7.2 0.0 copy-done.14
  7.2 0.1 broadcast_in_dim.22.refs_3_.refs_7_
  7.3 0.0 copy-done.2
  7.3 24.6 %propagate_downwind.1 = (bf16[4,192,256]{2,1,0:T(8,128)(2,1)S(1)}, bf16[4,192,256]{2,1,0:T(8,128)(2,1)S(1)}, bf16[4,192,256]{2,1,0:T(8,128)(2,1)}, bf16[4,192,256]{2,1,0:T(8,128)(2,1)}) custom-call(s32[1]{0:T(128)} %bitcast.pos, bf16[192,8,1024]{2,1,0:T(8,128)(2,1)S(1)} %copy-done.2, s32[8,1024]{1,0:T(8,128)S(1)} %multiply_add_fusion.refs_1_.refs_3_, ...), custom_call_target="tpu_custom_call" | custom-call | flops 47185920 | bytes 9437184 | tf_op jit(solution)/shard_map/propagate_downwind/pallas_call | solution.py:192
  31.9 0.0 collective-permute-start
  31.9 0.1 collective-permute-start.6
  32.0 0.5 collective-permute-start.5
  32.5 1.1 collective-permute-done.6.refs_5_
  33.6 3.1 %collective-permute-start.1 = (bf16[4,192,256]{2,1,0:T(8,128)(2,1)}, bf16[4,192,256]{2,1,0:T(8,128)(2,1)S(1)}, u32[]{:S(2)}, u32[]{:S(2)}) collective-permute-start(bf16[4,192,256]{2,1,0:T(8,128)(2,1)} %get-tuple-element.29), channel_id=1, source_target_pairs={{0,2},{1,3},{2,0},{3,1},{4,6},{5,7},{6,4},{7,5},{8,10},{9,11},{10,... | collective-permute-start | bytes 1179656 | tf_op jit(solution)/shard_map/ppermute | solution.py:323
  36.8 0.0 collective-permute-done.5.refs_4_
  36.8 2.6 %collective-permute-start.2 = (bf16[4,192,256]{2,1,0:T(8,128)(2,1)}, bf16[4,192,256]{2,1,0:T(8,128)(2,1)S(1)}, u32[]{:S(2)}, u32[]{:S(2)}) collective-permute-start(bf16[4,192,256]{2,1,0:T(8,128)(2,1)} %get-tuple-element.30), channel_id=1, source_target_pairs={{0,3},{1,2},{2,1},{3,0},{4,7},{5,6},{6,5},{7,4},{8,11},{9,10},{10,... | collective-permute-start | bytes 1179656 | tf_op jit(solution)/shard_map/ppermute | solution.py:323
  39.3 0.0 collective-permute-done.3.refs_1_
  39.3 0.0 collective-permute-done.4.refs_2_
  39.3 26.6 %propagate_upwind.1 = (bf16[4,192,128]{2,1,0:T(8,128)(2,1)S(1)}, bf16[4,192,128]{2,1,0:T(8,128)(2,1)}, bf16[4,192,128]{2,1,0:T(8,128)(2,1)S(1)}, bf16[4,192,128]...) custom-call(s32[1]{0:T(128)} %bitcast.pos, ...), custom_call_target="tpu_custom_call" | custom-call | flops 47185920 | bytes 9437184 | tf_op jit(solution)/shard_map/propagate_upwind/pallas_call | solution.py:192
  65.9 0.7 copy-done.4
  66.6 0.7 copy-done.6
  67.3 1.4 collective-permute-start.13
  68.6 0.1 collective-permute-start.14
  68.8 0.0 collective-permute-done.refs_1_
  68.8 2.0 %collective-permute-start.15 = (bf16[4,192,128]{2,1,0:T(8,128)(2,1)S(1)}, bf16[4,192,128]{2,1,0:T(8,128)(2,1)}, u32[]{:S(2)}, u32[]{:S(2)}) collective-permute-start(bf16[4,192,128]{2,1,0:T(8,128)(2,1)S(1)} %get-tuple-element.44), channel_id=1, source_target_pairs={{0,3},{1,2},{2,1},{3,0},{4,7},{5,6},{6,5},{7,4},{8,11},{9,10},{10,... | collective-permute-start | bytes 589832 | tf_op jit(solution)/shard_map/ppermute | solution.py:323
  70.8 0.8 sine_multiply_fusion
  71.6 0.0 collective-permute-done.1.refs_2_
  71.6 2.3 %collective-permute-start.7 = (bf16[4,192,128]{2,1,0:T(8,128)(2,1)}, bf16[4,192,128]{2,1,0:T(8,128)(2,1)S(1)}, u32[]{:S(2)}, u32[]{:S(2)}) collective-permute-start(bf16[4,192,128]{2,1,0:T(8,128)(2,1)} %get-tuple-element.34), channel_id=1, source_target_pairs={{0,1},{1,0},{2,3},{3,2},{4,5},{5,4},{6,7},{7,6},{8,9},{9,8},{10,11... | collective-permute-start | bytes 589832 | tf_op jit(solution)/shard_map/ppermute | solution.py:323
  73.9 0.0 collective-permute-done.2.refs_3_
  73.9 0.1 collective-permute-start.8
  74.0 1.1 collective-permute-done.13.refs_5_
  75.1 0.7 copy-done.8
  75.8 0.6 collective-permute-start.9
  76.4 8.9 %collective-permute-done.14.refs_6_ = bf16[4,192,128]{2,1,0:T(8,128)(2,1)S(1)} collective-permute-done((bf16[4,192,128]{2,1,0:T(8,128)(2,1)S(1)}, bf16[4,192,128]{2,1,0:T(8,128)(2,1)S(1)}, u32[]{:S(2)}, u32[]{:S(2)}) %collective-permute-start.14) | collective-permute-done | bytes 196640 | tf_op jit(solution)/shard_map/ppermute | solution.py:323
  85.3 0.7 copy-done.10
  86.0 12.1 %collective-permute-done.15.refs_7_ = bf16[4,192,128]{2,1,0:T(8,128)(2,1)} collective-permute-done((bf16[4,192,128]{2,1,0:T(8,128)(2,1)S(1)}, bf16[4,192,128]{2,1,0:T(8,128)(2,1)}, u32[]{:S(2)}, u32[]{:S(2)}) %collective-permute-start.15) | collective-permute-done | bytes 196640 | tf_op jit(solution)/shard_map/ppermute | solution.py:323
  98.2 0.1 broadcast_in_dim.25.refs_11_.refs_12_
  98.2 0.9 copy-done.7
  99.2 0.9 copy-done.9
  100.1 0.9 copy-done.11
  101.0 12.1 %source_terms.3 = (bf16[2,4,192,128]{3,2,1,0:T(8,128)(2,1)S(1)}, bf16[2,4,192,128]{3,2,1,0:T(8,128)(2,1)S(1)}, bf16[2,4,192,128]{3,2,1,0:T(8,128)(2,1)S(1)}, bf16[2,4,192,128]{3,2,1,0:T(8,128)(2,1)S(1)}) custom-call(s32[1]{0:T(128)} %bitcast.pos, bf16[4,192,256]{2,1,0:T(8,128)(2,1)S(1)} %get-tuple-element.27.refs_0_, ...), custom_call_target="tpu_custom_call" | custom-call | flops 4831838208 | bytes 3145728 | tf_op jit(solution)/shard_map/source_terms/pallas_call | solution.py:260
  113.1 0.1 collective-permute-start.16
  113.2 2.9 %collective-permute-start.17 = (bf16[2,4,192,128]{3,2,1,0:T(8,128)(2,1)S(1)}, bf16[2,4,192,128]{3,2,1,0:T(8,128)(2,1)S(1)}, u32[]{:S(2)}, u32[]{:S(2)}) collective-permute-start(bf16[2,4,192,128]{3,2,1,0:T(8,128)(2,1)S(1)} %get-tuple-element.47), channel_id=1, source_target_pairs={{0,2},{1,3},{2,0},{3,1},{4,6},{5,7},{6,4},{7,5},{8,10},{9,11},{10,... | collective-permute-start | bytes 1179656 | tf_op jit(solution)/shard_map/ppermute | solution.py:323
  116.1 0.0 collective-permute-done.7.refs_5_
  116.1 0.6 collective-permute-start.18
  116.7 0.0 collective-permute-done.8.refs_6_
  116.7 0.0 collective-permute-done.9.refs_7_
  116.7 11.2 %source_terms.2 = (bf16[2,4,192,128]{3,2,1,0:T(8,128)(2,1)S(1)}, bf16[2,4,192,128]{3,2,1,0:T(8,128)(2,1)S(1)}, bf16[2,4,192,128]{3,2,1,0:T(8,128)(2,1)S(1)}, bf16[2,4,192,128]{3,2,1,0:T(8,128)(2,1)S(1)}) custom-call(s32[1]{0:T(128)} %bitcast.pos, bf16[4,192,256]{2,1,0:T(8,128)(2,1)S(1)} %get-tuple-element.27.refs_0_, ...), custom_call_target="tpu_custom_call" | custom-call | flops 4831838208 | bytes 3145728 | tf_op jit(solution)/shard_map/source_terms/pallas_call | solution.py:260
  127.9 1.0 collective-permute-start.10
  129.0 1.9 %collective-permute-start.11 = (bf16[2,4,192,128]{3,2,1,0:T(8,128)(2,1)S(1)}, bf16[2,4,192,128]{3,2,1,0:T(8,128)(2,1)S(1)}, u32[]{:S(2)}, u32[]{:S(2)}) collective-permute-start(bf16[2,4,192,128]{3,2,1,0:T(8,128)(2,1)S(1)} %get-tuple-element.39), channel_id=1, source_target_pairs={{0,2},{1,3},{2,0},{3,1},{4,6},{5,7},{6,4},{7,5},{8,10},{9,11},{10,... | collective-permute-start | bytes 1179656 | tf_op jit(solution)/shard_map/ppermute | solution.py:323
  130.9 0.0 collective-permute-done.16.refs_1_
  130.9 0.6 collective-permute-start.12
  131.5 11.1 %collective-permute-done.17.refs_2_ = bf16[2,4,192,128]{3,2,1,0:T(8,128)(2,1)S(1)} collective-permute-done((bf16[2,4,192,128]{3,2,1,0:T(8,128)(2,1)S(1)}, bf16[2,4,192,128]{3,2,1,0:T(8,128)(2,1)S(1)}, u32[]{:S(2)}, u32[]{:S(2)}) %collective-permute-start.17) | collective-permute-done | bytes 393248 | tf_op jit(solution)/shard_map/ppermute | solution.py:323
  142.5 26.3 %collective-permute-done.18.refs_3_ = bf16[2,4,192,128]{3,2,1,0:T(8,128)(2,1)S(1)} collective-permute-done((bf16[2,4,192,128]{3,2,1,0:T(8,128)(2,1)S(1)}, bf16[2,4,192,128]{3,2,1,0:T(8,128)(2,1)S(1)}, u32[]{:S(2)}, u32[]{:S(2)}) %collective-permute-start.18) | collective-permute-done | bytes 393248 | tf_op jit(solution)/shard_map/ppermute | solution.py:323
  168.9 2.3 %assemble.2.refs_4_ = bf16[192,8,1024]{2,1,0:T(8,128)(2,1)} custom-call(s32[1]{0:T(128)} %bitcast.pos, bf16[2,4,192,128]{3,2,1,0:T(8,128)(2,1)S(1)} %get-tuple-element.45.refs_0_, bf16[2,4,192,128]{3,2,1,0:T(8,128)(2,1)S(1)} %collective-permute-done.16.refs_1_, bf16[2,4,192,128]{3,2,1,0:T(8,128)(2,1)S(1)} %collective-permute-done.17.refs_2_, ...), custom_call_target="tpu_custom_call" | custom-call | tf_op jit(solution)/shard_map/assemble/pallas_call | solution.py:303
  171.1 0.0 collective-permute-done.10.refs_1_
  171.1 5.1 %collective-permute-done.11.refs_2_ = bf16[2,4,192,128]{3,2,1,0:T(8,128)(2,1)S(1)} collective-permute-done((bf16[2,4,192,128]{3,2,1,0:T(8,128)(2,1)S(1)}, bf16[2,4,192,128]{3,2,1,0:T(8,128)(2,1)S(1)}, u32[]{:S(2)}, u32[]{:S(2)}) %collective-permute-start.11) | collective-permute-done | bytes 393248 | tf_op jit(solution)/shard_map/ppermute | solution.py:323
  176.2 8.1 %collective-permute-done.12.refs_3_ = bf16[2,4,192,128]{3,2,1,0:T(8,128)(2,1)S(1)} collective-permute-done((bf16[2,4,192,128]{3,2,1,0:T(8,128)(2,1)S(1)}, bf16[2,4,192,128]{3,2,1,0:T(8,128)(2,1)S(1)}, u32[]{:S(2)}, u32[]{:S(2)}) %collective-permute-start.12) | collective-permute-done | bytes 393248 | tf_op jit(solution)/shard_map/ppermute | solution.py:323
  184.3 2.3 %assemble.3 = bf16[192,8,1024]{2,1,0:T(8,128)(2,1)} custom-call(s32[1]{0:T(128)} %bitcast.pos, bf16[2,4,192,128]{3,2,1,0:T(8,128)(2,1)S(1)} %get-tuple-element.37.refs_0_, bf16[2,4,192,128]{3,2,1,0:T(8,128)(2,1)S(1)} %collective-permute-done.10.refs_1_, bf16[2,4,192,128]{3,2,1,0:T(8,128)(2,1)S(1)} %collective-permute-done.11.refs_2_, ...), custom_call_target="tpu_custom_call", output_to_operand_aliasing={{}: (5, {})} | custom-call | tf_op jit(solution)/shard_map/assemble/pallas_call | solution.py:303
  (20 shorter events, 0.1 us)
Async XLA Ops:
  0.0 6.3 %copy-start = (f32[16,32]{1,0:T(8,128)S(1)}, f32[16,32]{1,0:T(8,128)}, u32[]{:S(2)}) copy-start(f32[16,32]{1,0:T(8,128)} %param.12) | copy-start | bytes 6148
  0.0 7.2 %copy-start.14 = (f32[2,24]{1,0:T(2,128)S(1)}, f32[2,24]{1,0:T(2,128)}, u32[]{:S(2)}) copy-start(f32[2,24]{1,0:T(2,128)} %constant.24.clone) | copy-start | bytes 580
  0.0 1.9 %copy-start.1 = (bf16[192,8,1024]{2,1,0:T(8,128)(2,1)S(1)}, bf16[192,8,1024]{2,1,0:T(8,128)(2,1)}, u32[]{:S(2)}) copy-start(bf16[192,8,1024]{2,1,0:T(8,128)(2,1)} %refs_0_.3) | copy-start | bytes 9437188
  1.9 4.5 %copy-start.12 = (s32[8,1024]{1,0:T(8,128)S(1)}, s32[8,1024]{1,0:T(8,128)}, u32[]{:S(2)}) copy-start(s32[8,1024]{1,0:T(8,128)} %param.11) | copy-start | bytes 98308
  1.9 5.4 %copy-start.2 = (bf16[192,8,1024]{2,1,0:T(8,128)(2,1)S(1)}, bf16[192,8,1024]{2,1,0:T(8,128)(2,1)}, u32[]{:S(2)}) copy-start(bf16[192,8,1024]{2,1,0:T(8,128)(2,1)} %refs_0_.3) | copy-start | bytes 9437188
  3.7 35.7 %collective-permute-start.3 = (bf16[48,8,1024]{2,1,0:T(8,128)(2,1)}, bf16[48,8,1024]{2,1,0:T(8,128)(2,1)}, u32[]{:S(2)}, u32[]{:S(2)}) collective-permute-start(bf16[48,8,1024]{2,1,0:T(8,128)(2,1)} %get-tuple-element.31), channel_id=1, source_target_pairs={{0,4},{4,8},{8,12},{12,16},{16,20},{20,24},{24,28},{28,0},{1,5},{5... | collective-permute-start | bytes 2359304 | tf_op jit(solution)/shard_map/ppermute | solution.py:351
  3.7 35.7 %collective-permute-start.4 = (bf16[48,8,1024]{2,1,0:T(8,128)(2,1)}, bf16[48,8,1024]{2,1,0:T(8,128)(2,1)}, u32[]{:S(2)}, u32[]{:S(2)}) collective-permute-start(bf16[48,8,1024]{2,1,0:T(8,128)(2,1)} %get-tuple-element.32), channel_id=1, source_target_pairs={{4,0},{8,4},{12,8},{16,12},{20,16},{24,20},{28,24},{0,28},{5,1},{9... | collective-permute-start | bytes 2359304 | tf_op jit(solution)/shard_map/ppermute | solution.py:352
  31.9 66.2 %copy-start.13 = (f32[2,24]{1,0:T(2,128)S(1)}, f32[2,24]{1,0:T(2,128)}, u32[]{:S(2)}) copy-start(f32[2,24]{1,0:T(2,128)} %constant.25.clone) | copy-start | bytes 580
  31.9 66.3 %copy-start.3 = (bf16[768,768]{1,0:T(8,128)(2,1)S(1)}, bf16[768,768]{1,0:T(8,128)(2,1)}, u32[]{:S(2)}) copy-start(bf16[768,768]{1,0:T(8,128)(2,1)} %refs_10_.3) | copy-start | bytes 3538948
  31.9 36.8 %collective-permute-start = (bf16[4,192,256]{2,1,0:T(8,128)(2,1)S(1)}, bf16[4,192,256]{2,1,0:T(8,128)(2,1)S(1)}, u32[]{:S(2)}, u32[]{:S(2)}) collective-permute-start(bf16[4,192,256]{2,1,0:T(8,128)(2,1)S(1)} %get-tuple-element.28), channel_id=1, source_target_pairs={{0,1},{1,0},{2,3},{3,2},{4,5},{5,4},{6,7},{7,6},{8,9},{9,8},{10,11... | collective-permute-start | bytes 1179656 | tf_op jit(solution)/shard_map/ppermute | solution.py:323
  31.9 1.7 collective-permute-start.6
  32.0 4.7 %collective-permute-start.5 = (s32[8,1024]{1,0:T(8,128)S(1)}, s32[8,1024]{1,0:T(8,128)S(1)}, u32[]{:S(2)}, u32[]{:S(2)}) collective-permute-start(s32[8,1024]{1,0:T(8,128)S(1)} %multiply_add_fusion.refs_1_.refs_3_), channel_id=1, source_target_pairs={{0,4},{4,8},{8,12},{12,16},{16,20},{20,24},{24,28},{28,0},{1,5},{5... | collective-permute-start | bytes 98312 | tf_op jit(solution)/shard_map/ppermute | solution.py:353
  33.6 37.9 %collective-permute-start.1 = (bf16[4,192,256]{2,1,0:T(8,128)(2,1)}, bf16[4,192,256]{2,1,0:T(8,128)(2,1)S(1)}, u32[]{:S(2)}, u32[]{:S(2)}) collective-permute-start(bf16[4,192,256]{2,1,0:T(8,128)(2,1)} %get-tuple-element.29), channel_id=1, source_target_pairs={{0,2},{1,3},{2,0},{3,1},{4,6},{5,7},{6,4},{7,5},{8,10},{9,11},{10,... | collective-permute-start | bytes 1179656 | tf_op jit(solution)/shard_map/ppermute | solution.py:323
  36.8 37.1 %collective-permute-start.2 = (bf16[4,192,256]{2,1,0:T(8,128)(2,1)}, bf16[4,192,256]{2,1,0:T(8,128)(2,1)S(1)}, u32[]{:S(2)}, u32[]{:S(2)}) collective-permute-start(bf16[4,192,256]{2,1,0:T(8,128)(2,1)} %get-tuple-element.30), channel_id=1, source_target_pairs={{0,3},{1,2},{2,1},{3,0},{4,7},{5,6},{6,5},{7,4},{8,11},{9,10},{10,... | collective-permute-start | bytes 1179656 | tf_op jit(solution)/shard_map/ppermute | solution.py:323
  65.9 0.7 copy-start.4
  66.6 0.7 copy-start.6
  67.3 7.8 %collective-permute-start.13 = (bf16[4,192,128]{2,1,0:T(8,128)(2,1)}, bf16[4,192,128]{2,1,0:T(8,128)(2,1)S(1)}, u32[]{:S(2)}, u32[]{:S(2)}) collective-permute-start(bf16[4,192,128]{2,1,0:T(8,128)(2,1)} %get-tuple-element.42), channel_id=1, source_target_pairs={{0,1},{1,0},{2,3},{3,2},{4,5},{5,4},{6,7},{7,6},{8,9},{9,8},{10,11... | collective-permute-start | bytes 589832 | tf_op jit(solution)/shard_map/ppermute | solution.py:323
  68.6 16.7 %collective-permute-start.14 = (bf16[4,192,128]{2,1,0:T(8,128)(2,1)S(1)}, bf16[4,192,128]{2,1,0:T(8,128)(2,1)S(1)}, u32[]{:S(2)}, u32[]{:S(2)}) collective-permute-start(bf16[4,192,128]{2,1,0:T(8,128)(2,1)S(1)} %get-tuple-element.43), channel_id=1, source_target_pairs={{0,2},{1,3},{2,0},{3,1},{4,6},{5,7},{6,4},{7,5},{8,10},{9,11},{10,... | collective-permute-start | bytes 589832 | tf_op jit(solution)/shard_map/ppermute | solution.py:323
  68.8 29.4 %collective-permute-start.15 = (bf16[4,192,128]{2,1,0:T(8,128)(2,1)S(1)}, bf16[4,192,128]{2,1,0:T(8,128)(2,1)}, u32[]{:S(2)}, u32[]{:S(2)}) collective-permute-start(bf16[4,192,128]{2,1,0:T(8,128)(2,1)S(1)} %get-tuple-element.44), channel_id=1, source_target_pairs={{0,3},{1,2},{2,1},{3,0},{4,7},{5,6},{6,5},{7,4},{8,11},{9,10},{10,... | collective-permute-start | bytes 589832 | tf_op jit(solution)/shard_map/ppermute | solution.py:323
  71.6 44.5 %collective-permute-start.7 = (bf16[4,192,128]{2,1,0:T(8,128)(2,1)}, bf16[4,192,128]{2,1,0:T(8,128)(2,1)S(1)}, u32[]{:S(2)}, u32[]{:S(2)}) collective-permute-start(bf16[4,192,128]{2,1,0:T(8,128)(2,1)} %get-tuple-element.34), channel_id=1, source_target_pairs={{0,1},{1,0},{2,3},{3,2},{4,5},{5,4},{6,7},{7,6},{8,9},{9,8},{10,11... | collective-permute-start | bytes 589832 | tf_op jit(solution)/shard_map/ppermute | solution.py:323
  73.9 42.8 %collective-permute-start.8 = (bf16[4,192,128]{2,1,0:T(8,128)(2,1)}, bf16[4,192,128]{2,1,0:T(8,128)(2,1)S(1)}, u32[]{:S(2)}, u32[]{:S(2)}) collective-permute-start(bf16[4,192,128]{2,1,0:T(8,128)(2,1)} %get-tuple-element.35), channel_id=1, source_target_pairs={{0,2},{1,3},{2,0},{3,1},{4,6},{5,7},{6,4},{7,5},{8,10},{9,11},{10,... | collective-permute-start | bytes 589832 | tf_op jit(solution)/shard_map/ppermute | solution.py:323
  75.1 0.7 copy-start.8
  75.8 40.9 %collective-permute-start.9 = (bf16[4,192,128]{2,1,0:T(8,128)(2,1)}, bf16[4,192,128]{2,1,0:T(8,128)(2,1)S(1)}, u32[]{:S(2)}, u32[]{:S(2)}) collective-permute-start(bf16[4,192,128]{2,1,0:T(8,128)(2,1)} %get-tuple-element.36), channel_id=1, source_target_pairs={{0,3},{1,2},{2,1},{3,0},{4,7},{5,6},{6,5},{7,4},{8,11},{9,10},{10,... | collective-permute-start | bytes 589832 | tf_op jit(solution)/shard_map/ppermute | solution.py:323
  85.3 0.7 copy-start.10
  98.2 0.9 copy-start.7
  99.2 0.9 copy-start.9
  100.1 0.9 copy-start.11
  101.0 15.7 %copy-start.5 = (bf16[4,192,128]{2,1,0:T(8,128)(2,1)S(1)}, bf16[4,192,128]{2,1,0:T(8,128)(2,1)}, u32[]{:S(2)}) copy-start(bf16[4,192,128]{2,1,0:T(8,128)(2,1)} %copy-done.4) | copy-start | bytes 589828
  113.1 17.8 %collective-permute-start.16 = (bf16[2,4,192,128]{3,2,1,0:T(8,128)(2,1)S(1)}, bf16[2,4,192,128]{3,2,1,0:T(8,128)(2,1)S(1)}, u32[]{:S(2)}, u32[]{:S(2)}) collective-permute-start(bf16[2,4,192,128]{3,2,1,0:T(8,128)(2,1)S(1)} %get-tuple-element.46), channel_id=1, source_target_pairs={{0,1},{1,0},{2,3},{3,2},{4,5},{5,4},{6,7},{7,6},{8,9},{9,8},{10,11... | collective-permute-start | bytes 1179656 | tf_op jit(solution)/shard_map/ppermute | solution.py:323
  113.2 29.3 %collective-permute-start.17 = (bf16[2,4,192,128]{3,2,1,0:T(8,128)(2,1)S(1)}, bf16[2,4,192,128]{3,2,1,0:T(8,128)(2,1)S(1)}, u32[]{:S(2)}, u32[]{:S(2)}) collective-permute-start(bf16[2,4,192,128]{3,2,1,0:T(8,128)(2,1)S(1)} %get-tuple-element.47), channel_id=1, source_target_pairs={{0,2},{1,3},{2,0},{3,1},{4,6},{5,7},{6,4},{7,5},{8,10},{9,11},{10,... | collective-permute-start | bytes 1179656 | tf_op jit(solution)/shard_map/ppermute | solution.py:323
  116.1 52.8 %collective-permute-start.18 = (bf16[2,4,192,128]{3,2,1,0:T(8,128)(2,1)S(1)}, bf16[2,4,192,128]{3,2,1,0:T(8,128)(2,1)S(1)}, u32[]{:S(2)}, u32[]{:S(2)}) collective-permute-start(bf16[2,4,192,128]{3,2,1,0:T(8,128)(2,1)S(1)} %get-tuple-element.48), channel_id=1, source_target_pairs={{0,3},{1,2},{2,1},{3,0},{4,7},{5,6},{6,5},{7,4},{8,11},{9,10},{10,... | collective-permute-start | bytes 1179656 | tf_op jit(solution)/shard_map/ppermute | solution.py:323
  127.9 43.2 %collective-permute-start.10 = (bf16[2,4,192,128]{3,2,1,0:T(8,128)(2,1)S(1)}, bf16[2,4,192,128]{3,2,1,0:T(8,128)(2,1)S(1)}, u32[]{:S(2)}, u32[]{:S(2)}) collective-permute-start(bf16[2,4,192,128]{3,2,1,0:T(8,128)(2,1)S(1)} %get-tuple-element.38), channel_id=1, source_target_pairs={{0,1},{1,0},{2,3},{3,2},{4,5},{5,4},{6,7},{7,6},{8,9},{9,8},{10,11... | collective-permute-start | bytes 1179656 | tf_op jit(solution)/shard_map/ppermute | solution.py:323
  129.0 47.3 %collective-permute-start.11 = (bf16[2,4,192,128]{3,2,1,0:T(8,128)(2,1)S(1)}, bf16[2,4,192,128]{3,2,1,0:T(8,128)(2,1)S(1)}, u32[]{:S(2)}, u32[]{:S(2)}) collective-permute-start(bf16[2,4,192,128]{3,2,1,0:T(8,128)(2,1)S(1)} %get-tuple-element.39), channel_id=1, source_target_pairs={{0,2},{1,3},{2,0},{3,1},{4,6},{5,7},{6,4},{7,5},{8,10},{9,11},{10,... | collective-permute-start | bytes 1179656 | tf_op jit(solution)/shard_map/ppermute | solution.py:323
  130.9 53.4 %collective-permute-start.12 = (bf16[2,4,192,128]{3,2,1,0:T(8,128)(2,1)S(1)}, bf16[2,4,192,128]{3,2,1,0:T(8,128)(2,1)S(1)}, u32[]{:S(2)}, u32[]{:S(2)}) collective-permute-start(bf16[2,4,192,128]{3,2,1,0:T(8,128)(2,1)S(1)} %get-tuple-element.40), channel_id=1, source_target_pairs={{0,3},{1,2},{2,1},{3,0},{4,7},{5,6},{6,5},{7,4},{8,11},{9,10},{10,... | collective-permute-start | bytes 1179656 | tf_op jit(solution)/shard_map/ppermute | solution.py:323

commit v2 on v1

--- a/solution.py
+++ b/solution.py
@@ -27,9 +27,10 @@
     return (k < 6) | (k >= 18)
 
 
-def pack_kernel(raw, to_east, to_west):
+def pack_kernel(raw, code, to_east, to_west):
+    step = pl.program_id(0)
     for out, runs, low in ((to_east, ((0, 6), (18, 24)), 4), (to_west, ((6, 18),), 0)):
-        at = 0
+        at = step * (K // 2)
         for first, last in runs:
             one = raw[first:last].astype(jnp.float32)
             two = raw[K + first : K + last].astype(jnp.float32)
@@ -38,26 +39,30 @@
                 both = jnp.where(row < 4, pltpu.roll(one, 4, 1), two)
             else:
                 both = jnp.where(row < 4, one, pltpu.roll(two, 4, 1))
-            out[at : at + last - first] = both.astype(jnp.bfloat16)
+            out[pl.ds(at, last - first)] = both.astype(jnp.bfloat16)
             at += last - first
-
-
-def pack_halo(spectrum):
+        out[out.shape[0] - 1] = code[...].astype(jnp.float32).astype(jnp.bfloat16)
+
+
+def pack_halo(spectrum, code):
     comps, columns, rows = spectrum.shape
-    half = jax.ShapeDtypeStruct((comps // 4, columns, rows), jnp.bfloat16)
-    block = pl.BlockSpec((K // 2, columns, rows), lambda i: (i, 0, 0))
+    half = jax.ShapeDtypeStruct((comps // 4 + 1, columns, rows), jnp.bfloat16)
+    block = pl.BlockSpec(half.shape, lambda i: (0, 0, 0))
     return pl.pallas_call(
         pack_kernel,
         grid=(comps // PAIR,),
-        in_specs=[pl.BlockSpec((PAIR, columns, rows), lambda i: (i, 0, 0))],
+        in_specs=[
+            pl.BlockSpec((PAIR, columns, rows), lambda i: (i, 0, 0)),
+            pl.BlockSpec(code.shape, lambda i: (0, 0)),
+        ],
         out_specs=[block, block],
         out_shape=[half, half],
         compiler_params=pltpu.CompilerParams(vmem_limit_bytes=VMEM_LIMIT),
         name="pack_halo",
-    )(spectrum)
-
-
-def propagate_kernel(with_halo, parts, pos, *refs):
+    )(spectrum, code)
+
+
+def propagate_kernel(with_halo, parts, skip, pos, *refs):
     if with_halo:
         raw, west, east, code, code_west, code_east, table, trig = refs[:8]
         refs = refs[8:]
@@ -93,13 +98,13 @@
     if with_halo:
         turned = pltpu.roll(code[...], 4, 0)
         codes = (
-            jnp.where(row8 < 4, pltpu.roll(code_west[...], 4, 0), turned),
-            jnp.where(row8 < 4, turned, pltpu.roll(code_east[...], 4, 0)),
+            jnp.where(row8 < 4, pltpu.roll(code_west[0].astype(jnp.float32).astype(jnp.int32), 4, 0), turned),
+            jnp.where(row8 < 4, turned, pltpu.roll(code_east[0].astype(jnp.float32).astype(jnp.int32), 4, 0)),
         )
     else:
         codes = (code[...],)
     lane = lax.broadcasted_iota(jnp.int32, (8, rows), 1)
-    freq0 = step * 2
+    freq0 = (skip + step) * 2
     for f in range(2):
         line = jnp.broadcast_to(table[freq0 + f], (8, LANES))
         for n, c in enumerate(codes):
@@ -148,21 +153,18 @@
                     return pltpu.roll(e, rows - 1, 1)
                 return jnp.where(south, pltpu.roll(e, 1, 1), pltpu.roll(e, rows - 1, 1))
 
-            before = None
-            for p in range(8):
-                now = [upwind_order(lambda side, q: column(q), p)]
-                if p:
-                    rate = upwind_order(spread(0), p)
-                    sea = upwind_order(spread(1), p)
-                    keep = sea - rate * (cos + sin)
-                    from_x = rate * cos
-                    from_y = rate * inner_sin
-                    for t in range(1, min(p, PSTEPS) + 1):
-                        e = now[t - 1]
-                        now.append(keep * e + from_x * before[t - 1] + from_y * behind(e))
-                if p >= PSTEPS:
-                    result[p - PSTEPS, f * K + g * 8 : f * K + g * 8 + 8, :] = now[PSTEPS]
-                before = now
+            now = [upwind_order(lambda side, q: column(q), p) for p in range(8)]
+            rates = [upwind_order(spread(0), p) for p in range(1, 8)]
+            seas = [upwind_order(spread(1), p) for p in range(1, 8)]
+            keep = [None] + [sea - rate * (cos + sin) for sea, rate in zip(seas, rates)]
+            from_x = [None] + [rate * cos for rate in rates]
+            from_y = [None] + [rate * inner_sin for rate in rates]
+            for t in range(1, PSTEPS + 1):
+                now = [None] * t + [
+                    keep[p] * now[p] + from_x[p] * now[p - 1] + from_y[p] * behind(now[p]) for p in range(t, 8)
+                ]
+            for p in range(PSTEPS, 8):
+                result[p - PSTEPS, f * K + g * 8 : f * K + g * 8 + 8, :] = now[p]
 
     z = pos[0]
     width = rows // pos_count(parts)
@@ -175,25 +177,27 @@
     return max(s for s, _, _ in parts) + 1
 
 
-def propagate(z, spectrum, code, table, trig, parts, halo=None):
-    comps, columns, rows = spectrum.shape
+def propagate(z, spectrum, code, table, trig, parts, skip, steps, halo=None):
+    columns, rows = spectrum.shape[1:]
+    comps = steps * PAIR
     whole = lambda a: pl.BlockSpec(a.shape, lambda i, z: (0,) * a.ndim)
-    blocked = lambda a, n: pl.BlockSpec((n,) + a.shape[1:], lambda i, z: (i, 0, 0))
+    blocked = lambda a, n: pl.BlockSpec((n,) + a.shape[1:], lambda i, z: (skip + i, 0, 0))
     args, specs = [spectrum], [blocked(spectrum, PAIR)]
     if halo is not None:
-        west, east, code_west, code_east = halo
-        args += [west, east, code, code_west, code_east]
-        specs += [blocked(west, K // 2), blocked(east, K // 2), whole(code), whole(code), whole(code)]
+        west, east = halo
+        last = pl.BlockSpec((1, columns, rows), lambda i, z: (west.shape[0] - 1, 0, 0))
+        args += [west, east, code, west, east]
+        specs += [blocked(west, K // 2), blocked(east, K // 2), whole(code), last, last]
     else:
         args += [code]
         specs += [whole(code)]
     args += [table, trig]
     specs += [whole(table), whole(trig)]
     return pl.pallas_call(
-        functools.partial(propagate_kernel, halo is not None, parts),
+        functools.partial(propagate_kernel, halo is not None, parts, skip),
         grid_spec=pltpu.PrefetchScalarGridSpec(
             num_scalar_prefetch=1,
-            grid=(comps // PAIR,),
+            grid=(steps,),
             in_specs=specs,
             out_specs=[pl.BlockSpec((4, PAIR, size), lambda i, z: (0, i, 0)) for _, _, size in parts],
             scratch_shapes=[
@@ -210,18 +214,18 @@
 
 
 def sources_kernel(count, lane0, pos, *refs):
-    first, second = refs[:count], refs[count : 2 * count]
-    wind_c, wind_s, coupling, trig, rates = refs[2 * count : 2 * count + 5]
-    outs = refs[2 * count + 5 : 3 * count + 5]
-    state, rounded, nonlin, wind = refs[3 * count + 5 :]
-    comps = first[0].shape[1]
-    width = outs[0].shape[3]
+    pieces = len(refs) - 2 * count - 8
+    first, refs = refs[:pieces], refs[pieces:]
+    second, (wind_c, wind_s, coupling, trig) = refs[:count], refs[count : count + 4]
+    outs, (state, rounded, nonlin, wind) = refs[count + 4 : 2 * count + 4], refs[2 * count + 4 :]
+    comps, width = second[0].shape[1:]
     whole = comps * count
     z = pos[0]
     mask = eastward_rows(0, comps)
     for s in range(count):
         at = pl.multiple_of(jnp.bitwise_xor(z, s) * comps, comps)
-        down = first[s][0, :, lane0 : lane0 + width].astype(jnp.float32)
+        down = jnp.concatenate([first[n][0, :, lane0 : lane0 + width] for n in range(s, pieces, count)], axis=0)
+        down = down.astype(jnp.float32)
         up = second[s][0].astype(jnp.float32)
         state[pl.ds(at, comps), 0:width] = jnp.where(mask, up, down)
         state[pl.ds(at, comps), width : 2 * width] = jnp.where(mask, down, up)
@@ -254,7 +258,7 @@
 
 
 def sources(z, first, second, wind_c, wind_s, coupling, trig, lane0):
-    count = len(first)
+    count = len(second)
     comps, width = second[0].shape[1], second[0].shape[2]
     whole = lambda a: pl.BlockSpec(a.shape, lambda i, z: (0,) * a.ndim)
     return pl.pallas_call(
@@ -264,7 +268,7 @@
             grid=(4,),
             in_specs=[pl.BlockSpec((1,) + a.shape[1:], lambda i, z: (3 - i, 0, 0)) for a in first]
             + [pl.BlockSpec((1,) + a.shape[1:], lambda i, z: (i, 0, 0)) for a in second]
-            + [whole(wind_c), whole(wind_s), whole(coupling), whole(trig), whole(trig)],
+            + [whole(wind_c), whole(wind_s), whole(coupling), whole(trig)],
             out_specs=[pl.BlockSpec((2, 1, comps, width), lambda i, z: (0, i, 0, 0))] * count,
             scratch_shapes=[
                 pltpu.VMEM((comps * count, 2 * width), jnp.float32),
@@ -279,7 +283,7 @@
             flops=SRC_STEPS * 2 * (comps * count) ** 2 * 8 * width, bytes_accessed=4 * comps * count * 8 * width, transcendentals=0
         ),
         name="source_terms",
-    )(z, *first, *second, wind_c, wind_s, coupling, trig, trig)
+    )(z, *first, *second, wind_c, wind_s, coupling, trig)
 
 
 def assemble_kernel(count, pos, *refs):
@@ -319,9 +323,8 @@
 
 def exchange(blocks, axis):
     count = len(blocks)
-    return [blocks[0]] + [
-        lax.ppermute(blocks[s], axis, [(i, i ^ s) for i in range(count)]) for s in range(1, count)
-    ]
+    came = {s: lax.ppermute(blocks[s], axis, [(i, i ^ s) for i in range(count)]) for s in range(count - 1, 0, -1)}
+    return [blocks[0]] + [came[s] for s in range(1, count)]
 
 
 def on_device(spectrum, sea_mask, depth_class, group_speed, wind_speed, wind_dir, coupling):
@@ -346,18 +349,16 @@
     dir_part = lax.dynamic_slice_in_dim(wind_dir, start, width, 1)
     wind_c, wind_s = (speed_part * jnp.cos(dir_part))[:, None], (speed_part * jnp.sin(dir_part))[:, None]
 
-    to_east, to_west = pack_halo(spectrum)
-    halo = (
-        lax.ppermute(to_east, "tile", east),
-        lax.ppermute(to_west, "tile", west),
-        lax.ppermute(code, "tile", east),
-        lax.ppermute(code, "tile", west),
-    )
-    first = propagate(z, spectrum, code, table, trig, [(s, 0, width) for s in range(count)])
-    first = exchange(first, "comp")
+    to_east, to_west = pack_halo(spectrum, code)
+    halo = lax.ppermute(to_east, "tile", east), lax.ppermute(to_west, "tile", west)
+    pairs = comps // PAIR
+    parts = [(s, 0, width) for s in range(count)]
+    first = []
+    for skip in range(0, pairs, pairs // 2):
+        first += exchange(propagate(z, spectrum, code, table, trig, parts, skip, pairs // 2), "comp")
     size = width // chunks
     parts = [(s, c * size, size) for c in range(chunks) for s in range(count)]
-    second = propagate(z, spectrum, code, table, trig, parts, halo)
+    second = propagate(z, spectrum, code, table, trig, parts, 0, pairs, halo)
     out = None
     for c in range(chunks):
         arrived = exchange(second[c * count : (c + 1) * count], "comp")

time: 187 us -> 166 us (0.89)
  Pallas kernels: 80.8 us -> 51.3 us
  waiting for transfers between devices: 73.9 us -> 79.8 us
  starting transfers between devices: 22.5 us -> 25.3 us
    pallas_call x2 -> x3, Pallas kernels: 51.2 us -> 21.7 us  [propagate(): pl.pallas_call(functools.partial(propagate_kernel, halo is not None, part...]
    ppermute x15 -> x18, waiting for transfers between devices: 72.8 us -> 77.3 us  [exchange(): lax.ppermute(blocks[s], axis, [(i, i ^ s) for i in range(count)])]
    ppermute x15 -> x18, starting transfers between devices: 19.3 us -> 22.6 us  [exchange(): lax.ppermute(blocks[s], axis, [(i, i ^ s) for i in range(count)])]
    ppermute x1, waiting for transfers between devices: 0.01 us -> 2.46 us  [on_device(): lax.ppermute(to_east, 'tile', east)]
    unnamed x31 -> x29, local copies, waits for them, and re-layouts: 7.5 us -> 7.48 us
  transfers between devices with their start and end apart: 19 -> 20, of which waited for: 8 -> 8; matrix products, arithmetic and copies ran while one was open for 1% -> 1% of each run, Pallas kernels for 41% -> 29%
where the time goes in v2:
time: 166 us
  waiting for transfers between devices  79.8 us (48%)
  Pallas kernels  51.3 us (31%)
  starting transfers between devices  25.3 us (15%)
  local copies, waits for them, and re-layouts  7.72 us (5%)
    ppermute x18, waiting for transfers between devices, exchange(): lax.ppermute(blocks[s], axis, [(i, i ^ s) for i in range(count)])  77.3 us
    pallas_call x2, Pallas kernels, sources(): pl.pallas_call(functools.partial(sources_kernel, count, lane0), grid_spec...  23.3 us
    ppermute x18, starting transfers between devices, exchange(): lax.ppermute(blocks[s], axis, [(i, i ^ s) for i in range(count)])  22.6 us
    pallas_call x3, Pallas kernels, propagate(): pl.pallas_call(functools.partial(propagate_kernel, halo is not None, part...  21.7 us
    unnamed x29, local copies, waits for them, and re-layouts  7.48 us
    pallas_call x2, Pallas kernels, assemble(): pl.pallas_call(functools.partial(assemble_kernel, count), grid_spec=pltpu...  4.53 us
  transfers between devices with their start and end apart: 20, of which 8 were waited for; matrix products, arithmetic and copies ran while one was open for 1% of the time, Pallas kernels for 29%

profile of v2, /device:TPU:8, one launch (start us, length us, event | category | flops | bytes accessed | tf_op | source)
XLA Modules:
  0.0 165.8 jit_solution(13434727659364833325)
XLA Ops:
  0.0 0.8 multiply_add_fusion.refs_1_.code.refs_3_
  0.8 1.9 %copy-done.1 = bf16[192,8,1024]{2,1,0:T(8,128)(2,1)S(1)} copy-done((bf16[192,8,1024]{2,1,0:T(8,128)(2,1)S(1)}, bf16[192,8,1024]{2,1,0:T(8,128)(2,1)}, u32[]{:S(2)}) %copy-start.1) | copy-done | bytes 3145752
  2.7 1.7 %pack_halo.1 = (bf16[49,8,1024]{2,1,0:T(8,128)(2,1)}, bf16[49,8,1024]{2,1,0:T(8,128)(2,1)}) custom-call(bf16[192,8,1024]{2,1,0:T(8,128)(2,1)S(1)} %copy-done.1, s32[8,1024]{1,0:T(8,128)S(1)} %multiply_add_fusion.refs_1_.code.refs_3_), custom_call_target="tpu_custom_call" | custom-call | tf_op jit(solution)/shard_map/pack_halo/pallas_call | solution.py:51
  4.4 0.0 collective-permute-start.6
  4.4 2.6 %collective-permute-start.7 = (bf16[49,8,1024]{2,1,0:T(8,128)(2,1)}, bf16[49,8,1024]{2,1,0:T(8,128)(2,1)}, u32[]{:S(2)}, u32[]{:S(2)}) collective-permute-start(bf16[49,8,1024]{2,1,0:T(8,128)(2,1)} %get-tuple-element.40), channel_id=1, source_target_pairs={{4,0},{8,4},{12,8},{16,12},{20,16},{24,20},{28,24},{0,28},{5,1},{9... | collective-permute-start | bytes 2408456 | tf_op jit(solution)/shard_map/ppermute | solution.py:353
  7.0 0.0 copy-done
  7.0 0.1 constant_dynamic-slice_fusion
  7.1 0.1 copy.14
  7.2 0.1 broadcast_in_dim.22.refs_3_.refs_7_
  7.3 4.6 %propagate_downwind.3 = (bf16[4,96,256]{2,1,0:T(8,128)(2,1)S(1)}, bf16[4,96,256]{2,1,0:T(8,128)(2,1)S(1)}, bf16[4,96,256]{2,1,0:T(8,128)(2,1)S(1)}, bf16[4,96,256]{2,1,0:T(8,128)(2,1)S(1)}) custom-call(s32[1]{0:T(128)} %bitcast.pos, bf16[192,8,1024]{2,1,0:T(8,128)(2,1)S(1)} %copy-done.2, s32[8,1024]{1,0:T(8,128)S(1)} %multiply_add_fusion.refs_1_.code.refs_3_, ...), custom_call_target="tpu_custom_call" | custom-call | flops 23592960 | bytes 4718592 | tf_op jit(solution)/shard_map/propagate_downwind/pallas_call | solution.py:196
  11.9 0.1 collective-permute-start.3
  12.0 3.0 %collective-permute-start.4 = (bf16[4,96,256]{2,1,0:T(8,128)(2,1)S(1)}, bf16[4,96,256]{2,1,0:T(8,128)(2,1)S(1)}, u32[]{:S(2)}, u32[]{:S(2)}) collective-permute-start(bf16[4,96,256]{2,1,0:T(8,128)(2,1)S(1)} %get-tuple-element.37), channel_id=1, source_target_pairs={{0,2},{1,3},{2,0},{3,1},{4,6},{5,7},{6,4},{7,5},{8,10},{9,11},{10,... | collective-permute-start | bytes 589832 | tf_op jit(solution)/shard_map/ppermute | solution.py:326
  15.0 0.4 collective-permute-start.5
  15.4 5.3 %propagate_downwind.2 = (bf16[4,96,256]{2,1,0:T(8,128)(2,1)S(1)}, bf16[4,96,256]{2,1,0:T(8,128)(2,1)S(1)}, bf16[4,96,256]{2,1,0:T(8,128)(2,1)}, bf16[4,96,256]{2,1,0:T(8,128)(2,1)}) custom-call(s32[1]{0:T(128)} %bitcast.pos, bf16[192,8,1024]{2,1,0:T(8,128)(2,1)S(1)} %copy-done.2, s32[8,1024]{1,0:T(8,128)S(1)} %multiply_add_fusion.refs_1_.code.refs_3_, ...), custom_call_target="tpu_custom_call" | custom-call | flops 23592960 | bytes 4718592 | tf_op jit(solution)/shard_map/propagate_downwind/pallas_call | solution.py:196
  20.7 0.7 copy-done.10
  21.4 2.5 %collective-permute-done.6.refs_1_.refs_4_ = bf16[49,8,1024]{2,1,0:T(8,128)(2,1)} collective-permute-done((bf16[49,8,1024]{2,1,0:T(8,128)(2,1)}, bf16[49,8,1024]{2,1,0:T(8,128)(2,1)}, u32[]{:S(2)}, u32[]{:S(2)}) %collective-permute-start.6) | collective-permute-done | bytes 802848 | tf_op jit(solution)/shard_map/ppermute | solution.py:353
  23.9 0.0 collective-permute-start
  23.9 0.0 collective-permute-done.7.refs_2_.refs_5_
  23.9 3.1 %collective-permute-start.1 = (bf16[4,96,256]{2,1,0:T(8,128)(2,1)}, bf16[4,96,256]{2,1,0:T(8,128)(2,1)S(1)}, u32[]{:S(2)}, u32[]{:S(2)}) collective-permute-start(bf16[4,96,256]{2,1,0:T(8,128)(2,1)} %get-tuple-element.33), channel_id=1, source_target_pairs={{0,2},{1,3},{2,0},{3,1},{4,6},{5,7},{6,4},{7,5},{8,10},{9,11},{10,... | collective-permute-start | bytes 589832 | tf_op jit(solution)/shard_map/ppermute | solution.py:326
  27.0 11.8 %propagate_upwind.1 = (bf16[4,192,128]{2,1,0:T(8,128)(2,1)S(1)}, bf16[4,192,128]{2,1,0:T(8,128)(2,1)}, bf16[4,192,128]{2,1,0:T(8,128)(2,1)}, bf16[4,192,128]{2,1...) custom-call(s32[1]{0:T(128)} %bitcast.pos, ...), custom_call_target="tpu_custom_call" | custom-call | flops 47185920 | bytes 9437184 | tf_op jit(solution)/shard_map/propagate_upwind/pallas_call | solution.py:196
  38.8 0.0 collective-permute-done.3.refs_5_
  38.8 0.7 copy-done.4
  39.5 0.5 collective-permute-start.2
  40.0 0.0 collective-permute-done.4.refs_6_
  40.0 0.7 copy-done.6
  40.7 1.1 collective-permute-start.14
  41.8 0.0 collective-permute-done.5.refs_7_
  41.8 0.7 copy-done.8
  42.5 2.3 %collective-permute-start.15 = (bf16[4,192,128]{2,1,0:T(8,128)(2,1)}, bf16[4,192,128]{2,1,0:T(8,128)(2,1)}, u32[]{:S(2)}, u32[]{:S(2)}) collective-permute-start(bf16[4,192,128]{2,1,0:T(8,128)(2,1)} %get-tuple-element.51), channel_id=1, source_target_pairs={{0,2},{1,3},{2,0},{3,1},{4,6},{5,7},{6,4},{7,5},{8,10},{9,11},{10,... | collective-permute-start | bytes 589832 | tf_op jit(solution)/shard_map/ppermute | solution.py:326
  44.8 0.0 collective-permute-done.refs_1_
  44.8 0.6 collective-permute-start.16
  45.4 0.8 sine_multiply_fusion
  46.2 0.0 collective-permute-done.1.refs_2_
  46.2 1.5 collective-permute-start.8
  47.7 3.8 %collective-permute-done.2.refs_3_ = bf16[4,96,256]{2,1,0:T(8,128)(2,1)S(1)} collective-permute-done((bf16[4,96,256]{2,1,0:T(8,128)(2,1)}, bf16[4,96,256]{2,1,0:T(8,128)(2,1)S(1)}, u32[]{:S(2)}, u32[]{:S(2)}) %collective-permute-start.2) | collective-permute-done | bytes 196640 | tf_op jit(solution)/shard_map/ppermute | solution.py:326
  51.5 0.0 collective-permute-start.9
  51.5 0.0 collective-permute-done.14.refs_9_
  51.5 2.8 %collective-permute-start.10 = (bf16[4,192,128]{2,1,0:T(8,128)(2,1)S(1)}, bf16[4,192,128]{2,1,0:T(8,128)(2,1)S(1)}, u32[]{:S(2)}, u32[]{:S(2)}) collective-permute-start(bf16[4,192,128]{2,1,0:T(8,128)(2,1)S(1)} %get-tuple-element.44), channel_id=1, source_target_pairs={{0,3},{1,2},{2,1},{3,0},{4,7},{5,6},{6,5},{7,4},{8,11},{9,10},{10,... | collective-permute-start | bytes 589832 | tf_op jit(solution)/shard_map/ppermute | solution.py:326
  54.4 8.2 %collective-permute-done.15.refs_10_ = bf16[4,192,128]{2,1,0:T(8,128)(2,1)} collective-permute-done((bf16[4,192,128]{2,1,0:T(8,128)(2,1)}, bf16[4,192,128]{2,1,0:T(8,128)(2,1)}, u32[]{:S(2)}, u32[]{:S(2)}) %collective-permute-start.15) | collective-permute-done | bytes 196640 | tf_op jit(solution)/shard_map/ppermute | solution.py:326
  62.5 14.4 %collective-permute-done.16.refs_11_ = bf16[4,192,128]{2,1,0:T(8,128)(2,1)} collective-permute-done((bf16[4,192,128]{2,1,0:T(8,128)(2,1)S(1)}, bf16[4,192,128]{2,1,0:T(8,128)(2,1)}, u32[]{:S(2)}, u32[]{:S(2)}) %collective-permute-start.16) | collective-permute-done | bytes 196640 | tf_op jit(solution)/shard_map/ppermute | solution.py:326
  76.9 0.0 copy-done.12
  76.9 0.1 broadcast_in_dim.25.refs_15_
  77.0 0.9 copy-done.5
  77.9 0.9 copy-done.7
  78.9 0.9 copy-done.9
  79.8 12.1 %source_terms.3 = (bf16[2,4,192,128]{3,2,1,0:T(8,128)(2,1)S(1)}, bf16[2,4,192,128]{3,2,1,0:T(8,128)(2,1)S(1)}, bf16[2,4,192,128]{3,2,1,0:T(8,128)(2,1)S(1)}, bf16[2,4,192,128]{3,2,1,0:T(8,128)(2,1)S(1)}) custom-call(s32[1]{0:T(128)} %bitcast.pos, bf16[4,96,256]{2,1,0:T(8,128)(2,1)S(1)} %copy-done.11, bf16[4,96,256]{2,1,0:T(8,128)(2,1)S(1)} %collective-permute-done.refs_1_, ...), custom_call_target="tpu_custom_call" | custom-call | flops 4831838208 | bytes 3145728 | tf_op jit(solution)/shard_map/source_terms/pallas_call | solution.py:264
  91.9 0.1 collective-permute-start.17
  92.0 2.1 %collective-permute-start.18 = (bf16[2,4,192,128]{3,2,1,0:T(8,128)(2,1)S(1)}, bf16[2,4,192,128]{3,2,1,0:T(8,128)(2,1)S(1)}, u32[]{:S(2)}, u32[]{:S(2)}) collective-permute-start(bf16[2,4,192,128]{3,2,1,0:T(8,128)(2,1)S(1)} %get-tuple-element.55), channel_id=1, source_target_pairs={{0,2},{1,3},{2,0},{3,1},{4,6},{5,7},{6,4},{7,5},{8,10},{9,11},{10,... | collective-permute-start | bytes 1179656 | tf_op jit(solution)/shard_map/ppermute | solution.py:326
  94.1 0.0 collective-permute-done.8.refs_9_
  94.2 1.3 collective-permute-start.19
  95.5 0.0 collective-permute-done.9.refs_10_
  95.5 0.0 collective-permute-done.10.refs_11_
  95.5 11.2 %source_terms.2 = (bf16[2,4,192,128]{3,2,1,0:T(8,128)(2,1)S(1)}, bf16[2,4,192,128]{3,2,1,0:T(8,128)(2,1)S(1)}, bf16[2,4,192,128]{3,2,1,0:T(8,128)(2,1)S(1)}, bf16[2,4,192,128]{3,2,1,0:T(8,128)(2,1)S(1)}) custom-call(s32[1]{0:T(128)} %bitcast.pos, bf16[4,96,256]{2,1,0:T(8,128)(2,1)S(1)} %copy-done.11, bf16[4,96,256]{2,1,0:T(8,128)(2,1)S(1)} %collective-permute-done.refs_1_, ...), custom_call_target="tpu_custom_call" | custom-call | flops 4831838208 | bytes 3145728 | tf_op jit(solution)/shard_map/source_terms/pallas_call | solution.py:264
  106.7 1.0 collective-permute-start.11
  107.7 1.2 collective-permute-start.12
  108.9 0.0 collective-permute-done.17.refs_1_
  108.9 1.3 collective-permute-start.13
  110.3 10.2 %collective-permute-done.18.refs_2_ = bf16[2,4,192,128]{3,2,1,0:T(8,128)(2,1)S(1)} collective-permute-done((bf16[2,4,192,128]{3,2,1,0:T(8,128)(2,1)S(1)}, bf16[2,4,192,128]{3,2,1,0:T(8,128)(2,1)S(1)}, u32[]{:S(2)}, u32[]{:S(2)}) %collective-permute-start.18) | collective-permute-done | bytes 393248 | tf_op jit(solution)/shard_map/ppermute | solution.py:326
  120.4 27.2 %collective-permute-done.19.refs_3_ = bf16[2,4,192,128]{3,2,1,0:T(8,128)(2,1)S(1)} collective-permute-done((bf16[2,4,192,128]{3,2,1,0:T(8,128)(2,1)S(1)}, bf16[2,4,192,128]{3,2,1,0:T(8,128)(2,1)S(1)}, u32[]{:S(2)}, u32[]{:S(2)}) %collective-permute-start.19) | collective-permute-done | bytes 393248 | tf_op jit(solution)/shard_map/ppermute | solution.py:326
  147.6 2.3 %assemble.2.refs_4_ = bf16[192,8,1024]{2,1,0:T(8,128)(2,1)} custom-call(s32[1]{0:T(128)} %bitcast.pos, bf16[2,4,192,128]{3,2,1,0:T(8,128)(2,1)S(1)} %get-tuple-element.53.refs_0_, bf16[2,4,192,128]{3,2,1,0:T(8,128)(2,1)S(1)} %collective-permute-done.17.refs_1_, bf16[2,4,192,128]{3,2,1,0:T(8,128)(2,1)S(1)} %collective-permute-done.18.refs_2_, ...), custom_call_target="tpu_custom_call" | custom-call | tf_op jit(solution)/shard_map/assemble/pallas_call | solution.py:307
  149.9 0.0 collective-permute-done.11.refs_1_
  149.9 4.4 %collective-permute-done.12.refs_2_ = bf16[2,4,192,128]{3,2,1,0:T(8,128)(2,1)S(1)} collective-permute-done((bf16[2,4,192,128]{3,2,1,0:T(8,128)(2,1)S(1)}, bf16[2,4,192,128]{3,2,1,0:T(8,128)(2,1)S(1)}, u32[]{:S(2)}, u32[]{:S(2)}) %collective-permute-start.12) | collective-permute-done | bytes 393248 | tf_op jit(solution)/shard_map/ppermute | solution.py:326
  154.3 9.2 %collective-permute-done.13.refs_3_ = bf16[2,4,192,128]{3,2,1,0:T(8,128)(2,1)S(1)} collective-permute-done((bf16[2,4,192,128]{3,2,1,0:T(8,128)(2,1)S(1)}, bf16[2,4,192,128]{3,2,1,0:T(8,128)(2,1)S(1)}, u32[]{:S(2)}, u32[]{:S(2)}) %collective-permute-start.13) | collective-permute-done | bytes 393248 | tf_op jit(solution)/shard_map/ppermute | solution.py:326
  163.5 2.3 %assemble.3 = bf16[192,8,1024]{2,1,0:T(8,128)(2,1)} custom-call(s32[1]{0:T(128)} %bitcast.pos, bf16[2,4,192,128]{3,2,1,0:T(8,128)(2,1)S(1)} %get-tuple-element.45.refs_0_, bf16[2,4,192,128]{3,2,1,0:T(8,128)(2,1)S(1)} %collective-permute-done.11.refs_1_, bf16[2,4,192,128]{3,2,1,0:T(8,128)(2,1)S(1)} %collective-permute-done.12.refs_2_, ...), custom_call_target="tpu_custom_call", output_to_operand_aliasing={{}: (5, {})} | custom-call | tf_op jit(solution)/shard_map/assemble/pallas_call | solution.py:307
  (21 shorter events, 0.1 us)
Async XLA Ops:
  0.0 7.0 %copy-start = (f32[16,32]{1,0:T(8,128)S(1)}, f32[16,32]{1,0:T(8,128)}, u32[]{:S(2)}) copy-start(f32[16,32]{1,0:T(8,128)} %param.12) | copy-start | bytes 6148
  0.0 7.2 %copy-start.13 = (f32[2,24]{1,0:T(2,128)S(1)}, f32[2,24]{1,0:T(2,128)}, u32[]{:S(2)}) copy-start(f32[2,24]{1,0:T(2,128)} %constant.24.clone) | copy-start | bytes 580
  0.8 1.9 %copy-start.1 = (bf16[192,8,1024]{2,1,0:T(8,128)(2,1)S(1)}, bf16[192,8,1024]{2,1,0:T(8,128)(2,1)}, u32[]{:S(2)}) copy-start(bf16[192,8,1024]{2,1,0:T(8,128)(2,1)} %refs_0_.5) | copy-start | bytes 9437188
  2.7 4.5 %copy-start.2 = (bf16[192,8,1024]{2,1,0:T(8,128)(2,1)S(1)}, bf16[192,8,1024]{2,1,0:T(8,128)(2,1)}, u32[]{:S(2)}) copy-start(bf16[192,8,1024]{2,1,0:T(8,128)(2,1)} %refs_0_.5) | copy-start | bytes 9437188
  4.4 19.5 %collective-permute-start.6 = (bf16[49,8,1024]{2,1,0:T(8,128)(2,1)}, bf16[49,8,1024]{2,1,0:T(8,128)(2,1)}, u32[]{:S(2)}, u32[]{:S(2)}) collective-permute-start(bf16[49,8,1024]{2,1,0:T(8,128)(2,1)} %get-tuple-element.39), channel_id=1, source_target_pairs={{0,4},{4,8},{8,12},{12,16},{16,20},{20,24},{24,28},{28,0},{1,5},{5... | collective-permute-start | bytes 2408456 | tf_op jit(solution)/shard_map/ppermute | solution.py:353
  4.4 19.5 %collective-permute-start.7 = (bf16[49,8,1024]{2,1,0:T(8,128)(2,1)}, bf16[49,8,1024]{2,1,0:T(8,128)(2,1)}, u32[]{:S(2)}, u32[]{:S(2)}) collective-permute-start(bf16[49,8,1024]{2,1,0:T(8,128)(2,1)} %get-tuple-element.40), channel_id=1, source_target_pairs={{4,0},{8,4},{12,8},{16,12},{20,16},{24,20},{28,24},{0,28},{5,1},{9... | collective-permute-start | bytes 2408456 | tf_op jit(solution)/shard_map/ppermute | solution.py:353
  11.9 26.9 %collective-permute-start.3 = (bf16[4,96,256]{2,1,0:T(8,128)(2,1)S(1)}, bf16[4,96,256]{2,1,0:T(8,128)(2,1)S(1)}, u32[]{:S(2)}, u32[]{:S(2)}) collective-permute-start(bf16[4,96,256]{2,1,0:T(8,128)(2,1)S(1)} %get-tuple-element.36), channel_id=1, source_target_pairs={{0,1},{1,0},{2,3},{3,2},{4,5},{5,4},{6,7},{7,6},{8,9},{9,8},{10,11... | collective-permute-start | bytes 589832 | tf_op jit(solution)/shard_map/ppermute | solution.py:326
  12.0 28.0 %collective-permute-start.4 = (bf16[4,96,256]{2,1,0:T(8,128)(2,1)S(1)}, bf16[4,96,256]{2,1,0:T(8,128)(2,1)S(1)}, u32[]{:S(2)}, u32[]{:S(2)}) collective-permute-start(bf16[4,96,256]{2,1,0:T(8,128)(2,1)S(1)} %get-tuple-element.37), channel_id=1, source_target_pairs={{0,2},{1,3},{2,0},{3,1},{4,6},{5,7},{6,4},{7,5},{8,10},{9,11},{10,... | collective-permute-start | bytes 589832 | tf_op jit(solution)/shard_map/ppermute | solution.py:326
  15.0 26.8 %collective-permute-start.5 = (bf16[4,96,256]{2,1,0:T(8,128)(2,1)S(1)}, bf16[4,96,256]{2,1,0:T(8,128)(2,1)S(1)}, u32[]{:S(2)}, u32[]{:S(2)}) collective-permute-start(bf16[4,96,256]{2,1,0:T(8,128)(2,1)S(1)} %get-tuple-element.38), channel_id=1, source_target_pairs={{0,3},{1,2},{2,1},{3,0},{4,7},{5,6},{6,5},{7,4},{8,11},{9,10},{10,... | collective-permute-start | bytes 589832 | tf_op jit(solution)/shard_map/ppermute | solution.py:326
  20.7 0.7 copy-start.10
  23.9 21.0 %collective-permute-start = (bf16[4,96,256]{2,1,0:T(8,128)(2,1)S(1)}, bf16[4,96,256]{2,1,0:T(8,128)(2,1)S(1)}, u32[]{:S(2)}, u32[]{:S(2)}) collective-permute-start(bf16[4,96,256]{2,1,0:T(8,128)(2,1)S(1)} %get-tuple-element.32), channel_id=1, source_target_pairs={{0,1},{1,0},{2,3},{3,2},{4,5},{5,4},{6,7},{7,6},{8,9},{9,8},{10,11... | collective-permute-start | bytes 589832 | tf_op jit(solution)/shard_map/ppermute | solution.py:326
  23.9 53.0 %copy-start.12 = (f32[2,24]{1,0:T(2,128)S(1)}, f32[2,24]{1,0:T(2,128)}, u32[]{:S(2)}) copy-start(f32[2,24]{1,0:T(2,128)} %constant.25.clone) | copy-start | bytes 580
  23.9 53.1 %copy-start.3 = (bf16[768,768]{1,0:T(8,128)(2,1)S(1)}, bf16[768,768]{1,0:T(8,128)(2,1)}, u32[]{:S(2)}) copy-start(bf16[768,768]{1,0:T(8,128)(2,1)} %refs_14_.3) | copy-start | bytes 3538948
  23.9 53.1 %copy-start.11 = (bf16[4,96,256]{2,1,0:T(8,128)(2,1)S(1)}, bf16[4,96,256]{2,1,0:T(8,128)(2,1)}, u32[]{:S(2)}) copy-start(bf16[4,96,256]{2,1,0:T(8,128)(2,1)} %copy-done.10) | copy-start | bytes 589828
  23.9 22.3 %collective-permute-start.1 = (bf16[4,96,256]{2,1,0:T(8,128)(2,1)}, bf16[4,96,256]{2,1,0:T(8,128)(2,1)S(1)}, u32[]{:S(2)}, u32[]{:S(2)}) collective-permute-start(bf16[4,96,256]{2,1,0:T(8,128)(2,1)} %get-tuple-element.33), channel_id=1, source_target_pairs={{0,2},{1,3},{2,0},{3,1},{4,6},{5,7},{6,4},{7,5},{8,10},{9,11},{10,... | collective-permute-start | bytes 589832 | tf_op jit(solution)/shard_map/ppermute | solution.py:326
  38.8 0.7 copy-start.4
  39.5 12.0 %collective-permute-start.2 = (bf16[4,96,256]{2,1,0:T(8,128)(2,1)}, bf16[4,96,256]{2,1,0:T(8,128)(2,1)S(1)}, u32[]{:S(2)}, u32[]{:S(2)}) collective-permute-start(bf16[4,96,256]{2,1,0:T(8,128)(2,1)} %get-tuple-element.34), channel_id=1, source_target_pairs={{0,3},{1,2},{2,1},{3,0},{4,7},{5,6},{6,5},{7,4},{8,11},{9,10},{10,... | collective-permute-start | bytes 589832 | tf_op jit(solution)/shard_map/ppermute | solution.py:326
  40.0 0.7 copy-start.6
  40.7 10.8 %collective-permute-start.14 = (bf16[4,192,128]{2,1,0:T(8,128)(2,1)}, bf16[4,192,128]{2,1,0:T(8,128)(2,1)}, u32[]{:S(2)}, u32[]{:S(2)}) collective-permute-start(bf16[4,192,128]{2,1,0:T(8,128)(2,1)} %get-tuple-element.50), channel_id=1, source_target_pairs={{0,1},{1,0},{2,3},{3,2},{4,5},{5,4},{6,7},{7,6},{8,9},{9,8},{10,11... | collective-permute-start | bytes 589832 | tf_op jit(solution)/shard_map/ppermute | solution.py:326
  41.8 0.7 copy-start.8
  42.5 20.0 %collective-permute-start.15 = (bf16[4,192,128]{2,1,0:T(8,128)(2,1)}, bf16[4,192,128]{2,1,0:T(8,128)(2,1)}, u32[]{:S(2)}, u32[]{:S(2)}) collective-permute-start(bf16[4,192,128]{2,1,0:T(8,128)(2,1)} %get-tuple-element.51), channel_id=1, source_target_pairs={{0,2},{1,3},{2,0},{3,1},{4,6},{5,7},{6,4},{7,5},{8,10},{9,11},{10,... | collective-permute-start | bytes 589832 | tf_op jit(solution)/shard_map/ppermute | solution.py:326
  44.8 32.1 %collective-permute-start.16 = (bf16[4,192,128]{2,1,0:T(8,128)(2,1)S(1)}, bf16[4,192,128]{2,1,0:T(8,128)(2,1)}, u32[]{:S(2)}, u32[]{:S(2)}) collective-permute-start(bf16[4,192,128]{2,1,0:T(8,128)(2,1)S(1)} %get-tuple-element.52), channel_id=1, source_target_pairs={{0,3},{1,2},{2,1},{3,0},{4,7},{5,6},{6,5},{7,4},{8,11},{9,10},{10,... | collective-permute-start | bytes 589832 | tf_op jit(solution)/shard_map/ppermute | solution.py:326
  46.2 47.9 %collective-permute-start.8 = (bf16[4,192,128]{2,1,0:T(8,128)(2,1)S(1)}, bf16[4,192,128]{2,1,0:T(8,128)(2,1)S(1)}, u32[]{:S(2)}, u32[]{:S(2)}) collective-permute-start(bf16[4,192,128]{2,1,0:T(8,128)(2,1)S(1)} %get-tuple-element.42), channel_id=1, source_target_pairs={{0,1},{1,0},{2,3},{3,2},{4,5},{5,4},{6,7},{7,6},{8,9},{9,8},{10,11... | collective-permute-start | bytes 589832 | tf_op jit(solution)/shard_map/ppermute | solution.py:326
  51.5 44.0 %collective-permute-start.9 = (bf16[4,192,128]{2,1,0:T(8,128)(2,1)S(1)}, bf16[4,192,128]{2,1,0:T(8,128)(2,1)S(1)}, u32[]{:S(2)}, u32[]{:S(2)}) collective-permute-start(bf16[4,192,128]{2,1,0:T(8,128)(2,1)S(1)} %get-tuple-element.43), channel_id=1, source_target_pairs={{0,2},{1,3},{2,0},{3,1},{4,6},{5,7},{6,4},{7,5},{8,10},{9,11},{10,... | collective-permute-start | bytes 589832 | tf_op jit(solution)/shard_map/ppermute | solution.py:326
  51.5 44.0 %collective-permute-start.10 = (bf16[4,192,128]{2,1,0:T(8,128)(2,1)S(1)}, bf16[4,192,128]{2,1,0:T(8,128)(2,1)S(1)}, u32[]{:S(2)}, u32[]{:S(2)}) collective-permute-start(bf16[4,192,128]{2,1,0:T(8,128)(2,1)S(1)} %get-tuple-element.44), channel_id=1, source_target_pairs={{0,3},{1,2},{2,1},{3,0},{4,7},{5,6},{6,5},{7,4},{8,11},{9,10},{10,... | collective-permute-start | bytes 589832 | tf_op jit(solution)/shard_map/ppermute | solution.py:326
  77.0 0.9 copy-start.5
  77.9 0.9 copy-start.7
  78.9 0.9 copy-start.9
  91.9 17.0 %collective-permute-start.17 = (bf16[2,4,192,128]{3,2,1,0:T(8,128)(2,1)S(1)}, bf16[2,4,192,128]{3,2,1,0:T(8,128)(2,1)S(1)}, u32[]{:S(2)}, u32[]{:S(2)}) collective-permute-start(bf16[2,4,192,128]{3,2,1,0:T(8,128)(2,1)S(1)} %get-tuple-element.54), channel_id=1, source_target_pairs={{0,1},{1,0},{2,3},{3,2},{4,5},{5,4},{6,7},{7,6},{8,9},{9,8},{10,11... | collective-permute-start | bytes 1179656 | tf_op jit(solution)/shard_map/ppermute | solution.py:326
  92.0 28.4 %collective-permute-start.18 = (bf16[2,4,192,128]{3,2,1,0:T(8,128)(2,1)S(1)}, bf16[2,4,192,128]{3,2,1,0:T(8,128)(2,1)S(1)}, u32[]{:S(2)}, u32[]{:S(2)}) collective-permute-start(bf16[2,4,192,128]{3,2,1,0:T(8,128)(2,1)S(1)} %get-tuple-element.55), channel_id=1, source_target_pairs={{0,2},{1,3},{2,0},{3,1},{4,6},{5,7},{6,4},{7,5},{8,10},{9,11},{10,... | collective-permute-start | bytes 1179656 | tf_op jit(solution)/shard_map/ppermute | solution.py:326
  94.2 53.5 %collective-permute-start.19 = (bf16[2,4,192,128]{3,2,1,0:T(8,128)(2,1)S(1)}, bf16[2,4,192,128]{3,2,1,0:T(8,128)(2,1)S(1)}, u32[]{:S(2)}, u32[]{:S(2)}) collective-permute-start(bf16[2,4,192,128]{3,2,1,0:T(8,128)(2,1)S(1)} %get-tuple-element.56), channel_id=1, source_target_pairs={{0,3},{1,2},{2,1},{3,0},{4,7},{5,6},{6,5},{7,4},{8,11},{9,10},{10,... | collective-permute-start | bytes 1179656 | tf_op jit(solution)/shard_map/ppermute | solution.py:326
  106.7 43.2 %collective-permute-start.11 = (bf16[2,4,192,128]{3,2,1,0:T(8,128)(2,1)S(1)}, bf16[2,4,192,128]{3,2,1,0:T(8,128)(2,1)S(1)}, u32[]{:S(2)}, u32[]{:S(2)}) collective-permute-start(bf16[2,4,192,128]{3,2,1,0:T(8,128)(2,1)S(1)} %get-tuple-element.46), channel_id=1, source_target_pairs={{0,1},{1,0},{2,3},{3,2},{4,5},{5,4},{6,7},{7,6},{8,9},{9,8},{10,11... | collective-permute-start | bytes 1179656 | tf_op jit(solution)/shard_map/ppermute | solution.py:326
  107.7 46.5 %collective-permute-start.12 = (bf16[2,4,192,128]{3,2,1,0:T(8,128)(2,1)S(1)}, bf16[2,4,192,128]{3,2,1,0:T(8,128)(2,1)S(1)}, u32[]{:S(2)}, u32[]{:S(2)}) collective-permute-start(bf16[2,4,192,128]{3,2,1,0:T(8,128)(2,1)S(1)} %get-tuple-element.47), channel_id=1, source_target_pairs={{0,2},{1,3},{2,0},{3,1},{4,6},{5,7},{6,4},{7,5},{8,10},{9,11},{10,... | collective-permute-start | bytes 1179656 | tf_op jit(solution)/shard_map/ppermute | solution.py:326
  108.9 54.6 %collective-permute-start.13 = (bf16[2,4,192,128]{3,2,1,0:T(8,128)(2,1)S(1)}, bf16[2,4,192,128]{3,2,1,0:T(8,128)(2,1)S(1)}, u32[]{:S(2)}, u32[]{:S(2)}) collective-permute-start(bf16[2,4,192,128]{3,2,1,0:T(8,128)(2,1)S(1)} %get-tuple-element.48), channel_id=1, source_target_pairs={{0,3},{1,2},{2,1},{3,0},{4,7},{5,6},{6,5},{7,4},{8,11},{9,10},{10,... | collective-permute-start | bytes 1179656 | tf_op jit(solution)/shard_map/ppermute | solution.py:326

commit v3 on v2

--- a/solution.py
+++ b/solution.py
@@ -16,6 +16,7 @@
 PAIR = 2 * K
 LANES = 128
 VMEM_LIMIT = 48 * 1024 * 1024
+SHORT = pl.CostEstimate(flops=1, bytes_accessed=1, transcendentals=0)
 
 THETA = np.arange(K).astype(np.float32) * np.float32(2.0 * math.pi / K)
 COS = np.cos(THETA)
@@ -27,8 +28,9 @@
     return (k < 6) | (k >= 18)
 
 
-def pack_kernel(raw, code, to_east, to_west):
+def pack_kernel(raw, sea, depth, to_east, to_west, code):
     step = pl.program_id(0)
+    code[...] = depth[...] + 16 * sea[...]
     for out, runs, low in ((to_east, ((0, 6), (18, 24)), 4), (to_west, ((6, 18),), 0)):
         at = step * (K // 2)
         for first, last in runs:
@@ -44,22 +46,24 @@
         out[out.shape[0] - 1] = code[...].astype(jnp.float32).astype(jnp.bfloat16)
 
 
-def pack_halo(spectrum, code):
+def pack_halo(spectrum, sea_mask, depth_class):
     comps, columns, rows = spectrum.shape
     half = jax.ShapeDtypeStruct((comps // 4 + 1, columns, rows), jnp.bfloat16)
     block = pl.BlockSpec(half.shape, lambda i: (0, 0, 0))
+    cells = pl.BlockSpec(sea_mask.shape, lambda i: (0, 0))
     return pl.pallas_call(
         pack_kernel,
         grid=(comps // PAIR,),
         in_specs=[
             pl.BlockSpec((PAIR, columns, rows), lambda i: (i, 0, 0)),
-            pl.BlockSpec(code.shape, lambda i: (0, 0)),
+            cells,
+            cells,
         ],
-        out_specs=[block, block],
-        out_shape=[half, half],
-        compiler_params=pltpu.CompilerParams(vmem_limit_bytes=VMEM_LIMIT),
+        out_specs=[block, block, cells],
+        out_shape=[half, half, jax.ShapeDtypeStruct(sea_mask.shape, jnp.int32)],
+        compiler_params=pltpu.CompilerParams(vmem_limit_bytes=60 * 1024 * 1024),
         name="pack_halo",
-    )(spectrum, code)
+    )(spectrum, sea_mask, depth_class)
 
 
 def propagate_kernel(with_halo, parts, skip, pos, *refs):
@@ -213,27 +217,159 @@
     )(z, *args)
 
 
-def sources_kernel(count, lane0, pos, *refs):
-    pieces = len(refs) - 2 * count - 8
-    first, refs = refs[:pieces], refs[pieces:]
-    second, (wind_c, wind_s, coupling, trig) = refs[:count], refs[count : count + 4]
-    outs, (state, rounded, nonlin, wind) = refs[count + 4 : 2 * count + 4], refs[2 * count + 4 :]
+def rank_kernel(sea, ranks, most, mask):
+    blocks, span = mask.shape
+    width = span // 4
+    for r in range(blocks):
+        d, g = r // 2, r % 2
+        for i in range(4):
+            x = 4 + i if g else 3 - i
+            mask[r : r + 1, i * width : (i + 1) * width] = sea[x : x + 1, d * width : (d + 1) * width].astype(jnp.float32)
+    lane = lax.broadcasted_iota(jnp.int32, mask.shape, 1)
+    count = mask[...]
+    shift = 1
+    while shift < span:
+        count += jnp.where(lane >= shift, pltpu.roll(count, shift, 1), 0.0)
+        shift *= 2
+    place = jnp.where(mask[...] > 0.0, count - 1.0, -1.0).astype(jnp.int32)
+    for r in range(blocks):
+        ranks[r // 2, r % 2] = place[r : r + 1]
+    top = jnp.max(jnp.max(count, axis=1, keepdims=True), axis=0, keepdims=True)
+    most[...] = jnp.broadcast_to(top, most.shape).astype(jnp.int32)
+
+
+def sea_ranks(sea_mask, count):
+    span = 4 * (sea_mask.shape[1] // count)
+    return pl.pallas_call(
+        rank_kernel,
+        out_shape=[
+            jax.ShapeDtypeStruct((count, 2, 1, span), jnp.int32),
+            jax.ShapeDtypeStruct((8, LANES), jnp.int32),
+        ],
+        scratch_shapes=[pltpu.VMEM((2 * count, span), jnp.float32)],
+        cost_estimate=SHORT,
+        name="sea_ranks",
+    )(sea_mask)
+
+
+def one_hot(rank, first, size):
+    row = first + lax.broadcasted_iota(jnp.int32, (size, rank.shape[1]), 0)
+    return jnp.where(row == rank, 1.0, 0.0).astype(jnp.bfloat16)
+
+
+def pack(values, hot):
+    return lax.dot_general(values, hot, (((1,), (1,)), ((), ())), preferred_element_type=jnp.float32)
+
+
+def pack_points_kernel(downwind, first_block, pos, piece, ranks, *outs):
+    comps = piece.shape[1]
+    blocks = sum(out.shape[0] for out in outs)
+    values = jnp.concatenate([piece[i if downwind else 3 - i] for i in range(4)], axis=1)
+    low, high = (
+        pack(values, one_hot(ranks[0, g], first_block * LANES, blocks * LANES)) for g in range(2)
+    )
+    if downwind:
+        low, high = high, low
+    packed = jnp.where(eastward_rows(0, comps), low, high).astype(jnp.bfloat16)
+    at = 0
+    for out in outs:
+        for j in range(out.shape[0]):
+            out[j] = packed[:, at * LANES : (at + 1) * LANES]
+            at += 1
+
+
+def pack_points(z, s, piece, ranks, downwind, first_block, sizes):
+    comps = piece.shape[1]
+    whole = lambda a: pl.BlockSpec(a.shape, lambda i, z: (0,) * a.ndim)
+    outs = [jax.ShapeDtypeStruct((n, comps, LANES), jnp.bfloat16) for n in sizes]
+    return pl.pallas_call(
+        functools.partial(pack_points_kernel, downwind, first_block),
+        grid_spec=pltpu.PrefetchScalarGridSpec(
+            num_scalar_prefetch=1,
+            grid=(1,),
+            in_specs=[
+                whole(piece),
+                pl.BlockSpec((1,) + ranks.shape[1:], lambda i, z: (jnp.bitwise_xor(z[0], s), 0, 0, 0)),
+            ],
+            out_specs=[whole(out) for out in outs],
+        ),
+        out_shape=outs,
+        compiler_params=pltpu.CompilerParams(vmem_limit_bytes=VMEM_LIMIT),
+        cost_estimate=SHORT,
+        name="pack_points",
+    )(z, piece, ranks)
+
+
+def pack_first_kernel(first_block, count, pos, *refs):
+    pieces, (ranks, wind_c, wind_s, packed, wind) = refs[:-5], refs[-5:]
+    z = pos[0]
+    blocks, total, _ = packed.shape
+    comps = total // count
+    hots = [one_hot(ranks[0, g], first_block * LANES, blocks * LANES) for g in range(2)]
+    mask = eastward_rows(0, comps)
+    for s in range(count):
+        at = pl.multiple_of(jnp.bitwise_xor(z, s) * comps, comps)
+        values = jnp.concatenate([pieces[s][i] for i in range(4)], axis=1)
+        low, high = (pack(values, hot) for hot in hots)
+        both = jnp.where(mask, high, low).astype(jnp.bfloat16)
+        for j in range(blocks):
+            packed[j, pl.ds(at, comps), :] = both[:, j * LANES : (j + 1) * LANES]
+    for g in range(2):
+        parts = []
+        for source in (wind_c, wind_s):
+            left = jnp.concatenate([source[4 + i if g else 3 - i] for i in range(4)], axis=1)
+            for _ in range(3):
+                part = left.astype(jnp.bfloat16).astype(jnp.float32)
+                parts.append(part)
+                left = left - part
+        parts += [jnp.zeros_like(left)] * 2
+        row = pack(jnp.concatenate(parts, axis=0).astype(jnp.bfloat16), hots[g])
+        for n in range(2):
+            wind[2 * g + n] = row[3 * n : 3 * n + 1] + row[3 * n + 1 : 3 * n + 2] + row[3 * n + 2 : 3 * n + 3]
+
+
+def pack_first(z, pieces, ranks, wind_c, wind_s, count, first_block, blocks):
+    total = sum(piece.shape[1] for piece in pieces)
+    whole = lambda a: pl.BlockSpec(a.shape, lambda i, z: (0,) * a.ndim)
+    outs = [
+        jax.ShapeDtypeStruct((blocks, total, LANES), jnp.bfloat16),
+        jax.ShapeDtypeStruct((4, 1, blocks * LANES), jnp.float32),
+    ]
+    return pl.pallas_call(
+        functools.partial(pack_first_kernel, first_block, count),
+        grid_spec=pltpu.PrefetchScalarGridSpec(
+            num_scalar_prefetch=1,
+            grid=(1,),
+            in_specs=[whole(piece) for piece in pieces]
+            + [pl.BlockSpec((1,) + ranks.shape[1:], lambda i, z: (z[0], 0, 0, 0)), whole(wind_c), whole(wind_s)],
+            out_specs=[whole(out) for out in outs],
+        ),
+        out_shape=outs,
+        compiler_params=pltpu.CompilerParams(vmem_limit_bytes=VMEM_LIMIT),
+        cost_estimate=SHORT,
+        name="pack_first",
+    )(z, *pieces, ranks, wind_c, wind_s)
+
+
+def sources_kernel(count, pos, *refs):
+    first, later, refs = refs[0], refs[1 : 1 + count], refs[1 + count :]
+    second, (winds, coupling, trig) = refs[:count], refs[count : count + 3]
+    outs, (state, rounded, nonlin, wind) = refs[count + 3 : 2 * count + 3], refs[2 * count + 3 :]
     comps, width = second[0].shape[1:]
-    whole = comps * count
     z = pos[0]
     mask = eastward_rows(0, comps)
     for s in range(count):
-        at = pl.multiple_of(jnp.bitwise_xor(z, s) * comps, comps)
-        down = jnp.concatenate([first[n][0, :, lane0 : lane0 + width] for n in range(s, pieces, count)], axis=0)
-        down = down.astype(jnp.float32)
+        source = jnp.bitwise_xor(z, s)
+        at = pl.ds(pl.multiple_of(source * comps, comps), comps)
+        part = comps - later[s].shape[1]
+        early = first[0, pl.ds(pl.multiple_of(source * part, part), part), :]
+        down = jnp.concatenate([early, later[s][0]], axis=0).astype(jnp.float32)
         up = second[s][0].astype(jnp.float32)
-        state[pl.ds(at, comps), 0:width] = jnp.where(mask, up, down)
-        state[pl.ds(at, comps), width : 2 * width] = jnp.where(mask, down, up)
-    pair = pl.program_id(0)
-    for n, x in enumerate((pair, 7 - pair)):
-        c = wind_c[x, :, lane0 : lane0 + width]
-        d = wind_s[x, :, lane0 : lane0 + width]
-        wind[:, n * width : (n + 1) * width] = jnp.maximum(trig[0, :, 0:1] * c + trig[1, :, 0:1] * d, 0.0)
+        state[at, 0:width] = jnp.where(mask, up, down)
+        state[at, width : 2 * width] = jnp.where(mask, down, up)
+    for g in range(2):
+        toward = trig[0, :, 0:1] * winds[2 * g] + trig[1, :, 0:1] * winds[2 * g + 1]
+        wind[:, g * width : (g + 1) * width] = jnp.maximum(toward, 0.0)
 
     for step in range(SRC_STEPS):
         total = jnp.zeros((8, 2 * width), jnp.float32)
@@ -252,79 +388,119 @@
             state[at, :] = jnp.maximum(gain * here + 0.125 * nonlin[at, :], 0.0)
 
     for s in range(count):
-        at = pl.multiple_of(jnp.bitwise_xor(z, s) * comps, comps)
-        for n in range(2):
-            outs[s][n, 0] = state[pl.ds(at, comps), n * width : (n + 1) * width].astype(jnp.bfloat16)
-
-
-def sources(z, first, second, wind_c, wind_s, coupling, trig, lane0):
+        at = pl.ds(pl.multiple_of(jnp.bitwise_xor(z, s) * comps, comps), comps)
+        for g in range(2):
+            outs[s][g, 0] = state[at, g * width : (g + 1) * width].astype(jnp.bfloat16)
+
+
+def sources(z, first, later, second, winds, coupling, trig, first_block):
     count = len(second)
-    comps, width = second[0].shape[1], second[0].shape[2]
+    blocks, comps, width = second[0].shape
+    total = comps * count
     whole = lambda a: pl.BlockSpec(a.shape, lambda i, z: (0,) * a.ndim)
     return pl.pallas_call(
-        functools.partial(sources_kernel, count, lane0),
+        functools.partial(sources_kernel, count),
         grid_spec=pltpu.PrefetchScalarGridSpec(
             num_scalar_prefetch=1,
-            grid=(4,),
-            in_specs=[pl.BlockSpec((1,) + a.shape[1:], lambda i, z: (3 - i, 0, 0)) for a in first]
-            + [pl.BlockSpec((1,) + a.shape[1:], lambda i, z: (i, 0, 0)) for a in second]
-            + [whole(wind_c), whole(wind_s), whole(coupling), whole(trig)],
+            grid=(blocks,),
+            in_specs=[pl.BlockSpec((1,) + a.shape[1:], lambda i, z: (first_block + i, 0, 0)) for a in [first, *later]]
+            + [pl.BlockSpec((1, comps, width), lambda i, z: (i, 0, 0)) for a in second]
+            + [pl.BlockSpec((4, 1, width), lambda i, z: (0, 0, first_block + i)), whole(coupling), whole(trig)],
             out_specs=[pl.BlockSpec((2, 1, comps, width), lambda i, z: (0, i, 0, 0))] * count,
             scratch_shapes=[
-                pltpu.VMEM((comps * count, 2 * width), jnp.float32),
-                pltpu.VMEM((comps * count, 2 * width), jnp.bfloat16),
-                pltpu.VMEM((comps * count, 2 * width), jnp.float32),
+                pltpu.VMEM((total, 2 * width), jnp.float32),
+                pltpu.VMEM((total, 2 * width), jnp.bfloat16),
+                pltpu.VMEM((total, 2 * width), jnp.float32),
                 pltpu.VMEM((K, 2 * width), jnp.float32),
             ],
         ),
-        out_shape=[jax.ShapeDtypeStruct((2, 4, comps, width), jnp.bfloat16)] * count,
+        out_shape=[jax.ShapeDtypeStruct((2, blocks, comps, width), jnp.bfloat16)] * count,
         compiler_params=pltpu.CompilerParams(vmem_limit_bytes=VMEM_LIMIT),
         cost_estimate=pl.CostEstimate(
-            flops=SRC_STEPS * 2 * (comps * count) ** 2 * 8 * width, bytes_accessed=4 * comps * count * 8 * width, transcendentals=0
+            flops=SRC_STEPS * 2 * total**2 * 2 * blocks * width, bytes_accessed=8 * total * blocks * width, transcendentals=0
         ),
         name="source_terms",
-    )(z, *first, *second, wind_c, wind_s, coupling, trig)
-
-
-def assemble_kernel(count, pos, *refs):
-    blocks, out, turned = refs[:count], refs[-2], refs[-1]
-    for s in range(count):
-
-        @pl.when(pl.program_id(0) == s)
+    )(z, first, *later, *second, winds, coupling, trig)
+
+
+def unpack_kernel(partners, first_block, rest_block, scalars, *refs):
+    n = len(partners)
+    blocks, refs = refs[:n], refs[n:]
+    rest = refs[:n] if rest_block else ()
+    ranks, (out, turned) = refs[len(rest)], refs[-2:]
+    comps, _, width = out.shape
+    tiles = width // LANES
+
+    def spread(part, first, add):
+        for g in range(2):
+            values = jnp.concatenate([part[g, j] for j in range(part.shape[1])], axis=1)
+            hot = one_hot(ranks[0, g], first * LANES, values.shape[1])
+            wide = jnp.dot(values, hot, preferred_element_type=jnp.float32)
+            for i in range(4):
+                x = 4 + i if g else 3 - i
+                for t in range(tiles):
+                    at = i * width + t * LANES
+                    here = wide[:, at : at + LANES]
+                    if add:
+                        here += turned[t, pl.ds(x, comps, stride=8), :]
+                    turned[t, pl.ds(x, comps, stride=8), :] = here
+
+    for i in range(n):
+
+        @pl.when(pl.program_id(0) == i)
         def _():
-            comps = blocks[s].shape[2]
-            for n in range(2):
-                for i in range(4):
-                    x = i if n == 0 else 7 - i
-                    turned[pl.ds(x, comps, stride=8), :] = blocks[s][n, i].astype(jnp.float32)
-            out[...] = turned[...].reshape(out.shape).astype(jnp.bfloat16)
-
-
-def assemble(z, blocks, rows, chunk, chunks, into):
-    count = len(blocks)
-    comps, width = blocks[0].shape[2], blocks[0].shape[3]
+            spread(blocks[i], first_block, False)
+            if rest:
+
+                @pl.when(scalars[1] > 0)
+                def _():
+                    spread(rest[i], rest_block, True)
+
+    for t in range(tiles):
+        here = turned[t].reshape(comps, 8, LANES)
+        if len(refs) > len(rest) + 3:
+            here += refs[len(rest) + 1][:, :, t * LANES : (t + 1) * LANES].astype(jnp.float32)
+        out[:, :, t * LANES : (t + 1) * LANES] = here.astype(jnp.bfloat16)
+
+
+def unpack(scalars, partners, blocks, first_block, rest, rest_block, ranks, rows, into):
+    comps = blocks[0].shape[2]
+    width = ranks.shape[3] // 4
+    whole = lambda a: pl.BlockSpec(a.shape, lambda i, z: (0,) * a.ndim)
+    first = partners[0]
+    device = lambda i, z: jnp.bitwise_xor(z[0], first + i)
+    place = pl.BlockSpec((comps, 8, width), lambda i, z: (0, 0, device(i, z)))
     extra = [] if into is None else [into]
-    return pl.pallas_call(
-        functools.partial(assemble_kernel, count),
+    inputs = [*blocks, *rest]
+    return pl.pallas_call(
+        functools.partial(unpack_kernel, partners, first_block, rest_block),
         grid_spec=pltpu.PrefetchScalarGridSpec(
             num_scalar_prefetch=1,
-            grid=(count,),
-            in_specs=[pl.BlockSpec(b.shape, lambda i, z: (0, 0, 0, 0)) for b in blocks]
-            + [pl.BlockSpec(memory_space=pl.ANY)] * len(extra),
-            out_specs=pl.BlockSpec((comps, 8, width), lambda i, z: (0, 0, jnp.bitwise_xor(z[0], i) * chunks + chunk)),
-            scratch_shapes=[pltpu.VMEM((comps * 8, width), jnp.float32)],
+            grid=(len(partners),),
+            in_specs=[whole(part) for part in inputs]
+            + [pl.BlockSpec((1,) + ranks.shape[1:], lambda i, z: (device(i, z), 0, 0, 0))]
+            + [place] * len(extra),
+            out_specs=place,
+            scratch_shapes=[pltpu.VMEM((width // LANES, comps * 8, LANES), jnp.float32)],
         ),
         out_shape=jax.ShapeDtypeStruct((comps, 8, rows), jnp.bfloat16),
-        input_output_aliases={count + 1: 0} if extra else {},
+        input_output_aliases={len(inputs) + 2: 0} if extra else {},
         compiler_params=pltpu.CompilerParams(vmem_limit_bytes=VMEM_LIMIT),
-        name="assemble",
-    )(z, *blocks, *extra)
+        cost_estimate=SHORT,
+        name="unpack",
+    )(scalars, *inputs, ranks, *extra)
 
 
 def exchange(blocks, axis):
     count = len(blocks)
     came = {s: lax.ppermute(blocks[s], axis, [(i, i ^ s) for i in range(count)]) for s in range(count - 1, 0, -1)}
     return [blocks[0]] + [came[s] for s in range(1, count)]
+
+
+def exchange_rare(blocks, axis):
+    order = jnp.bitwise_xor(lax.axis_index(axis), jnp.arange(len(blocks)))
+    came = lax.all_to_all(jnp.stack(blocks)[order], axis, split_axis=0, concat_axis=0, tiled=True)[order]
+    return [came[s] for s in range(len(blocks))]
 
 
 def on_device(spectrum, sea_mask, depth_class, group_speed, wind_speed, wind_dir, coupling):
@@ -334,11 +510,9 @@
     place = lax.axis_index("comp")
     z = place.astype(jnp.int32).reshape(1)
     width = rows // count
-    chunks = max(1, width // LANES)
     east = [(i, (i + 1) % tiles) for i in range(tiles)]
     west = [(j, i) for i, j in east]
 
-    code = depth_class + 16 * sea_mask
     freqs = comps // K
     table = lax.dynamic_slice_in_dim(group_speed, place * freqs, freqs, 1).T
     table = jnp.pad(table, ((0, 0), (0, LANES - table.shape[1])))[:, None]
@@ -349,21 +523,51 @@
     dir_part = lax.dynamic_slice_in_dim(wind_dir, start, width, 1)
     wind_c, wind_s = (speed_part * jnp.cos(dir_part))[:, None], (speed_part * jnp.sin(dir_part))[:, None]
 
-    to_east, to_west = pack_halo(spectrum, code)
+    to_east, to_west, code = pack_halo(spectrum, sea_mask, depth_class)
     halo = lax.ppermute(to_east, "tile", east), lax.ppermute(to_west, "tile", west)
     pairs = comps // PAIR
+    half = pairs // 2
+    blocks = 4 * width // LANES
+    main = blocks * 3 // 4
+    chunks = 2 if main % 2 == 0 else 1
+    size = main // chunks
     parts = [(s, 0, width) for s in range(count)]
-    first = []
-    for skip in range(0, pairs, pairs // 2):
-        first += exchange(propagate(z, spectrum, code, table, trig, parts, skip, pairs // 2), "comp")
-    size = width // chunks
-    parts = [(s, c * size, size) for c in range(chunks) for s in range(count)]
+    first = exchange(propagate(z, spectrum, code, table, trig, parts, 0, half), "comp")
+    later = propagate(z, spectrum, code, table, trig, parts, half, pairs - half)
+    ranks, most = sea_ranks(sea_mask, count)
+    packed_later = [pack_points(z, s, later[s], ranks, True, 0, [main])[0] for s in range(count)]
+    packed_later = exchange(packed_later, "comp")
     second = propagate(z, spectrum, code, table, trig, parts, 0, pairs, halo)
-    out = None
+    packed = [pack_points(z, s, second[s], ranks, False, 0, [size] * chunks) for s in range(count)]
+    packed_first, winds = pack_first(z, first, ranks, wind_c, wind_s, count, 0, main)
+
+    def remainder(first, later, second, ranks, wind_c, wind_s, coupling):
+        rest = blocks - main
+        down, winds = pack_first(z, first, ranks, wind_c, wind_s, count, main, rest)
+        low = [pack_points(z, s, later[s], ranks, True, main, [rest])[0] for s in range(count)]
+        high = [pack_points(z, s, second[s], ranks, False, main, [rest])[0] for s in range(count)]
+        low, high = exchange_rare(low, "comp"), exchange_rare(high, "comp")
+        return exchange_rare(sources(z, down, low, high, winds, coupling, signed, 0), "comp")
+
+    def nothing(*args):
+        return [jnp.zeros((2, blocks - main, comps, LANES), jnp.bfloat16)] * count
+
+    updated = []
     for c in range(chunks):
-        arrived = exchange(second[c * count : (c + 1) * count], "comp")
-        updated = sources(z, first, arrived, wind_c, wind_s, coupling, signed, c * size)
-        out = assemble(z, exchange(updated, "comp"), rows, c, chunks, out)
+        arrived = exchange([packed[s][c] for s in range(count)], "comp")
+        sent = sources(z, packed_first, packed_later, arrived, winds, coupling, signed, c * size)
+        updated.append(exchange(sent, "comp"))
+        if c == 0:
+            most, _ = lax.optimization_barrier((most, arrived[0]))
+            full = lax.pmax(most[0, 0], "tile") > main * LANES
+    full, _ = lax.optimization_barrier((full, sent[0]))
+    rest = lax.cond(full, remainder, nothing, first, later, second, ranks, wind_c, wind_s, coupling)
+    scalars = jnp.concatenate([z, full.astype(jnp.int32).reshape(1)])
+    everyone = list(range(count))
+    out = unpack(scalars, everyone, updated[0], 0, rest, main, ranks, rows, None)
+    for partners in (everyone[: count // 2], everyone[count // 2 :]):
+        for c in range(1, chunks):
+            out = unpack(scalars, partners, [updated[c][s] for s in partners], c * size, [], 0, ranks, rows, out)
     return out
 
 

time: 166 us -> 134 us (0.81)
  waiting for transfers between devices: 79.8 us -> 10.2 us
  Pallas kernels: 51.3 us -> 77.6 us
  blocking collectives: 0 us -> 8.01 us
  starting transfers between devices: 25.3 us -> 28 us
    ppermute x18, waiting for transfers between devices: 77.3 us -> 10.2 us  [exchange(): lax.ppermute(blocks[s], axis, [(i, i ^ s) for i in range(count)])]
    pallas_call x4 -> x15, Pallas kernels: 27.8 us -> 51.9 us  [the longest x2 19.6 us: sources(): pl.pallas_call(functools.partial(sources_kernel, count), grid_spec=pltpu....]
    pmax x0 -> x1, blocking collectives: none -> 8.01 us  [on_device(): full = lax.pmax(most[0, 0], 'tile') > main * LANES]
    unnamed x29 -> x37, local copies, waits for them, and re-layouts: 7.48 us -> 3.02 us
    another operation x0 -> x4, local copies, waits for them, and re-layouts: none -> 2.82 us
    ppermute x18, starting transfers between devices: 22.6 us -> 25.4 us  [exchange(): lax.ppermute(blocks[s], axis, [(i, i ^ s) for i in range(count)])]
    pallas_call x1, Pallas kernels: 1.67 us -> 4.2 us  [pack_halo(): pl.pallas_call(pack_kernel, grid=(comps // PAIR,), in_specs=[pl.BlockSpec...]
    ppermute x1, waiting for transfers between devices: 2.46 us -> 0.01 us  [on_device(): lax.ppermute(to_east, 'tile', east)]
  transfers between devices with their start and end apart: 20 -> 20, of which waited for: 8 -> 1; matrix products, arithmetic and copies ran while one was open for 1% -> 4% of each run, Pallas kernels for 29% -> 52%
where the time goes in v3:
time: 134 us; the launch traced here: 133 us
  Pallas kernels  77.6 us (58%)
  starting transfers between devices  28 us (21%)
  waiting for transfers between devices  10.2 us (8%)
  blocking collectives  8.01 us (6%)
  local copies, waits for them, and re-layouts  7.27 us (5%)
    ppermute x18, starting transfers between devices, exchange(): lax.ppermute(blocks[s], axis, [(i, i ^ s) for i in range(count)])  25.4 us
    pallas_call x3, Pallas kernels, propagate(): pl.pallas_call(functools.partial(propagate_kernel, halo is not None, part...  21.5 us
    pallas_call x2, Pallas kernels, sources(): pl.pallas_call(functools.partial(sources_kernel, count), grid_spec=pltpu....  19.6 us
    pallas_call x3, Pallas kernels, unpack(): pl.pallas_call(functools.partial(unpack_kernel, partners, first_block, re...  14.2 us
    ppermute x18, waiting for transfers between devices, exchange(): lax.ppermute(blocks[s], axis, [(i, i ^ s) for i in range(count)])  10.2 us
    pallas_call x8, Pallas kernels, pack_points(): pl.pallas_call(functools.partial(pack_points_kernel, downwind, first_bloc...  10.2 us
    pmax x1, blocking collectives, on_device(): full = lax.pmax(most[0, 0], 'tile') > main * LANES  8.01 us
    pallas_call x1, Pallas kernels, pack_first(): pl.pallas_call(functools.partial(pack_first_kernel, first_block, count),...  5.95 us
  transfers between devices with their start and end apart: 20, of which 1 were waited for; matrix products, arithmetic and copies ran while one was open for 4% of the time, Pallas kernels for 52%

profile of v3, /device:TPU:8, one launch (start us, length us, event | category | flops | bytes accessed | tf_op | source)
XLA Modules:
  0.0 132.9 jit_solution(17193311315311549039)
XLA Ops:
  0.0 4.2 %pack_halo.1 = (bf16[49,8,1024]{2,1,0:T(8,128)(2,1)}, bf16[49,8,1024]{2,1,0:T(8,128)(2,1)}, s32[8,1024]{1,0:T(8,128)}) custom-call(bf16[192,8,1024]{2,1,0:T(8,128)(2,1)} %refs_0_.5, s32[8,1024]{1,0:T(8,128)} %sea.3, s32[8,1024]{1,0:T(8,128)} %depth.1), custom_call_target="tpu_custom_call" | custom-call | tf_op jit(solution)/shard_map/pack_halo/pallas_call | solution.py:54
  4.2 0.0 collective-permute-start
  4.2 2.6 %collective-permute-start.1 = (bf16[49,8,1024]{2,1,0:T(8,128)(2,1)}, bf16[49,8,1024]{2,1,0:T(8,128)(2,1)}, u32[]{:S(2)}, u32[]{:S(2)}) collective-permute-start(bf16[49,8,1024]{2,1,0:T(8,128)(2,1)} %get-tuple-element.108), channel_id=1, source_target_pairs={{4,0},{8,4},{12,8},{16,12},{20,16},{24,20},{28,24},{0,28},{5,1},{9... | collective-permute-start | bytes 2408456 | tf_op jit(solution)/shard_map/ppermute | solution.py:527
  6.9 0.1 constant_dynamic-slice_fusion
  6.9 0.1 copy.15
  7.0 0.1 broadcast_in_dim.11.refs_7_.refs_3_
  7.1 0.8 copy-done.2
  7.9 5.4 %propagate_downwind.2 = (bf16[4,96,256]{2,1,0:T(8,128)(2,1)}, bf16[4,96,256]{2,1,0:T(8,128)(2,1)}, bf16[4,96,256]{2,1,0:T(8,128)(2,1)}, bf16[4,96,256]{2,1,0:T(8,128)(2,1)}) custom-call(s32[1]{0:T(128)} %bitcast.25.pos, bf16[192,8,1024]{2,1,0:T(8,128)(2,1)S(1)} %copy-done.1, s32[8,1024]{1,0:T(8,128)S(1)} %copy-done.2, f32[8,1,128]{2,1,0:T(1,128)S(1)} %bitcast.57, ...), custom_call_target="tpu_custom_call" | custom-call | flops 23592960 | bytes 4718592 | tf_op jit(solution)/shard_map/propagate_downwind/pallas_call | solution.py:200
  13.2 0.0 collective-permute-start.2
  13.2 3.0 %collective-permute-start.3 = (bf16[4,96,256]{2,1,0:T(8,128)(2,1)}, bf16[4,96,256]{2,1,0:T(8,128)(2,1)}, u32[]{:S(2)}, u32[]{:S(2)}) collective-permute-start(bf16[4,96,256]{2,1,0:T(8,128)(2,1)} %get-tuple-element.116), channel_id=1, source_target_pairs={{0,2},{1,3},{2,0},{3,1},{4,6},{5,7},{6,4},{7,5},{8,10},{9,11},{10,... | collective-permute-start | bytes 589832 | tf_op jit(solution)/shard_map/ppermute | solution.py:496
  16.3 0.5 collective-permute-start.4
  16.7 2.0 %sea_ranks.1 = (s32[4,2,1,1024]{3,2,1,0:T(1,128)S(1)}, s32[8,128]{1,0:T(8,128)}) custom-call(s32[8,1024]{1,0:T(8,128)} %sea.3), custom_call_target="tpu_custom_call" | custom-call | flops 1 | bytes 1 | tf_op jit(solution)/shard_map/sea_ranks/pallas_call | solution.py:243
  18.7 4.6 %propagate_downwind.3 = (bf16[4,96,256]{2,1,0:T(8,128)(2,1)S(1)}, bf16[4,96,256]{2,1,0:T(8,128)(2,1)S(1)}, bf16[4,96,256]{2,1,0:T(8,128)(2,1)S(1)}, bf16[4,96,256]{2,1,0:T(8,128)(2,1)S(1)}) custom-call(s32[1]{0:T(128)} %bitcast.25.pos, bf16[192,8,1024]{2,1,0:T(8,128)(2,1)S(1)} %copy-done.1, s32[8,1024]{1,0:T(8,128)S(1)} %copy-done.3, ...), custom_call_target="tpu_custom_call" | custom-call | flops 23592960 | bytes 4718592 | tf_op jit(solution)/shard_map/propagate_downwind/pallas_call | solution.py:200
  23.3 1.1 pack_points.28
  24.4 0.0 collective-permute-done.refs_1_.refs_4_
  24.5 1.6 %collective-permute-start.7 = (bf16[6,96,128]{2,1,0:T(8,128)(2,1)S(1)}, bf16[6,96,128]{2,1,0:T(8,128)(2,1)S(1)}, u32[]{:S(2)}, u32[]{:S(2)}) collective-permute-start(bf16[6,96,128]{2,1,0:T(8,128)(2,1)S(1)} %pack_points.28), channel_id=1, source_target_pairs={{0,3},{1,2},{2,1},{3,0},{4,7},{5,6},{6,5},{7,4},{8,11},{9,10},{10,... | collective-permute-start | bytes 442376 | tf_op jit(solution)/shard_map/ppermute | solution.py:496
  26.1 1.1 pack_points.26
  27.2 1.1 pack_points.27
  28.3 0.0 copy-start.19
  28.3 2.0 %collective-permute-start.6 = (bf16[6,96,128]{2,1,0:T(8,128)(2,1)S(1)}, bf16[6,96,128]{2,1,0:T(8,128)(2,1)}, u32[]{:S(2)}, u32[]{:S(2)}) collective-permute-start(bf16[6,96,128]{2,1,0:T(8,128)(2,1)S(1)} %pack_points.27), channel_id=1, source_target_pairs={{0,2},{1,3},{2,0},{3,1},{4,6},{5,7},{6,4},{7,5},{8,10},{9,11},{10,... | collective-permute-start | bytes 442376 | tf_op jit(solution)/shard_map/ppermute | solution.py:496
  30.3 11.6 %propagate_upwind.1 = (bf16[4,192,256]{2,1,0:T(8,128)(2,1)}, bf16[4,192,256]{2,1,0:T(8,128)(2,1)S(1)}, bf16[4,192,256]{2,1,0:T(8,128)(2,1)S(1)}, bf16[4,192,256]{2,1,0:T(8,128)(2,1)S(1)}) custom-call(s32[1]{0:T(128)} %bitcast.25.pos, bf16[192,8,1024]{2,1,0:T(8,128)(2,1)S(1)} %copy-done.1, bf16[49,8,1024]{2,1,0:T(8,128)(2,1)} %collective-permute-done.refs_1_.refs_4_, ...), custom_call_target="tpu_custom_call" | custom-call | flops 47185920 | bytes 9437184 | tf_op jit(solution)/shard_map/propagate_upwind/pallas_call | solution.py:200
  41.9 1.2 pack_points.29
  43.1 1.2 pack_points.30
  44.3 1.2 pack_points.31
  45.5 0.0 collective-permute-done.7.refs_4_
  45.5 0.0 copy-start.6
  45.5 0.7 copy-done.6
  46.2 1.5 %collective-permute-start.5 = (bf16[6,96,128]{2,1,0:T(8,128)(2,1)S(1)}, bf16[6,96,128]{2,1,0:T(8,128)(2,1)S(1)}, u32[]{:S(2)}, u32[]{:S(2)}) collective-permute-start(bf16[6,96,128]{2,1,0:T(8,128)(2,1)S(1)} %pack_points.26), channel_id=1, source_target_pairs={{0,1},{1,0},{2,3},{3,2},{4,5},{5,4},{6,7},{7,6},{8,9},{9,8},{10,11... | collective-permute-start | bytes 442376 | tf_op jit(solution)/shard_map/ppermute | solution.py:496
  47.7 0.6 collective-permute-start.14
  48.2 0.0 collective-permute-done.3.refs_2_
  48.2 2.4 %collective-permute-start.15 = (bf16[3,192,128]{2,1,0:T(8,128)(2,1)S(1)}, bf16[3,192,128]{2,1,0:T(8,128)(2,1)S(1)}, u32[]{:S(2)}, u32[]{:S(2)}) collective-permute-start(bf16[3,192,128]{2,1,0:T(8,128)(2,1)S(1)} %get-tuple-element.137), channel_id=1, source_target_pairs={{0,2},{1,3},{2,0},{3,1},{4,6},{5,7},{6,4},{7,5},{8,10},{9,11},{10,... | collective-permute-start | bytes 442376 | tf_op jit(solution)/shard_map/ppermute | solution.py:496
  50.7 0.6 collective-permute-start.16
  51.2 1.1 pack_points.25.refs_1_
  52.3 0.8 sine_multiply_fusion
  53.1 0.6 copy-done.16
  53.7 6.0 %pack_first.3 = (bf16[6,384,128]{2,1,0:T(8,128)(2,1)S(1)}, f32[4,1,768]{2,1,0:T(1,128)S(1)}) custom-call(s32[1]{0:T(128)} %bitcast.25.pos, bf16[4,96,256]{2,1,0:T(8,128)(2,1)} %get-tuple-element.114.refs_0_, bf16[4,96,256]{2,1,0:T(8,128)(2,1)} %collective-permute-done.2.refs_1_, bf16[4,96,256]{2,1,0:T(8,128)(2,1)} %collective-permute-done.3.refs_2_, ...), custom_call_target="tpu_custom_call" | custom-call | flops 1 | bytes 1 | tf_op jit(solution)/shard_map/pack_first/pallas_call | solution.py:338
  59.7 2.2 %pack_points.24 = (bf16[3,192,128]{2,1,0:T(8,128)(2,1)S(1)}, bf16[3,192,128]{2,1,0:T(8,128)(2,1)S(1)}) custom-call(s32[1]{0:T(128)} %bitcast.25.pos, bf16[4,192,256]{2,1,0:T(8,128)(2,1)} %get-tuple-element.110.piece, s32[4,2,1,1024]{3,2,1,0:T(1,128)S(1)} %get-tuple-element.111.ranks.refs_4_.refs_8_.refs_2_), custom_call_target="tpu_custom_call" | custom-call | flops 1 | bytes 1 | tf_op jit(solution)/shard_map/pack_points/pallas_call | solution.py:285
  61.9 0.0 collective-permute-done.6.refs_3_
  61.9 1.5 %collective-permute-start.8 = (bf16[3,192,128]{2,1,0:T(8,128)(2,1)S(1)}, bf16[3,192,128]{2,1,0:T(8,128)(2,1)S(1)}, u32[]{:S(2)}, u32[]{:S(2)}) collective-permute-start(bf16[3,192,128]{2,1,0:T(8,128)(2,1)S(1)} %get-tuple-element.125), channel_id=1, source_target_pairs={{0,1},{1,0},{2,3},{3,2},{4,5},{5,4},{6,7},{7,6},{8,9},{9,8},{10,11... | collective-permute-start | bytes 442376 | tf_op jit(solution)/shard_map/ppermute | solution.py:496
  63.4 0.0 collective-permute-done.5.refs_2_
  63.4 2.4 %collective-permute-start.9 = (bf16[3,192,128]{2,1,0:T(8,128)(2,1)S(1)}, bf16[3,192,128]{2,1,0:T(8,128)(2,1)S(1)}, u32[]{:S(2)}, u32[]{:S(2)}) collective-permute-start(bf16[3,192,128]{2,1,0:T(8,128)(2,1)S(1)} %get-tuple-element.127), channel_id=1, source_target_pairs={{0,2},{1,3},{2,0},{3,1},{4,6},{5,7},{6,4},{7,5},{8,10},{9,11},{10,... | collective-permute-start | bytes 442376 | tf_op jit(solution)/shard_map/ppermute | solution.py:496
  65.8 0.0 collective-permute-done.14.refs_6_
  65.8 0.5 collective-permute-start.10
  66.4 0.1 broadcast_in_dim.14.refs_11_
  66.4 0.9 copy-done.7
  67.3 9.7 %source_terms.5 = (bf16[2,3,192,128]{3,2,1,0:T(8,128)(2,1)S(1)}, bf16[2,3,192,128]{3,2,1,0:T(8,128)(2,1)S(1)}, bf16[2,3,192,128]{3,2,1,0:T(8,128)(2,1)S(1)}, bf16[2,3,192,128]{3,2,1,0:T(8,128)(2,1)S(1)}) custom-call(s32[1]{0:T(128)} %bitcast.25.pos, bf16[6,384,128]{2,1,0:T(8,128)(2,1)S(1)} %get-tuple-element.118.refs_0_, ...), custom_call_target="tpu_custom_call" | custom-call | flops 3623878656 | bytes 2359296 | tf_op jit(solution)/shard_map/source_terms/pallas_call | solution.py:401
  77.1 1.5 %collective-permute-start.17 = (bf16[2,3,192,128]{3,2,1,0:T(8,128)(2,1)S(1)}, bf16[2,3,192,128]{3,2,1,0:T(8,128)(2,1)S(1)}, u32[]{:S(2)}, u32[]{:S(2)}) collective-permute-start(bf16[2,3,192,128]{3,2,1,0:T(8,128)(2,1)S(1)} %get-tuple-element.140), channel_id=1, source_target_pairs={{0,1},{1,0},{2,3},{3,2},{4,5},{5,4},{6,7},{7,6},{8,9},{9,8},{10,11... | collective-permute-start | bytes 884744 | tf_op jit(solution)/shard_map/ppermute | solution.py:496
  78.5 2.4 %collective-permute-start.18 = (bf16[2,3,192,128]{3,2,1,0:T(8,128)(2,1)S(1)}, bf16[2,3,192,128]{3,2,1,0:T(8,128)(2,1)S(1)}, u32[]{:S(2)}, u32[]{:S(2)}) collective-permute-start(bf16[2,3,192,128]{3,2,1,0:T(8,128)(2,1)S(1)} %get-tuple-element.141), channel_id=1, source_target_pairs={{0,2},{1,3},{2,0},{3,1},{4,6},{5,7},{6,4},{7,5},{8,10},{9,11},{10,... | collective-permute-start | bytes 884744 | tf_op jit(solution)/shard_map/ppermute | solution.py:496
  81.0 0.5 collective-permute-start.19
  81.5 9.9 %source_terms.4 = (bf16[2,3,192,128]{3,2,1,0:T(8,128)(2,1)S(1)}, bf16[2,3,192,128]{3,2,1,0:T(8,128)(2,1)}, bf16[2,3,192,128]{3,2,1,0:T(8,128)(2,1)}, bf16[2,3,192,128]{3,2,1,0:T(8,128)(2,1)S(1)}) custom-call(s32[1]{0:T(128)} %bitcast.25.pos, bf16[6,384,128]{2,1,0:T(8,128)(2,1)S(1)} %get-tuple-element.118.refs_0_, ...), custom_call_target="tpu_custom_call" | custom-call | flops 3623878656 | bytes 2359296 | tf_op jit(solution)/shard_map/source_terms/pallas_call | solution.py:401
  91.4 3.8 %collective-permute-start.11 = (bf16[2,3,192,128]{3,2,1,0:T(8,128)(2,1)}, bf16[2,3,192,128]{3,2,1,0:T(8,128)(2,1)S(1)}, u32[]{:S(2)}, u32[]{:S(2)}) collective-permute-start(bf16[2,3,192,128]{3,2,1,0:T(8,128)(2,1)} %get-tuple-element.133), channel_id=1, source_target_pairs={{0,2},{1,3},{2,0},{3,1},{4,6},{5,7},{6,4},{7,5},{8,10},{9,11},{10,... | collective-permute-start | bytes 884744 | tf_op jit(solution)/shard_map/ppermute | solution.py:496
  95.2 0.6 collective-permute-start.12
  95.8 1.2 slice.39
  97.0 8.0 %pmax.7 = s32[]{:T(128)} all-reduce(s32[]{:T(128)} %bitcast.28), channel_id=1, replica_groups=mesh['tile'=8,'comp'=4] {'tile'}, use_global_device_ids=true, to_apply=%region_0.1 | all-reduce | flops 1 | bytes 8 | tf_op jit(solution)/shard_map/pmax | solution.py:562
  105.7 2.8 %conditional.1 = (bf16[2,2,192,128]{3,2,1,0:T(8,128)(2,1)}, bf16[2,2,192,128]{3,2,1,0:T(8,128)(2,1)}, bf16[2,2,192,128]{3,2,1,0:T(8,128)(2,1)}, bf16[2,2,192,128]{3,2,1,0:T(8,128)(2,1)}) conditional(s32[]{:T(128)} %convert_element_type.6, () %tuple.17, (s32[1]{0:T(128)}, bf16[4,96,256]{2,1,0:T(8,128)(2,1)}, bf16[4,96,256]{2,1,0:T(8,128)(2,1)}, ...), branch_computations={%region_1.2_spmd, %region_2.3_spmd} | conditional | flops 2417984512 | bytes 17715568 | solution.py:564
  105.7 0.7 broadcast.29.clone.2
  106.4 0.7 broadcast.29.clone.1
  107.1 0.7 broadcast.29.clone
  107.8 0.7 broadcast.29
  108.5 0.1 pad_add_fusion.scalars
  108.6 10.2 %collective-permute-done.19.refs_3_ = bf16[2,3,192,128]{3,2,1,0:T(8,128)(2,1)S(1)} collective-permute-done((bf16[2,3,192,128]{3,2,1,0:T(8,128)(2,1)S(1)}, bf16[2,3,192,128]{3,2,1,0:T(8,128)(2,1)S(1)}, u32[]{:S(2)}, u32[]{:S(2)}) %collective-permute-start.19) | collective-permute-done | bytes 294944 | tf_op jit(solution)/shard_map/ppermute | solution.py:496
  118.8 5.8 %unpack.3.refs_3_ = bf16[192,8,1024]{2,1,0:T(8,128)(2,1)} custom-call(s32[2]{0:T(128)S(1)} %pad_add_fusion.scalars, bf16[2,3,192,128]{3,2,1,0:T(8,128)(2,1)S(1)} %get-tuple-element.139.refs_0_, bf16[2,3,192,128]{3,2,1,0:T(8,128)(2,1)S(1)} %collective-permute-done.17.refs_1_, bf16[2,3,192,128]{3,2,1,0:T(8,128)(2,1)S(1)} %collective-permute-done.18.refs_2_, ...), custom_call_target="tpu_custom_call" | custom-call | flops 1 | bytes 1 | tf_op jit(solution)/shard_map/unpack/pallas_call | solution.py:475
  124.6 4.2 %unpack.4.refs_3_ = bf16[192,8,1024]{2,1,0:T(8,128)(2,1)} custom-call(s32[2]{0:T(128)S(1)} %pad_add_fusion.scalars, bf16[2,3,192,128]{3,2,1,0:T(8,128)(2,1)S(1)} %get-tuple-element.131.refs_0_, bf16[2,3,192,128]{3,2,1,0:T(8,128)(2,1)S(1)} %collective-permute-done.13.refs_1_, ...), custom_call_target="tpu_custom_call", output_to_operand_aliasing={{}: (4, {})} | custom-call | flops 1 | bytes 1 | tf_op jit(solution)/shard_map/unpack/pallas_call | solution.py:475
  128.8 4.2 %unpack.5 = bf16[192,8,1024]{2,1,0:T(8,128)(2,1)} custom-call(s32[2]{0:T(128)S(1)} %pad_add_fusion.scalars, bf16[2,3,192,128]{3,2,1,0:T(8,128)(2,1)S(1)} %collective-permute-done.11.refs_0_, bf16[2,3,192,128]{3,2,1,0:T(8,128)(2,1)S(1)} %collective-permute-done.12.refs_1_, ...), custom_call_target="tpu_custom_call", output_to_operand_aliasing={{}: (4, {})} | custom-call | flops 1 | bytes 1 | tf_op jit(solution)/shard_map/unpack/pallas_call | solution.py:475
  (47 shorter events, 0.1 us)
Async XLA Ops:
  0.0 6.9 %copy-start = (f32[16,32]{1,0:T(8,128)S(1)}, f32[16,32]{1,0:T(8,128)}, u32[]{:S(2)}) copy-start(f32[16,32]{1,0:T(8,128)} %param.14) | copy-start | bytes 6148
  0.0 7.0 %copy-start.20 = (f32[2,24]{1,0:T(2,128)S(1)}, f32[2,24]{1,0:T(2,128)}, u32[]{:S(2)}) copy-start(f32[2,24]{1,0:T(2,128)} %constant.34.clone) | copy-start | bytes 580
  0.0 7.1 %copy-start.1 = (bf16[192,8,1024]{2,1,0:T(8,128)(2,1)S(1)}, bf16[192,8,1024]{2,1,0:T(8,128)(2,1)}, u32[]{:S(2)}) copy-start(bf16[192,8,1024]{2,1,0:T(8,128)(2,1)} %refs_0_.5) | copy-start | bytes 9437188
  4.2 14.5 %copy-start.3 = (s32[8,1024]{1,0:T(8,128)S(1)}, s32[8,1024]{1,0:T(8,128)}, u32[]{:S(2)}) copy-start(s32[8,1024]{1,0:T(8,128)} %get-tuple-element.109.refs_3_.refs_1_) | copy-start | bytes 98308
  4.2 20.2 %collective-permute-start = (bf16[49,8,1024]{2,1,0:T(8,128)(2,1)}, bf16[49,8,1024]{2,1,0:T(8,128)(2,1)}, u32[]{:S(2)}, u32[]{:S(2)}) collective-permute-start(bf16[49,8,1024]{2,1,0:T(8,128)(2,1)} %get-tuple-element.107), channel_id=1, source_target_pairs={{0,4},{4,8},{8,12},{12,16},{16,20},{20,24},{24,28},{28,0},{1,5},{5... | collective-permute-start | bytes 2408456 | tf_op jit(solution)/shard_map/ppermute | solution.py:527
  4.2 24.1 %collective-permute-start.1 = (bf16[49,8,1024]{2,1,0:T(8,128)(2,1)}, bf16[49,8,1024]{2,1,0:T(8,128)(2,1)}, u32[]{:S(2)}, u32[]{:S(2)}) collective-permute-start(bf16[49,8,1024]{2,1,0:T(8,128)(2,1)} %get-tuple-element.108), channel_id=1, source_target_pairs={{4,0},{8,4},{12,8},{16,12},{20,16},{24,20},{28,24},{0,28},{5,1},{9... | collective-permute-start | bytes 2408456 | tf_op jit(solution)/shard_map/ppermute | solution.py:527
  7.1 0.8 copy-start.2
  13.2 34.5 %collective-permute-start.2 = (bf16[4,96,256]{2,1,0:T(8,128)(2,1)}, bf16[4,96,256]{2,1,0:T(8,128)(2,1)}, u32[]{:S(2)}, u32[]{:S(2)}) collective-permute-start(bf16[4,96,256]{2,1,0:T(8,128)(2,1)} %get-tuple-element.115), channel_id=1, source_target_pairs={{0,1},{1,0},{2,3},{3,2},{4,5},{5,4},{6,7},{7,6},{8,9},{9,8},{10,11... | collective-permute-start | bytes 589832 | tf_op jit(solution)/shard_map/ppermute | solution.py:496
  13.2 35.0 %collective-permute-start.3 = (bf16[4,96,256]{2,1,0:T(8,128)(2,1)}, bf16[4,96,256]{2,1,0:T(8,128)(2,1)}, u32[]{:S(2)}, u32[]{:S(2)}) collective-permute-start(bf16[4,96,256]{2,1,0:T(8,128)(2,1)} %get-tuple-element.116), channel_id=1, source_target_pairs={{0,2},{1,3},{2,0},{3,1},{4,6},{5,7},{6,4},{7,5},{8,10},{9,11},{10,... | collective-permute-start | bytes 589832 | tf_op jit(solution)/shard_map/ppermute | solution.py:496
  16.3 34.4 %collective-permute-start.4 = (bf16[4,96,256]{2,1,0:T(8,128)(2,1)}, bf16[4,96,256]{2,1,0:T(8,128)(2,1)}, u32[]{:S(2)}, u32[]{:S(2)}) collective-permute-start(bf16[4,96,256]{2,1,0:T(8,128)(2,1)} %get-tuple-element.117), channel_id=1, source_target_pairs={{0,3},{1,2},{2,1},{3,0},{4,7},{5,6},{6,5},{7,4},{8,11},{9,10},{10,... | collective-permute-start | bytes 589832 | tf_op jit(solution)/shard_map/ppermute | solution.py:496
  23.3 5.0 %copy-start.13 = (bf16[4,96,256]{2,1,0:T(8,128)(2,1)}, bf16[4,96,256]{2,1,0:T(8,128)(2,1)S(1)}, u32[]{:S(2)}) copy-start(bf16[4,96,256]{2,1,0:T(8,128)(2,1)S(1)} %get-tuple-element.120.piece) | copy-start | bytes 589828
  23.3 5.0 %copy-start.14 = (bf16[4,96,256]{2,1,0:T(8,128)(2,1)}, bf16[4,96,256]{2,1,0:T(8,128)(2,1)S(1)}, u32[]{:S(2)}) copy-start(bf16[4,96,256]{2,1,0:T(8,128)(2,1)S(1)} %get-tuple-element.121.piece) | copy-start | bytes 589828
  23.3 5.0 %copy-start.15 = (bf16[4,96,256]{2,1,0:T(8,128)(2,1)}, bf16[4,96,256]{2,1,0:T(8,128)(2,1)S(1)}, u32[]{:S(2)}) copy-start(bf16[4,96,256]{2,1,0:T(8,128)(2,1)S(1)} %get-tuple-element.122.piece) | copy-start | bytes 589828
  23.3 27.9 %copy-start.11 = (bf16[4,96,256]{2,1,0:T(8,128)(2,1)}, bf16[4,96,256]{2,1,0:T(8,128)(2,1)S(1)}, u32[]{:S(2)}) copy-start(bf16[4,96,256]{2,1,0:T(8,128)(2,1)S(1)} %get-tuple-element.119.piece) | copy-start | bytes 589828
  24.5 21.1 %collective-permute-start.7 = (bf16[6,96,128]{2,1,0:T(8,128)(2,1)S(1)}, bf16[6,96,128]{2,1,0:T(8,128)(2,1)S(1)}, u32[]{:S(2)}, u32[]{:S(2)}) collective-permute-start(bf16[6,96,128]{2,1,0:T(8,128)(2,1)S(1)} %pack_points.28), channel_id=1, source_target_pairs={{0,3},{1,2},{2,1},{3,0},{4,7},{5,6},{6,5},{7,4},{8,11},{9,10},{10,... | collective-permute-start | bytes 442376 | tf_op jit(solution)/shard_map/ppermute | solution.py:496
  28.3 38.1 %copy-start.19 = (f32[2,24]{1,0:T(2,128)S(1)}, f32[2,24]{1,0:T(2,128)}, u32[]{:S(2)}) copy-start(f32[2,24]{1,0:T(2,128)} %constant.35.clone) | copy-start | bytes 580
  28.3 33.5 %collective-permute-start.6 = (bf16[6,96,128]{2,1,0:T(8,128)(2,1)S(1)}, bf16[6,96,128]{2,1,0:T(8,128)(2,1)}, u32[]{:S(2)}, u32[]{:S(2)}) collective-permute-start(bf16[6,96,128]{2,1,0:T(8,128)(2,1)S(1)} %pack_points.27), channel_id=1, source_target_pairs={{0,2},{1,3},{2,0},{3,1},{4,6},{5,7},{6,4},{7,5},{8,10},{9,11},{10,... | collective-permute-start | bytes 442376 | tf_op jit(solution)/shard_map/ppermute | solution.py:496
  41.9 9.3 %copy-start.8 = (bf16[4,192,256]{2,1,0:T(8,128)(2,1)}, bf16[4,192,256]{2,1,0:T(8,128)(2,1)S(1)}, u32[]{:S(2)}) copy-start(bf16[4,192,256]{2,1,0:T(8,128)(2,1)S(1)} %get-tuple-element.124.piece) | copy-start | bytes 1179652
  41.9 9.3 %copy-start.9 = (bf16[4,192,256]{2,1,0:T(8,128)(2,1)}, bf16[4,192,256]{2,1,0:T(8,128)(2,1)S(1)}, u32[]{:S(2)}) copy-start(bf16[4,192,256]{2,1,0:T(8,128)(2,1)S(1)} %get-tuple-element.126.piece) | copy-start | bytes 1179652
  41.9 9.3 %copy-start.10 = (bf16[4,192,256]{2,1,0:T(8,128)(2,1)}, bf16[4,192,256]{2,1,0:T(8,128)(2,1)S(1)}, u32[]{:S(2)}) copy-start(bf16[4,192,256]{2,1,0:T(8,128)(2,1)S(1)} %get-tuple-element.128.piece) | copy-start | bytes 1179652
  45.5 0.7 copy-start.6
  46.2 17.2 %collective-permute-start.5 = (bf16[6,96,128]{2,1,0:T(8,128)(2,1)S(1)}, bf16[6,96,128]{2,1,0:T(8,128)(2,1)S(1)}, u32[]{:S(2)}, u32[]{:S(2)}) collective-permute-start(bf16[6,96,128]{2,1,0:T(8,128)(2,1)S(1)} %pack_points.26), channel_id=1, source_target_pairs={{0,1},{1,0},{2,3},{3,2},{4,5},{5,4},{6,7},{7,6},{8,9},{9,8},{10,11... | collective-permute-start | bytes 442376 | tf_op jit(solution)/shard_map/ppermute | solution.py:496
  47.7 18.1 %collective-permute-start.14 = (bf16[3,192,128]{2,1,0:T(8,128)(2,1)S(1)}, bf16[3,192,128]{2,1,0:T(8,128)(2,1)S(1)}, u32[]{:S(2)}, u32[]{:S(2)}) collective-permute-start(bf16[3,192,128]{2,1,0:T(8,128)(2,1)S(1)} %get-tuple-element.136), channel_id=1, source_target_pairs={{0,1},{1,0},{2,3},{3,2},{4,5},{5,4},{6,7},{7,6},{8,9},{9,8},{10,11... | collective-permute-start | bytes 442376 | tf_op jit(solution)/shard_map/ppermute | solution.py:496
  48.2 18.1 %collective-permute-start.15 = (bf16[3,192,128]{2,1,0:T(8,128)(2,1)S(1)}, bf16[3,192,128]{2,1,0:T(8,128)(2,1)S(1)}, u32[]{:S(2)}, u32[]{:S(2)}) collective-permute-start(bf16[3,192,128]{2,1,0:T(8,128)(2,1)S(1)} %get-tuple-element.137), channel_id=1, source_target_pairs={{0,2},{1,3},{2,0},{3,1},{4,6},{5,7},{6,4},{7,5},{8,10},{9,11},{10,... | collective-permute-start | bytes 442376 | tf_op jit(solution)/shard_map/ppermute | solution.py:496
  50.7 15.7 %collective-permute-start.16 = (bf16[3,192,128]{2,1,0:T(8,128)(2,1)S(1)}, bf16[3,192,128]{2,1,0:T(8,128)(2,1)S(1)}, u32[]{:S(2)}, u32[]{:S(2)}) collective-permute-start(bf16[3,192,128]{2,1,0:T(8,128)(2,1)S(1)} %get-tuple-element.138), channel_id=1, source_target_pairs={{0,3},{1,2},{2,1},{3,0},{4,7},{5,6},{6,5},{7,4},{8,11},{9,10},{10,... | collective-permute-start | bytes 442376 | tf_op jit(solution)/shard_map/ppermute | solution.py:496
  53.1 0.6 copy-start.16
  61.9 19.1 %collective-permute-start.8 = (bf16[3,192,128]{2,1,0:T(8,128)(2,1)S(1)}, bf16[3,192,128]{2,1,0:T(8,128)(2,1)S(1)}, u32[]{:S(2)}, u32[]{:S(2)}) collective-permute-start(bf16[3,192,128]{2,1,0:T(8,128)(2,1)S(1)} %get-tuple-element.125), channel_id=1, source_target_pairs={{0,1},{1,0},{2,3},{3,2},{4,5},{5,4},{6,7},{7,6},{8,9},{9,8},{10,11... | collective-permute-start | bytes 442376 | tf_op jit(solution)/shard_map/ppermute | solution.py:496
  63.4 18.1 %collective-permute-start.9 = (bf16[3,192,128]{2,1,0:T(8,128)(2,1)S(1)}, bf16[3,192,128]{2,1,0:T(8,128)(2,1)S(1)}, u32[]{:S(2)}, u32[]{:S(2)}) collective-permute-start(bf16[3,192,128]{2,1,0:T(8,128)(2,1)S(1)} %get-tuple-element.127), channel_id=1, source_target_pairs={{0,2},{1,3},{2,0},{3,1},{4,6},{5,7},{6,4},{7,5},{8,10},{9,11},{10,... | collective-permute-start | bytes 442376 | tf_op jit(solution)/shard_map/ppermute | solution.py:496
  65.8 15.7 %collective-permute-start.10 = (bf16[3,192,128]{2,1,0:T(8,128)(2,1)S(1)}, bf16[3,192,128]{2,1,0:T(8,128)(2,1)S(1)}, u32[]{:S(2)}, u32[]{:S(2)}) collective-permute-start(bf16[3,192,128]{2,1,0:T(8,128)(2,1)S(1)} %get-tuple-element.129), channel_id=1, source_target_pairs={{0,3},{1,2},{2,1},{3,0},{4,7},{5,6},{6,5},{7,4},{8,11},{9,10},{10,... | collective-permute-start | bytes 442376 | tf_op jit(solution)/shard_map/ppermute | solution.py:496
  66.4 0.9 copy-start.7
  67.3 14.1 %copy-start.21 = (bf16[768,768]{1,0:T(8,128)(2,1)S(1)}, bf16[768,768]{1,0:T(8,128)(2,1)}, u32[]{:S(2)}) copy-start(bf16[768,768]{1,0:T(8,128)(2,1)} %refs_10_.3) | copy-start | bytes 3538948
  77.1 18.2 %collective-permute-start.17 = (bf16[2,3,192,128]{3,2,1,0:T(8,128)(2,1)S(1)}, bf16[2,3,192,128]{3,2,1,0:T(8,128)(2,1)S(1)}, u32[]{:S(2)}, u32[]{:S(2)}) collective-permute-start(bf16[2,3,192,128]{3,2,1,0:T(8,128)(2,1)S(1)} %get-tuple-element.140), channel_id=1, source_target_pairs={{0,1},{1,0},{2,3},{3,2},{4,5},{5,4},{6,7},{7,6},{8,9},{9,8},{10,11... | collective-permute-start | bytes 884744 | tf_op jit(solution)/shard_map/ppermute | solution.py:496
  78.5 30.0 %collective-permute-start.18 = (bf16[2,3,192,128]{3,2,1,0:T(8,128)(2,1)S(1)}, bf16[2,3,192,128]{3,2,1,0:T(8,128)(2,1)S(1)}, u32[]{:S(2)}, u32[]{:S(2)}) collective-permute-start(bf16[2,3,192,128]{3,2,1,0:T(8,128)(2,1)S(1)} %get-tuple-element.141), channel_id=1, source_target_pairs={{0,2},{1,3},{2,0},{3,1},{4,6},{5,7},{6,4},{7,5},{8,10},{9,11},{10,... | collective-permute-start | bytes 884744 | tf_op jit(solution)/shard_map/ppermute | solution.py:496
  81.0 37.8 %collective-permute-start.19 = (bf16[2,3,192,128]{3,2,1,0:T(8,128)(2,1)S(1)}, bf16[2,3,192,128]{3,2,1,0:T(8,128)(2,1)S(1)}, u32[]{:S(2)}, u32[]{:S(2)}) collective-permute-start(bf16[2,3,192,128]{3,2,1,0:T(8,128)(2,1)S(1)} %get-tuple-element.142), channel_id=1, source_target_pairs={{0,3},{1,2},{2,1},{3,0},{4,7},{5,6},{6,5},{7,4},{8,11},{9,10},{10,... | collective-permute-start | bytes 884744 | tf_op jit(solution)/shard_map/ppermute | solution.py:496
  81.5 24.2 %copy-start.12 = (bf16[4,96,256]{2,1,0:T(8,128)(2,1)S(1)}, bf16[4,96,256]{2,1,0:T(8,128)(2,1)}, u32[]{:S(2)}) copy-start(bf16[4,96,256]{2,1,0:T(8,128)(2,1)} %copy-done.11) | copy-start | bytes 589828
  91.4 37.4 %collective-permute-start.11 = (bf16[2,3,192,128]{3,2,1,0:T(8,128)(2,1)}, bf16[2,3,192,128]{3,2,1,0:T(8,128)(2,1)S(1)}, u32[]{:S(2)}, u32[]{:S(2)}) collective-permute-start(bf16[2,3,192,128]{3,2,1,0:T(8,128)(2,1)} %get-tuple-element.133), channel_id=1, source_target_pairs={{0,2},{1,3},{2,0},{3,1},{4,6},{5,7},{6,4},{7,5},{8,10},{9,11},{10,... | collective-permute-start | bytes 884744 | tf_op jit(solution)/shard_map/ppermute | solution.py:496
  95.2 29.4 %collective-permute-start.13 = (bf16[2,3,192,128]{3,2,1,0:T(8,128)(2,1)}, bf16[2,3,192,128]{3,2,1,0:T(8,128)(2,1)S(1)}, u32[]{:S(2)}, u32[]{:S(2)}) collective-permute-start(bf16[2,3,192,128]{3,2,1,0:T(8,128)(2,1)} %get-tuple-element.135), channel_id=1, source_target_pairs={{0,1},{1,0},{2,3},{3,2},{4,5},{5,4},{6,7},{7,6},{8,9},{9,8},{10,11... | collective-permute-start | bytes 884744 | tf_op jit(solution)/shard_map/ppermute | solution.py:496
  95.2 33.6 %collective-permute-start.12 = (bf16[2,3,192,128]{3,2,1,0:T(8,128)(2,1)S(1)}, bf16[2,3,192,128]{3,2,1,0:T(8,128)(2,1)S(1)}, u32[]{:S(2)}, u32[]{:S(2)}) collective-permute-start(bf16[2,3,192,128]{3,2,1,0:T(8,128)(2,1)S(1)} %get-tuple-element.134), channel_id=1, source_target_pairs={{0,3},{1,2},{2,1},{3,0},{4,7},{5,6},{6,5},{7,4},{8,11},{9,10},{10,... | collective-permute-start | bytes 884744 | tf_op jit(solution)/shard_map/ppermute | solution.py:496

commit v4 on v3

--- a/solution.py
+++ b/solution.py
@@ -346,7 +346,7 @@
         ),
         out_shape=outs,
         compiler_params=pltpu.CompilerParams(vmem_limit_bytes=VMEM_LIMIT),
-        cost_estimate=SHORT,
+        cost_estimate=pl.CostEstimate(flops=int(5.0e6 * 1153), bytes_accessed=1, transcendentals=0),
         name="pack_first",
     )(z, *pieces, ranks, wind_c, wind_s)
 
@@ -393,9 +393,9 @@
             outs[s][g, 0] = state[at, g * width : (g + 1) * width].astype(jnp.bfloat16)
 
 
-def sources(z, first, later, second, winds, coupling, trig, first_block):
+def sources(z, first, later, second, winds, coupling, trig, first_block, blocks):
     count = len(second)
-    blocks, comps, width = second[0].shape
+    _, comps, width = second[0].shape
     total = comps * count
     whole = lambda a: pl.BlockSpec(a.shape, lambda i, z: (0,) * a.ndim)
     return pl.pallas_call(
@@ -404,7 +404,10 @@
             num_scalar_prefetch=1,
             grid=(blocks,),
             in_specs=[pl.BlockSpec((1,) + a.shape[1:], lambda i, z: (first_block + i, 0, 0)) for a in [first, *later]]
-            + [pl.BlockSpec((1, comps, width), lambda i, z: (i, 0, 0)) for a in second]
+            + [
+                pl.BlockSpec((1, comps, width), lambda i, z, at=0 if a.shape[0] == blocks else first_block: (at + i, 0, 0))
+                for a in second
+            ]
             + [pl.BlockSpec((4, 1, width), lambda i, z: (0, 0, first_block + i)), whole(coupling), whole(trig)],
             out_specs=[pl.BlockSpec((2, 1, comps, width), lambda i, z: (0, i, 0, 0))] * count,
             scratch_shapes=[
@@ -417,7 +420,7 @@
         out_shape=[jax.ShapeDtypeStruct((2, blocks, comps, width), jnp.bfloat16)] * count,
         compiler_params=pltpu.CompilerParams(vmem_limit_bytes=VMEM_LIMIT),
         cost_estimate=pl.CostEstimate(
-            flops=SRC_STEPS * 2 * total**2 * 2 * blocks * width, bytes_accessed=8 * total * blocks * width, transcendentals=0
+            flops=int(SRC_STEPS * 2 * total**2 * 2 * blocks * width / 1.0), bytes_accessed=1, transcendentals=0
         ),
         name="source_terms",
     )(z, first, *later, *second, winds, coupling, trig)
@@ -491,9 +494,13 @@
     )(scalars, *inputs, ranks, *extra)
 
 
+def send(block, s, count):
+    return lax.ppermute(block, "comp", [(i, i ^ s) for i in range(count)])
+
+
 def exchange(blocks, axis):
     count = len(blocks)
-    came = {s: lax.ppermute(blocks[s], axis, [(i, i ^ s) for i in range(count)]) for s in range(count - 1, 0, -1)}
+    came = {s: send(blocks[s], s, count) for s in range(count - 1, 0, -1)}
     return [blocks[0]] + [came[s] for s in range(1, count)]
 
 
@@ -519,9 +526,6 @@
     trig = jnp.broadcast_to(jnp.asarray(np.stack([np.abs(COS), np.abs(SIN)]))[:, :, None], (2, K, LANES))
     signed = jnp.broadcast_to(jnp.asarray(np.stack([COS, SIN]))[:, :, None], (2, K, LANES))
     start = place * width
-    speed_part = 0.002 * lax.dynamic_slice_in_dim(wind_speed, start, width, 1)
-    dir_part = lax.dynamic_slice_in_dim(wind_dir, start, width, 1)
-    wind_c, wind_s = (speed_part * jnp.cos(dir_part))[:, None], (speed_part * jnp.sin(dir_part))[:, None]
 
     to_east, to_west, code = pack_halo(spectrum, sea_mask, depth_class)
     halo = lax.ppermute(to_east, "tile", east), lax.ppermute(to_west, "tile", west)
@@ -532,13 +536,26 @@
     chunks = 2 if main % 2 == 0 else 1
     size = main // chunks
     parts = [(s, 0, width) for s in range(count)]
-    first = exchange(propagate(z, spectrum, code, table, trig, parts, 0, half), "comp")
+    first = propagate(z, spectrum, code, table, trig, parts, 0, half)
+    first = list(first)
+    sea_late, _ = lax.optimization_barrier((sea_mask, first[0]))
+    ranks, most = sea_ranks(sea_late, count)
+    first[1], _ = lax.optimization_barrier((first[1], ranks))
+    first = exchange(first, "comp")
     later = propagate(z, spectrum, code, table, trig, parts, half, pairs - half)
-    ranks, most = sea_ranks(sea_mask, count)
-    packed_later = [pack_points(z, s, later[s], ranks, True, 0, [main])[0] for s in range(count)]
-    packed_later = exchange(packed_later, "comp")
+    pack_later = lambda s, piece: pack_points(z, s, piece, ranks, True, 0, [main])[0]
+    later = list(later)
+    packed_later = {s: send(pack_later(s, later[s]), s, count) for s in range(count - 1, 1, -1)}
     second = propagate(z, spectrum, code, table, trig, parts, 0, pairs, halo)
-    packed = [pack_points(z, s, second[s], ranks, False, 0, [size] * chunks) for s in range(count)]
+    later[1], _ = lax.optimization_barrier((later[1], second[0]))
+    packed_later[1] = send(pack_later(1, later[1]), 1, count)
+    packed = [pack_points(z, s, second[s], ranks, False, 0, [main] if s == 1 else [size] * chunks) for s in range(count)]
+    near = send(packed[1][0], 1, count)
+    own, speed, direction, _ = lax.optimization_barrier((later[0], wind_speed, wind_dir, packed[1][0]))
+    speed_part = 0.002 * lax.dynamic_slice_in_dim(speed, start, width, 1)
+    dir_part = lax.dynamic_slice_in_dim(direction, start, width, 1)
+    wind_c, wind_s = (speed_part * jnp.cos(dir_part))[:, None], (speed_part * jnp.sin(dir_part))[:, None]
+    packed_later = [pack_later(0, own)] + [packed_later[s] for s in range(1, count)]
     packed_first, winds = pack_first(z, first, ranks, wind_c, wind_s, count, 0, main)
 
     def remainder(first, later, second, ranks, wind_c, wind_s, coupling):
@@ -547,15 +564,16 @@
         low = [pack_points(z, s, later[s], ranks, True, main, [rest])[0] for s in range(count)]
         high = [pack_points(z, s, second[s], ranks, False, main, [rest])[0] for s in range(count)]
         low, high = exchange_rare(low, "comp"), exchange_rare(high, "comp")
-        return exchange_rare(sources(z, down, low, high, winds, coupling, signed, 0), "comp")
+        return exchange_rare(sources(z, down, low, high, winds, coupling, signed, 0, rest), "comp")
 
     def nothing(*args):
         return [jnp.zeros((2, blocks - main, comps, LANES), jnp.bfloat16)] * count
 
     updated = []
     for c in range(chunks):
-        arrived = exchange([packed[s][c] for s in range(count)], "comp")
-        sent = sources(z, packed_first, packed_later, arrived, winds, coupling, signed, c * size)
+        far = {s: send(packed[s][c], s, count) for s in range(count - 1, 1, -1)}
+        arrived = [packed[0][c], near] + [far[s] for s in range(2, count)]
+        sent = sources(z, packed_first, packed_later, arrived, winds, coupling, signed, c * size, size)
         updated.append(exchange(sent, "comp"))
         if c == 0:
             most, _ = lax.optimization_barrier((most, arrived[0]))

time: 134 us -> 132 us (0.985)
  waiting for transfers between devices: 10.2 us -> 13.1 us
  local copies, waits for them, and re-layouts: 7.27 us -> 4.49 us
  Pallas kernels: 77.6 us -> 75.8 us
    ppermute x18 -> x17, waiting for transfers between devices: 10.2 us -> 13.1 us  [send(): return lax.ppermute(block, 'comp', [(i, i ^ s) for i in range(count)])]
    unnamed x37, local copies, waits for them, and re-layouts: 3.02 us -> 0.91 us
    ppermute x18 -> x17, starting transfers between devices: 25.4 us -> 24.7 us  [send(): return lax.ppermute(block, 'comp', [(i, i ^ s) for i in range(count)])]
  transfers between devices with their start and end apart: 20 -> 19, of which waited for: 1 -> 4; matrix products, arithmetic and copies ran while one was open for 4% -> 3% of each run, Pallas kernels for 52% -> 52%
where the time goes in v4:
time: 132 us; the launch traced here: 131 us
  Pallas kernels  75.8 us (57%)
  starting transfers between devices  27.3 us (21%)
  waiting for transfers between devices  13.1 us (10%)
  blocking collectives  8.27 us (6%)
  local copies, waits for them, and re-layouts  4.49 us (3%)
    ppermute x17, starting transfers between devices, send(): return lax.ppermute(block, 'comp', [(i, i ^ s) for i in range(count)])  24.7 us
    pallas_call x3, Pallas kernels, propagate(): pl.pallas_call(functools.partial(propagate_kernel, halo is not None, part...  21.7 us
    pallas_call x2, Pallas kernels, sources(): pl.pallas_call(functools.partial(sources_kernel, count), grid_spec=pltpu....  18.9 us
    pallas_call x3, Pallas kernels, unpack(): pl.pallas_call(functools.partial(unpack_kernel, partners, first_block, re...  14 us
    ppermute x17, waiting for transfers between devices, send(): return lax.ppermute(block, 'comp', [(i, i ^ s) for i in range(count)])  13.1 us
    pallas_call x8, Pallas kernels, pack_points(): pl.pallas_call(functools.partial(pack_points_kernel, downwind, first_bloc...  9.15 us
    pmax x1, blocking collectives, on_device(): full = lax.pmax(most[0, 0], 'tile') > main * LANES  8.27 us
    pallas_call x1, Pallas kernels, pack_first(): pl.pallas_call(functools.partial(pack_first_kernel, first_block, count),...  5.85 us
  transfers between devices with their start and end apart: 19, of which 4 were waited for; matrix products, arithmetic and copies ran while one was open for 3% of the time, Pallas kernels for 52%

profile of v4, /device:TPU:8, one launch (start us, length us, event | category | flops | bytes accessed | tf_op | source)
XLA Modules:
  0.0 130.9 jit_solution(17889670689969183520)
XLA Ops:
  0.0 4.2 %pack_halo.1 = (bf16[49,8,1024]{2,1,0:T(8,128)(2,1)}, bf16[49,8,1024]{2,1,0:T(8,128)(2,1)}, s32[8,1024]{1,0:T(8,128)}) custom-call(bf16[192,8,1024]{2,1,0:T(8,128)(2,1)} %refs_0_.5, s32[8,1024]{1,0:T(8,128)} %sea.2, s32[8,1024]{1,0:T(8,128)} %depth.1), custom_call_target="tpu_custom_call" | custom-call | tf_op jit(solution)/shard_map/pack_halo/pallas_call | solution.py:54
  4.2 0.0 collective-permute-start
  4.2 2.6 %collective-permute-start.1 = (bf16[49,8,1024]{2,1,0:T(8,128)(2,1)}, bf16[49,8,1024]{2,1,0:T(8,128)(2,1)}, u32[]{:S(2)}, u32[]{:S(2)}) collective-permute-start(bf16[49,8,1024]{2,1,0:T(8,128)(2,1)} %get-tuple-element.115), channel_id=1, source_target_pairs={{4,0},{8,4},{12,8},{16,12},{20,16},{24,20},{28,24},{0,28},{5,1},{9... | collective-permute-start | bytes 2408456 | tf_op jit(solution)/shard_map/ppermute | solution.py:531
  6.9 0.1 constant_dynamic-slice_fusion
  6.9 0.1 copy.15
  7.0 0.1 broadcast_in_dim.11.refs_3_.refs_7_
  7.1 0.8 copy-done.2
  7.9 5.4 %propagate_downwind.2 = (bf16[4,96,256]{2,1,0:T(8,128)(2,1)}, bf16[4,96,256]{2,1,0:T(8,128)(2,1)}, bf16[4,96,256]{2,1,0:T(8,128)(2,1)}, bf16[4,96,256]{2,1,0:T(8,128)(2,1)}) custom-call(s32[1]{0:T(128)} %bitcast.25.pos, bf16[192,8,1024]{2,1,0:T(8,128)(2,1)S(1)} %copy-done.1, s32[8,1024]{1,0:T(8,128)S(1)} %copy-done.2, f32[8,1,128]{2,1,0:T(1,128)S(1)} %bitcast.57, ...), custom_call_target="tpu_custom_call" | custom-call | flops 23592960 | bytes 4718592 | tf_op jit(solution)/shard_map/propagate_downwind/pallas_call | solution.py:200
  13.2 2.0 %sea_ranks.1 = (s32[4,2,1,1024]{3,2,1,0:T(1,128)S(1)}, s32[8,128]{1,0:T(8,128)}) custom-call(s32[8,1024]{1,0:T(8,128)} %sea.2), custom_call_target="tpu_custom_call" | custom-call | flops 1 | bytes 1 | tf_op jit(solution)/shard_map/sea_ranks/pallas_call | solution.py:243
  15.2 3.0 %collective-permute-start.3 = (bf16[4,96,256]{2,1,0:T(8,128)(2,1)}, bf16[4,96,256]{2,1,0:T(8,128)(2,1)}, u32[]{:S(2)}, u32[]{:S(2)}) collective-permute-start(bf16[4,96,256]{2,1,0:T(8,128)(2,1)} %get-tuple-element.122), channel_id=1, source_target_pairs={{0,2},{1,3},{2,0},{3,1},{4,6},{5,7},{6,4},{7,5},{8,10},{9,11},{10,... | collective-permute-start | bytes 589832 | tf_op jit(solution)/shard_map/ppermute | solution.py:498
  18.2 0.5 collective-permute-start.4
  18.7 5.3 %propagate_downwind.3 = (bf16[4,96,256]{2,1,0:T(8,128)(2,1)}, bf16[4,96,256]{2,1,0:T(8,128)(2,1)}, bf16[4,96,256]{2,1,0:T(8,128)(2,1)S(1)}, bf16[4,96,256]{2,1,0:T(8,128)(2,1)S(1)}) custom-call(s32[1]{0:T(128)} %bitcast.25.pos, bf16[192,8,1024]{2,1,0:T(8,128)(2,1)S(1)} %copy-done.1, s32[8,1024]{1,0:T(8,128)S(1)} %copy-done.3, f32[8,1,128]{2,1,0:T(1,128)S(1)} %bitcast.58, ...), custom_call_target="tpu_custom_call" | custom-call | flops 23592960 | bytes 4718592 | tf_op jit(solution)/shard_map/propagate_downwind/pallas_call | solution.py:200
  23.9 1.1 pack_points.28
  25.0 0.0 collective-permute-done.refs_1_.refs_4_
  25.0 3.5 %collective-permute-start.6 = (bf16[6,96,128]{2,1,0:T(8,128)(2,1)S(1)}, bf16[6,96,128]{2,1,0:T(8,128)(2,1)}, u32[]{:S(2)}, u32[]{:S(2)}) collective-permute-start(bf16[6,96,128]{2,1,0:T(8,128)(2,1)S(1)} %pack_points.28), channel_id=1, source_target_pairs={{0,2},{1,3},{2,0},{3,1},{4,6},{5,7},{6,4},{7,5},{8,10},{9,11},{10,... | collective-permute-start | bytes 442376 | tf_op jit(solution)/shard_map/ppermute | solution.py:498
  28.6 1.1 pack_points.29
  29.7 0.0 collective-permute-done.1.refs_2_.refs_5_
  29.7 0.1 collective-permute-start.7
  29.8 11.1 %propagate_upwind.1 = (bf16[4,192,256]{2,1,0:T(8,128)(2,1)S(1)}, bf16[4,192,256]{2,1,0:T(8,128)(2,1)S(1)}, bf16[4,192,256]{2,1,0:T(8,128)(2,1)S(1)}, bf16[4,192,256]{2,1,0:T(8,128)(2,1)S(1)}) custom-call(s32[1]{0:T(128)} %bitcast.25.pos, bf16[192,8,1024]{2,1,0:T(8,128)(2,1)S(1)} %copy-done.1, bf16[49,8,1024]{2,1,0:T(8,128)(2,1)} %collective-permute-done.refs_1_.refs_4_, ...), custom_call_target="tpu_custom_call" | custom-call | flops 47185920 | bytes 9437184 | tf_op jit(solution)/shard_map/propagate_upwind/pallas_call | solution.py:200
  40.9 1.1 pack_points.27
  42.0 1.2 pack_points.25
  43.2 1.2 pack_points.30
  44.5 1.2 pack_points.31
  45.7 0.8 sine_multiply_fusion
  46.5 0.0 copy-start.14
  46.5 0.0 collective-permute-done.6.refs_3_
  46.5 1.5 %collective-permute-start.8 = (bf16[6,192,128]{2,1,0:T(8,128)(2,1)S(1)}, bf16[6,192,128]{2,1,0:T(8,128)(2,1)S(1)}, u32[]{:S(2)}, u32[]{:S(2)}) collective-permute-start(bf16[6,192,128]{2,1,0:T(8,128)(2,1)S(1)} %pack_points.25), channel_id=1, source_target_pairs={{0,1},{1,0},{2,3},{3,2},{4,5},{5,4},{6,7},{7,6},{8,9},{9,8},{10,11... | collective-permute-start | bytes 884744 | tf_op jit(solution)/shard_map/ppermute | solution.py:498
  48.0 0.0 collective-permute-done.2.refs_1_
  48.0 0.6 collective-permute-start.5
  48.6 0.0 collective-permute-done.3.refs_2_
  48.6 2.1 %collective-permute-start.14 = (bf16[3,192,128]{2,1,0:T(8,128)(2,1)S(1)}, bf16[3,192,128]{2,1,0:T(8,128)(2,1)S(1)}, u32[]{:S(2)}, u32[]{:S(2)}) collective-permute-start(bf16[3,192,128]{2,1,0:T(8,128)(2,1)S(1)} %get-tuple-element.145), channel_id=1, source_target_pairs={{0,2},{1,3},{2,0},{3,1},{4,6},{5,7},{6,4},{7,5},{8,10},{9,11},{10,... | collective-permute-start | bytes 442376 | tf_op jit(solution)/shard_map/ppermute | solution.py:498
  50.7 0.0 collective-permute-done.4.refs_3_
  50.7 0.0 copy-start.16
  50.7 0.0 copy-start.18
  50.7 0.8 collective-permute-start.15
  51.6 5.9 %pack_first.3 = (bf16[6,384,128]{2,1,0:T(8,128)(2,1)S(1)}, f32[4,1,768]{2,1,0:T(1,128)S(1)}) custom-call(s32[1]{0:T(128)} %bitcast.25.pos, bf16[4,96,256]{2,1,0:T(8,128)(2,1)S(1)} %copy-done.19, bf16[4,96,256]{2,1,0:T(8,128)(2,1)} %collective-permute-done.2.refs_1_, bf16[4,96,256]{2,1,0:T(8,128)(2,1)} %collective-permute-done.3.refs_2_, ...), custom_call_target="tpu_custom_call" | custom-call | flops 5765000192 | bytes 1 | tf_op jit(solution)/shard_map/pack_first/pallas_call | solution.py:338
  57.5 1.2 pack_points.24
  58.7 1.1 pack_points.26.refs_1_
  59.8 0.0 collective-permute-done.7.refs_4_
  59.8 3.0 %collective-permute-start.9 = (bf16[3,192,128]{2,1,0:T(8,128)(2,1)S(1)}, bf16[3,192,128]{2,1,0:T(8,128)(2,1)S(1)}, u32[]{:S(2)}, u32[]{:S(2)}) collective-permute-start(bf16[3,192,128]{2,1,0:T(8,128)(2,1)S(1)} %get-tuple-element.136), channel_id=1, source_target_pairs={{0,2},{1,3},{2,0},{3,1},{4,6},{5,7},{6,4},{7,5},{8,10},{9,11},{10,... | collective-permute-start | bytes 442376 | tf_op jit(solution)/shard_map/ppermute | solution.py:498
  62.8 0.0 collective-permute-done.5.refs_2_
  62.8 0.1 collective-permute-start.10
  62.8 1.4 %collective-permute-done.14.refs_7_ = bf16[3,192,128]{2,1,0:T(8,128)(2,1)S(1)} collective-permute-done((bf16[3,192,128]{2,1,0:T(8,128)(2,1)S(1)}, bf16[3,192,128]{2,1,0:T(8,128)(2,1)S(1)}, u32[]{:S(2)}, u32[]{:S(2)}) %collective-permute-start.14) | collective-permute-done | bytes 147488 | tf_op jit(solution)/shard_map/ppermute | solution.py:498
  64.2 0.1 broadcast_in_dim.14.refs_11_
  64.3 9.1 %source_terms.5 = (bf16[2,3,192,128]{3,2,1,0:T(8,128)(2,1)S(1)}, bf16[2,3,192,128]{3,2,1,0:T(8,128)(2,1)S(1)}, bf16[2,3,192,128]{3,2,1,0:T(8,128)(2,1)S(1)}, bf16[2,3,192,128]{3,2,1,0:T(8,128)(2,1)S(1)}) custom-call(s32[1]{0:T(128)} %bitcast.25.pos, bf16[6,384,128]{2,1,0:T(8,128)(2,1)S(1)} %get-tuple-element.128.refs_0_, ...), custom_call_target="tpu_custom_call" | custom-call | flops 3623878656 | bytes 1 | tf_op jit(solution)/shard_map/source_terms/pallas_call | solution.py:401
  73.4 4.5 %collective-permute-start.16 = (bf16[2,3,192,128]{3,2,1,0:T(8,128)(2,1)S(1)}, bf16[2,3,192,128]{3,2,1,0:T(8,128)(2,1)S(1)}, u32[]{:S(2)}, u32[]{:S(2)}) collective-permute-start(bf16[2,3,192,128]{3,2,1,0:T(8,128)(2,1)S(1)} %get-tuple-element.148), channel_id=1, source_target_pairs={{0,1},{1,0},{2,3},{3,2},{4,5},{5,4},{6,7},{7,6},{8,9},{9,8},{10,11... | collective-permute-start | bytes 884744 | tf_op jit(solution)/shard_map/ppermute | solution.py:498
  77.9 1.5 %collective-permute-start.18 = (bf16[2,3,192,128]{3,2,1,0:T(8,128)(2,1)S(1)}, bf16[2,3,192,128]{3,2,1,0:T(8,128)(2,1)S(1)}, u32[]{:S(2)}, u32[]{:S(2)}) collective-permute-start(bf16[2,3,192,128]{3,2,1,0:T(8,128)(2,1)S(1)} %get-tuple-element.150), channel_id=1, source_target_pairs={{0,3},{1,2},{2,1},{3,0},{4,7},{5,6},{6,5},{7,4},{8,11},{9,10},{10,... | collective-permute-start | bytes 884744 | tf_op jit(solution)/shard_map/ppermute | solution.py:498
  79.5 2.6 %collective-permute-done.10.refs_8_ = bf16[3,192,128]{2,1,0:T(8,128)(2,1)S(1)} collective-permute-done((bf16[3,192,128]{2,1,0:T(8,128)(2,1)S(1)}, bf16[3,192,128]{2,1,0:T(8,128)(2,1)S(1)}, u32[]{:S(2)}, u32[]{:S(2)}) %collective-permute-start.10) | collective-permute-done | bytes 147488 | tf_op jit(solution)/shard_map/ppermute | solution.py:498
  82.1 9.8 %source_terms.4 = (bf16[2,3,192,128]{3,2,1,0:T(8,128)(2,1)S(1)}, bf16[2,3,192,128]{3,2,1,0:T(8,128)(2,1)}, bf16[2,3,192,128]{3,2,1,0:T(8,128)(2,1)}, bf16[2,3,192,128]{3,2,1,0:T(8,128)(2,1)S(1)}) custom-call(s32[1]{0:T(128)} %bitcast.25.pos, bf16[6,384,128]{2,1,0:T(8,128)(2,1)S(1)} %get-tuple-element.128.refs_0_, ...), custom_call_target="tpu_custom_call" | custom-call | flops 3623878656 | bytes 1 | tf_op jit(solution)/shard_map/source_terms/pallas_call | solution.py:401
  91.9 0.1 collective-permute-start.11
  92.0 1.2 collective-permute-start.13
  93.2 2.2 %collective-permute-start.12 = (bf16[2,3,192,128]{3,2,1,0:T(8,128)(2,1)S(1)}, bf16[2,3,192,128]{3,2,1,0:T(8,128)(2,1)S(1)}, u32[]{:S(2)}, u32[]{:S(2)}) collective-permute-start(bf16[2,3,192,128]{3,2,1,0:T(8,128)(2,1)S(1)} %get-tuple-element.143), channel_id=1, source_target_pairs={{0,3},{1,2},{2,1},{3,0},{4,7},{5,6},{6,5},{7,4},{8,11},{9,10},{10,... | collective-permute-start | bytes 884744 | tf_op jit(solution)/shard_map/ppermute | solution.py:498
  95.4 1.2 slice.39
  96.6 8.3 %pmax.7 = s32[]{:T(128)} all-reduce(s32[]{:T(128)} %bitcast.28), channel_id=1, replica_groups=mesh['tile'=8,'comp'=4] {'tile'}, use_global_device_ids=true, to_apply=%region_0.1 | all-reduce | flops 1 | bytes 8 | tf_op jit(solution)/shard_map/pmax | solution.py:580
  105.5 2.2 %conditional.1 = (bf16[2,2,192,128]{3,2,1,0:T(8,128)(2,1)}, bf16[2,2,192,128]{3,2,1,0:T(8,128)(2,1)}, bf16[2,2,192,128]{3,2,1,0:T(8,128)(2,1)}, bf16[2,2,192,128]{3,2,1,0:T(8,128)(2,1)S(1)}) conditional(s32[]{:T(128)} %convert_element_type.6, () %tuple.25, (s32[1]{0:T(128)}, bf16[4,96,256]{2,1,0:T(8,128)(2,1)}, bf16[4,96,256]{2,1,0:T(8,128)(2,1)}, ...), branch_computations={%region_1.2_spmd, %region_2.3_spmd} | conditional | flops 8182984704 | bytes 15946042 | solution.py:582
  105.5 0.7 broadcast.29.clone.1
  106.2 0.7 broadcast.29.clone
  107.0 0.7 broadcast.29
  107.7 0.1 pad_add_fusion.scalars
  107.7 6.9 %collective-permute-done.18.refs_3_ = bf16[2,3,192,128]{3,2,1,0:T(8,128)(2,1)S(1)} collective-permute-done((bf16[2,3,192,128]{3,2,1,0:T(8,128)(2,1)S(1)}, bf16[2,3,192,128]{3,2,1,0:T(8,128)(2,1)S(1)}, u32[]{:S(2)}, u32[]{:S(2)}) %collective-permute-start.18) | collective-permute-done | bytes 294944 | tf_op jit(solution)/shard_map/ppermute | solution.py:498
  114.6 5.7 %unpack.3.refs_3_ = bf16[192,8,1024]{2,1,0:T(8,128)(2,1)} custom-call(s32[2]{0:T(128)S(1)} %pad_add_fusion.scalars, bf16[2,3,192,128]{3,2,1,0:T(8,128)(2,1)S(1)} %get-tuple-element.147.refs_0_, bf16[2,3,192,128]{3,2,1,0:T(8,128)(2,1)S(1)} %collective-permute-done.16.refs_1_, bf16[2,3,192,128]{3,2,1,0:T(8,128)(2,1)S(1)} %collective-permute-done.17.refs_2_, ...), custom_call_target="tpu_custom_call" | custom-call | flops 1 | bytes 1 | tf_op jit(solution)/shard_map/unpack/pallas_call | solution.py:478
  120.3 4.2 %unpack.4.refs_3_ = bf16[192,8,1024]{2,1,0:T(8,128)(2,1)} custom-call(s32[2]{0:T(128)S(1)} %pad_add_fusion.scalars, bf16[2,3,192,128]{3,2,1,0:T(8,128)(2,1)S(1)} %get-tuple-element.140.refs_0_, bf16[2,3,192,128]{3,2,1,0:T(8,128)(2,1)S(1)} %collective-permute-done.13.refs_1_, ...), custom_call_target="tpu_custom_call", output_to_operand_aliasing={{}: (4, {})} | custom-call | flops 1 | bytes 1 | tf_op jit(solution)/shard_map/unpack/pallas_call | solution.py:478
  124.5 2.2 %collective-permute-done.12.refs_1_ = bf16[2,3,192,128]{3,2,1,0:T(8,128)(2,1)S(1)} collective-permute-done((bf16[2,3,192,128]{3,2,1,0:T(8,128)(2,1)S(1)}, bf16[2,3,192,128]{3,2,1,0:T(8,128)(2,1)S(1)}, u32[]{:S(2)}, u32[]{:S(2)}) %collective-permute-start.12) | collective-permute-done | bytes 294944 | tf_op jit(solution)/shard_map/ppermute | solution.py:498
  126.7 4.2 %unpack.5 = bf16[192,8,1024]{2,1,0:T(8,128)(2,1)} custom-call(s32[2]{0:T(128)S(1)} %pad_add_fusion.scalars, bf16[2,3,192,128]{3,2,1,0:T(8,128)(2,1)S(1)} %collective-permute-done.11.refs_0_, bf16[2,3,192,128]{3,2,1,0:T(8,128)(2,1)S(1)} %collective-permute-done.12.refs_1_, ...), custom_call_target="tpu_custom_call", output_to_operand_aliasing={{}: (4, {})} | custom-call | flops 1 | bytes 1 | tf_op jit(solution)/shard_map/unpack/pallas_call | solution.py:478
  (45 shorter events, 0.1 us)
Async XLA Ops:
  0.0 6.9 %copy-start = (f32[16,32]{1,0:T(8,128)S(1)}, f32[16,32]{1,0:T(8,128)}, u32[]{:S(2)}) copy-start(f32[16,32]{1,0:T(8,128)} %param.14) | copy-start | bytes 6148
  0.0 7.0 %copy-start.17 = (f32[2,24]{1,0:T(2,128)S(1)}, f32[2,24]{1,0:T(2,128)}, u32[]{:S(2)}) copy-start(f32[2,24]{1,0:T(2,128)} %constant.34.clone) | copy-start | bytes 580
  0.0 7.1 %copy-start.1 = (bf16[192,8,1024]{2,1,0:T(8,128)(2,1)S(1)}, bf16[192,8,1024]{2,1,0:T(8,128)(2,1)}, u32[]{:S(2)}) copy-start(bf16[192,8,1024]{2,1,0:T(8,128)(2,1)} %refs_0_.5) | copy-start | bytes 9437188
  4.2 14.5 %copy-start.3 = (s32[8,1024]{1,0:T(8,128)S(1)}, s32[8,1024]{1,0:T(8,128)}, u32[]{:S(2)}) copy-start(s32[8,1024]{1,0:T(8,128)} %get-tuple-element.110.refs_1_.refs_3_) | copy-start | bytes 98308
  4.2 20.8 %collective-permute-start = (bf16[49,8,1024]{2,1,0:T(8,128)(2,1)}, bf16[49,8,1024]{2,1,0:T(8,128)(2,1)}, u32[]{:S(2)}, u32[]{:S(2)}) collective-permute-start(bf16[49,8,1024]{2,1,0:T(8,128)(2,1)} %get-tuple-element.114), channel_id=1, source_target_pairs={{0,4},{4,8},{8,12},{12,16},{16,20},{20,24},{24,28},{28,0},{1,5},{5... | collective-permute-start | bytes 2408456 | tf_op jit(solution)/shard_map/ppermute | solution.py:531
  4.2 25.5 %collective-permute-start.1 = (bf16[49,8,1024]{2,1,0:T(8,128)(2,1)}, bf16[49,8,1024]{2,1,0:T(8,128)(2,1)}, u32[]{:S(2)}, u32[]{:S(2)}) collective-permute-start(bf16[49,8,1024]{2,1,0:T(8,128)(2,1)} %get-tuple-element.115), channel_id=1, source_target_pairs={{4,0},{8,4},{12,8},{16,12},{20,16},{24,20},{28,24},{0,28},{5,1},{9... | collective-permute-start | bytes 2408456 | tf_op jit(solution)/shard_map/ppermute | solution.py:531
  7.1 0.8 copy-start.2
  15.2 32.8 %collective-permute-start.2 = (bf16[4,96,256]{2,1,0:T(8,128)(2,1)}, bf16[4,96,256]{2,1,0:T(8,128)(2,1)}, u32[]{:S(2)}, u32[]{:S(2)}) collective-permute-start(bf16[4,96,256]{2,1,0:T(8,128)(2,1)} %get-tuple-element.121), channel_id=1, source_target_pairs={{0,1},{1,0},{2,3},{3,2},{4,5},{5,4},{6,7},{7,6},{8,9},{9,8},{10,11... | collective-permute-start | bytes 589832 | tf_op jit(solution)/shard_map/ppermute | solution.py:498
  15.2 33.4 %collective-permute-start.3 = (bf16[4,96,256]{2,1,0:T(8,128)(2,1)}, bf16[4,96,256]{2,1,0:T(8,128)(2,1)}, u32[]{:S(2)}, u32[]{:S(2)}) collective-permute-start(bf16[4,96,256]{2,1,0:T(8,128)(2,1)} %get-tuple-element.122), channel_id=1, source_target_pairs={{0,2},{1,3},{2,0},{3,1},{4,6},{5,7},{6,4},{7,5},{8,10},{9,11},{10,... | collective-permute-start | bytes 589832 | tf_op jit(solution)/shard_map/ppermute | solution.py:498
  18.2 32.5 %collective-permute-start.4 = (bf16[4,96,256]{2,1,0:T(8,128)(2,1)}, bf16[4,96,256]{2,1,0:T(8,128)(2,1)}, u32[]{:S(2)}, u32[]{:S(2)}) collective-permute-start(bf16[4,96,256]{2,1,0:T(8,128)(2,1)} %get-tuple-element.123), channel_id=1, source_target_pairs={{0,3},{1,2},{2,1},{3,0},{4,7},{5,6},{6,5},{7,4},{8,11},{9,10},{10,... | collective-permute-start | bytes 589832 | tf_op jit(solution)/shard_map/ppermute | solution.py:498
  23.9 4.7 %copy-start.12 = (bf16[4,96,256]{2,1,0:T(8,128)(2,1)}, bf16[4,96,256]{2,1,0:T(8,128)(2,1)S(1)}, u32[]{:S(2)}) copy-start(bf16[4,96,256]{2,1,0:T(8,128)(2,1)S(1)} %get-tuple-element.132.piece) | copy-start | bytes 589828
  23.9 4.7 %copy-start.13 = (bf16[4,96,256]{2,1,0:T(8,128)(2,1)}, bf16[4,96,256]{2,1,0:T(8,128)(2,1)S(1)}, u32[]{:S(2)}) copy-start(bf16[4,96,256]{2,1,0:T(8,128)(2,1)S(1)} %get-tuple-element.133.piece) | copy-start | bytes 589828
  25.0 21.4 %collective-permute-start.6 = (bf16[6,96,128]{2,1,0:T(8,128)(2,1)S(1)}, bf16[6,96,128]{2,1,0:T(8,128)(2,1)}, u32[]{:S(2)}, u32[]{:S(2)}) collective-permute-start(bf16[6,96,128]{2,1,0:T(8,128)(2,1)S(1)} %pack_points.28), channel_id=1, source_target_pairs={{0,2},{1,3},{2,0},{3,1},{4,6},{5,7},{6,4},{7,5},{8,10},{9,11},{10,... | collective-permute-start | bytes 442376 | tf_op jit(solution)/shard_map/ppermute | solution.py:498
  29.7 11.2 %copy-start.11 = (bf16[4,96,256]{2,1,0:T(8,128)(2,1)S(1)}, bf16[4,96,256]{2,1,0:T(8,128)(2,1)}, u32[]{:S(2)}) copy-start(bf16[4,96,256]{2,1,0:T(8,128)(2,1)} %get-tuple-element.131.piece) | copy-start | bytes 589828
  29.7 21.9 %copy-start.19 = (bf16[4,96,256]{2,1,0:T(8,128)(2,1)S(1)}, bf16[4,96,256]{2,1,0:T(8,128)(2,1)}, u32[]{:S(2)}) copy-start(bf16[4,96,256]{2,1,0:T(8,128)(2,1)} %get-tuple-element.111.refs_0_) | copy-start | bytes 589828
  29.7 30.1 %collective-permute-start.7 = (bf16[6,96,128]{2,1,0:T(8,128)(2,1)S(1)}, bf16[6,96,128]{2,1,0:T(8,128)(2,1)S(1)}, u32[]{:S(2)}, u32[]{:S(2)}) collective-permute-start(bf16[6,96,128]{2,1,0:T(8,128)(2,1)S(1)} %pack_points.29), channel_id=1, source_target_pairs={{0,3},{1,2},{2,1},{3,0},{4,7},{5,6},{6,5},{7,4},{8,11},{9,10},{10,... | collective-permute-start | bytes 442376 | tf_op jit(solution)/shard_map/ppermute | solution.py:498
  40.9 5.6 %copy-start.8 = (bf16[4,192,256]{2,1,0:T(8,128)(2,1)}, bf16[4,192,256]{2,1,0:T(8,128)(2,1)S(1)}, u32[]{:S(2)}) copy-start(bf16[4,192,256]{2,1,0:T(8,128)(2,1)S(1)} %get-tuple-element.135.piece) | copy-start | bytes 1179652
  40.9 9.8 %copy-start.9 = (bf16[4,192,256]{2,1,0:T(8,128)(2,1)}, bf16[4,192,256]{2,1,0:T(8,128)(2,1)S(1)}, u32[]{:S(2)}) copy-start(bf16[4,192,256]{2,1,0:T(8,128)(2,1)S(1)} %get-tuple-element.137.piece) | copy-start | bytes 1179652
  40.9 9.8 %copy-start.7 = (bf16[4,192,256]{2,1,0:T(8,128)(2,1)}, bf16[4,192,256]{2,1,0:T(8,128)(2,1)S(1)}, u32[]{:S(2)}) copy-start(bf16[4,192,256]{2,1,0:T(8,128)(2,1)S(1)} %get-tuple-element.125.piece) | copy-start | bytes 1179652
  40.9 16.5 %copy-start.6 = (bf16[4,192,256]{2,1,0:T(8,128)(2,1)}, bf16[4,192,256]{2,1,0:T(8,128)(2,1)S(1)}, u32[]{:S(2)}) copy-start(bf16[4,192,256]{2,1,0:T(8,128)(2,1)S(1)} %get-tuple-element.116.piece) | copy-start | bytes 1179652
  46.5 11.0 %copy-start.14 = (f32[8,1,256]{2,1,0:T(1,128)}, f32[8,1,256]{2,1,0:T(1,128)S(1)}, u32[]{:S(2)}) copy-start(f32[8,1,256]{2,1,0:T(1,128)S(1)} %broadcast_in_dim.13.refs_6_) | copy-start | bytes 24580
  46.5 17.7 %collective-permute-start.8 = (bf16[6,192,128]{2,1,0:T(8,128)(2,1)S(1)}, bf16[6,192,128]{2,1,0:T(8,128)(2,1)S(1)}, u32[]{:S(2)}, u32[]{:S(2)}) collective-permute-start(bf16[6,192,128]{2,1,0:T(8,128)(2,1)S(1)} %pack_points.25), channel_id=1, source_target_pairs={{0,1},{1,0},{2,3},{3,2},{4,5},{5,4},{6,7},{7,6},{8,9},{9,8},{10,11... | collective-permute-start | bytes 884744 | tf_op jit(solution)/shard_map/ppermute | solution.py:498
  48.0 14.8 %collective-permute-start.5 = (bf16[6,96,128]{2,1,0:T(8,128)(2,1)S(1)}, bf16[6,96,128]{2,1,0:T(8,128)(2,1)S(1)}, u32[]{:S(2)}, u32[]{:S(2)}) collective-permute-start(bf16[6,96,128]{2,1,0:T(8,128)(2,1)S(1)} %pack_points.27), channel_id=1, source_target_pairs={{0,1},{1,0},{2,3},{3,2},{4,5},{5,4},{6,7},{7,6},{8,9},{9,8},{10,11... | collective-permute-start | bytes 442376 | tf_op jit(solution)/shard_map/ppermute | solution.py:498
  48.6 15.6 %collective-permute-start.14 = (bf16[3,192,128]{2,1,0:T(8,128)(2,1)S(1)}, bf16[3,192,128]{2,1,0:T(8,128)(2,1)S(1)}, u32[]{:S(2)}, u32[]{:S(2)}) collective-permute-start(bf16[3,192,128]{2,1,0:T(8,128)(2,1)S(1)} %get-tuple-element.145), channel_id=1, source_target_pairs={{0,2},{1,3},{2,0},{3,1},{4,6},{5,7},{6,4},{7,5},{8,10},{9,11},{10,... | collective-permute-start | bytes 442376 | tf_op jit(solution)/shard_map/ppermute | solution.py:498
  50.7 8.0 %copy-start.10 = (bf16[4,96,256]{2,1,0:T(8,128)(2,1)S(1)}, bf16[4,96,256]{2,1,0:T(8,128)(2,1)}, u32[]{:S(2)}) copy-start(bf16[4,96,256]{2,1,0:T(8,128)(2,1)} %get-tuple-element.129.piece) | copy-start | bytes 589828
  50.7 13.5 %copy-start.16 = (f32[2,24]{1,0:T(2,128)S(1)}, f32[2,24]{1,0:T(2,128)}, u32[]{:S(2)}) copy-start(f32[2,24]{1,0:T(2,128)} %constant.35.clone) | copy-start | bytes 580
  50.7 13.5 %copy-start.18 = (bf16[768,768]{1,0:T(8,128)(2,1)S(1)}, bf16[768,768]{1,0:T(8,128)(2,1)}, u32[]{:S(2)}) copy-start(bf16[768,768]{1,0:T(8,128)(2,1)} %refs_10_.3) | copy-start | bytes 3538948
  50.7 13.5 %collective-permute-start.15 = (bf16[3,192,128]{2,1,0:T(8,128)(2,1)S(1)}, bf16[3,192,128]{2,1,0:T(8,128)(2,1)S(1)}, u32[]{:S(2)}, u32[]{:S(2)}) collective-permute-start(bf16[3,192,128]{2,1,0:T(8,128)(2,1)S(1)} %get-tuple-element.146), channel_id=1, source_target_pairs={{0,3},{1,2},{2,1},{3,0},{4,7},{5,6},{6,5},{7,4},{8,11},{9,10},{10,... | collective-permute-start | bytes 442376 | tf_op jit(solution)/shard_map/ppermute | solution.py:498
  59.8 19.7 %collective-permute-start.9 = (bf16[3,192,128]{2,1,0:T(8,128)(2,1)S(1)}, bf16[3,192,128]{2,1,0:T(8,128)(2,1)S(1)}, u32[]{:S(2)}, u32[]{:S(2)}) collective-permute-start(bf16[3,192,128]{2,1,0:T(8,128)(2,1)S(1)} %get-tuple-element.136), channel_id=1, source_target_pairs={{0,2},{1,3},{2,0},{3,1},{4,6},{5,7},{6,4},{7,5},{8,10},{9,11},{10,... | collective-permute-start | bytes 442376 | tf_op jit(solution)/shard_map/ppermute | solution.py:498
  62.8 19.3 %collective-permute-start.10 = (bf16[3,192,128]{2,1,0:T(8,128)(2,1)S(1)}, bf16[3,192,128]{2,1,0:T(8,128)(2,1)S(1)}, u32[]{:S(2)}, u32[]{:S(2)}) collective-permute-start(bf16[3,192,128]{2,1,0:T(8,128)(2,1)S(1)} %get-tuple-element.138), channel_id=1, source_target_pairs={{0,3},{1,2},{2,1},{3,0},{4,7},{5,6},{6,5},{7,4},{8,11},{9,10},{10,... | collective-permute-start | bytes 442376 | tf_op jit(solution)/shard_map/ppermute | solution.py:498
  73.4 19.8 %collective-permute-start.16 = (bf16[2,3,192,128]{3,2,1,0:T(8,128)(2,1)S(1)}, bf16[2,3,192,128]{3,2,1,0:T(8,128)(2,1)S(1)}, u32[]{:S(2)}, u32[]{:S(2)}) collective-permute-start(bf16[2,3,192,128]{3,2,1,0:T(8,128)(2,1)S(1)} %get-tuple-element.148), channel_id=1, source_target_pairs={{0,1},{1,0},{2,3},{3,2},{4,5},{5,4},{6,7},{7,6},{8,9},{9,8},{10,11... | collective-permute-start | bytes 884744 | tf_op jit(solution)/shard_map/ppermute | solution.py:498
  77.9 29.8 %collective-permute-start.17 = (bf16[2,3,192,128]{3,2,1,0:T(8,128)(2,1)S(1)}, bf16[2,3,192,128]{3,2,1,0:T(8,128)(2,1)S(1)}, u32[]{:S(2)}, u32[]{:S(2)}) collective-permute-start(bf16[2,3,192,128]{3,2,1,0:T(8,128)(2,1)S(1)} %get-tuple-element.149), channel_id=1, source_target_pairs={{0,2},{1,3},{2,0},{3,1},{4,6},{5,7},{6,4},{7,5},{8,10},{9,11},{10,... | collective-permute-start | bytes 884744 | tf_op jit(solution)/shard_map/ppermute | solution.py:498
  77.9 36.7 %collective-permute-start.18 = (bf16[2,3,192,128]{3,2,1,0:T(8,128)(2,1)S(1)}, bf16[2,3,192,128]{3,2,1,0:T(8,128)(2,1)S(1)}, u32[]{:S(2)}, u32[]{:S(2)}) collective-permute-start(bf16[2,3,192,128]{3,2,1,0:T(8,128)(2,1)S(1)} %get-tuple-element.150), channel_id=1, source_target_pairs={{0,3},{1,2},{2,1},{3,0},{4,7},{5,6},{6,5},{7,4},{8,11},{9,10},{10,... | collective-permute-start | bytes 884744 | tf_op jit(solution)/shard_map/ppermute | solution.py:498
  82.1 23.4 %copy-start.15 = (f32[8,1,256]{2,1,0:T(1,128)S(1)}, f32[8,1,256]{2,1,0:T(1,128)}, u32[]{:S(2)}) copy-start(f32[8,1,256]{2,1,0:T(1,128)} %copy-done.14) | copy-start | bytes 24580
  91.9 32.6 %collective-permute-start.11 = (bf16[2,3,192,128]{3,2,1,0:T(8,128)(2,1)}, bf16[2,3,192,128]{3,2,1,0:T(8,128)(2,1)S(1)}, u32[]{:S(2)}, u32[]{:S(2)}) collective-permute-start(bf16[2,3,192,128]{3,2,1,0:T(8,128)(2,1)} %get-tuple-element.142), channel_id=1, source_target_pairs={{0,2},{1,3},{2,0},{3,1},{4,6},{5,7},{6,4},{7,5},{8,10},{9,11},{10,... | collective-permute-start | bytes 884744 | tf_op jit(solution)/shard_map/ppermute | solution.py:498
  92.0 28.4 %collective-permute-start.13 = (bf16[2,3,192,128]{3,2,1,0:T(8,128)(2,1)}, bf16[2,3,192,128]{3,2,1,0:T(8,128)(2,1)S(1)}, u32[]{:S(2)}, u32[]{:S(2)}) collective-permute-start(bf16[2,3,192,128]{3,2,1,0:T(8,128)(2,1)} %get-tuple-element.144), channel_id=1, source_target_pairs={{0,1},{1,0},{2,3},{3,2},{4,5},{5,4},{6,7},{7,6},{8,9},{9,8},{10,11... | collective-permute-start | bytes 884744 | tf_op jit(solution)/shard_map/ppermute | solution.py:498
  93.2 33.5 %collective-permute-start.12 = (bf16[2,3,192,128]{3,2,1,0:T(8,128)(2,1)S(1)}, bf16[2,3,192,128]{3,2,1,0:T(8,128)(2,1)S(1)}, u32[]{:S(2)}, u32[]{:S(2)}) collective-permute-start(bf16[2,3,192,128]{3,2,1,0:T(8,128)(2,1)S(1)} %get-tuple-element.143), channel_id=1, source_target_pairs={{0,3},{1,2},{2,1},{3,0},{4,7},{5,6},{6,5},{7,4},{8,11},{9,10},{10,... | collective-permute-start | bytes 884744 | tf_op jit(solution)/shard_map/ppermute | solution.py:498

commit v5 on v4

--- a/solution.py
+++ b/solution.py
@@ -301,7 +301,7 @@
 
 
 def pack_first_kernel(first_block, count, pos, *refs):
-    pieces, (ranks, wind_c, wind_s, packed, wind) = refs[:-5], refs[-5:]
+    pieces, (ranks, wind_speed, wind_dir, packed, wind) = refs[:-5], refs[-5:]
     z = pos[0]
     blocks, total, _ = packed.shape
     comps = total // count
@@ -314,10 +314,14 @@
         both = jnp.where(mask, high, low).astype(jnp.bfloat16)
         for j in range(blocks):
             packed[j, pl.ds(at, comps), :] = both[:, j * LANES : (j + 1) * LANES]
+    width = ranks.shape[3] // 4
+    here = pl.ds(pl.multiple_of(z * width, LANES), width)
+    speed, direction = 0.002 * wind_speed[:, here], wind_dir[:, here]
+    winds = speed * jnp.cos(direction), speed * jnp.sin(direction)
     for g in range(2):
         parts = []
-        for source in (wind_c, wind_s):
-            left = jnp.concatenate([source[4 + i if g else 3 - i] for i in range(4)], axis=1)
+        for source in winds:
+            left = jnp.concatenate([source[x : x + 1] for x in (range(4, 8) if g else range(3, -1, -1))], axis=1)
             for _ in range(3):
                 part = left.astype(jnp.bfloat16).astype(jnp.float32)
                 parts.append(part)
@@ -328,7 +332,7 @@
             wind[2 * g + n] = row[3 * n : 3 * n + 1] + row[3 * n + 1 : 3 * n + 2] + row[3 * n + 2 : 3 * n + 3]
 
 
-def pack_first(z, pieces, ranks, wind_c, wind_s, count, first_block, blocks):
+def pack_first(z, pieces, ranks, wind_speed, wind_dir, count, first_block, blocks):
     total = sum(piece.shape[1] for piece in pieces)
     whole = lambda a: pl.BlockSpec(a.shape, lambda i, z: (0,) * a.ndim)
     outs = [
@@ -341,14 +345,14 @@
             num_scalar_prefetch=1,
             grid=(1,),
             in_specs=[whole(piece) for piece in pieces]
-            + [pl.BlockSpec((1,) + ranks.shape[1:], lambda i, z: (z[0], 0, 0, 0)), whole(wind_c), whole(wind_s)],
+            + [pl.BlockSpec((1,) + ranks.shape[1:], lambda i, z: (z[0], 0, 0, 0)), whole(wind_speed), whole(wind_dir)],
             out_specs=[whole(out) for out in outs],
         ),
         out_shape=outs,
         compiler_params=pltpu.CompilerParams(vmem_limit_bytes=VMEM_LIMIT),
         cost_estimate=pl.CostEstimate(flops=int(5.0e6 * 1153), bytes_accessed=1, transcendentals=0),
         name="pack_first",
-    )(z, *pieces, ranks, wind_c, wind_s)
+    )(z, *pieces, ranks, wind_speed, wind_dir)
 
 
 def sources_kernel(count, pos, *refs):
@@ -525,7 +529,6 @@
     table = jnp.pad(table, ((0, 0), (0, LANES - table.shape[1])))[:, None]
     trig = jnp.broadcast_to(jnp.asarray(np.stack([np.abs(COS), np.abs(SIN)]))[:, :, None], (2, K, LANES))
     signed = jnp.broadcast_to(jnp.asarray(np.stack([COS, SIN]))[:, :, None], (2, K, LANES))
-    start = place * width
 
     to_east, to_west, code = pack_halo(spectrum, sea_mask, depth_class)
     halo = lax.ppermute(to_east, "tile", east), lax.ppermute(to_west, "tile", west)
@@ -551,16 +554,13 @@
     packed_later[1] = send(pack_later(1, later[1]), 1, count)
     packed = [pack_points(z, s, second[s], ranks, False, 0, [main] if s == 1 else [size] * chunks) for s in range(count)]
     near = send(packed[1][0], 1, count)
-    own, speed, direction, _ = lax.optimization_barrier((later[0], wind_speed, wind_dir, packed[1][0]))
-    speed_part = 0.002 * lax.dynamic_slice_in_dim(speed, start, width, 1)
-    dir_part = lax.dynamic_slice_in_dim(direction, start, width, 1)
-    wind_c, wind_s = (speed_part * jnp.cos(dir_part))[:, None], (speed_part * jnp.sin(dir_part))[:, None]
+    own, _ = lax.optimization_barrier((later[0], packed[1][0]))
     packed_later = [pack_later(0, own)] + [packed_later[s] for s in range(1, count)]
-    packed_first, winds = pack_first(z, first, ranks, wind_c, wind_s, count, 0, main)
-
-    def remainder(first, later, second, ranks, wind_c, wind_s, coupling):
+    packed_first, winds = pack_first(z, first, ranks, wind_speed, wind_dir, count, 0, main)
+
+    def remainder(first, later, second, ranks, wind_speed, wind_dir, coupling):
         rest = blocks - main
-        down, winds = pack_first(z, first, ranks, wind_c, wind_s, count, main, rest)
+        down, winds = pack_first(z, first, ranks, wind_speed, wind_dir, count, main, rest)
         low = [pack_points(z, s, later[s], ranks, True, main, [rest])[0] for s in range(count)]
         high = [pack_points(z, s, second[s], ranks, False, main, [rest])[0] for s in range(count)]
         low, high = exchange_rare(low, "comp"), exchange_rare(high, "comp")
@@ -579,7 +579,7 @@
             most, _ = lax.optimization_barrier((most, arrived[0]))
             full = lax.pmax(most[0, 0], "tile") > main * LANES
     full, _ = lax.optimization_barrier((full, sent[0]))
-    rest = lax.cond(full, remainder, nothing, first, later, second, ranks, wind_c, wind_s, coupling)
+    rest = lax.cond(full, remainder, nothing, first, later, second, ranks, wind_speed, wind_dir, coupling)
     scalars = jnp.concatenate([z, full.astype(jnp.int32).reshape(1)])
     everyone = list(range(count))
     out = unpack(scalars, everyone, updated[0], 0, rest, main, ranks, rows, None)

time: 132 us -> 132 us (level)
  Pallas kernels: 75.8 us -> 72.7 us
  waiting for transfers between devices: 13.1 us -> 15.3 us
  local copies, waits for them, and re-layouts: 4.49 us -> 6.52 us
    ppermute x17, waiting for transfers between devices: 13.1 us -> 15.3 us  [send(): return lax.ppermute(block, 'comp', [(i, i ^ s) for i in range(count)])]
    pallas_call x2, Pallas kernels: 18.9 us -> 17.5 us  [sources(): pl.pallas_call(functools.partial(sources_kernel, count), grid_spec=pltpu....]
    unnamed x37 -> x49, local copies, waits for them, and re-layouts: 0.91 us -> 2.27 us
  transfers between devices with their start and end apart: 19 -> 19, of which waited for: 4 -> 3; matrix products, arithmetic and copies ran while one was open for 3% -> 3% of each run, Pallas kernels for 52% -> 49%
where the time goes in v5:
time: 132 us; the launch traced here: 130 us
  Pallas kernels  72.7 us (55%)
  starting transfers between devices  26.8 us (20%)
  waiting for transfers between devices  15.3 us (12%)
  blocking collectives  8.01 us (6%)
  local copies, waits for them, and re-layouts  6.52 us (5%)
    ppermute x17, starting transfers between devices, send(): return lax.ppermute(block, 'comp', [(i, i ^ s) for i in range(count)])  24.2 us
    pallas_call x3, Pallas kernels, propagate(): pl.pallas_call(functools.partial(propagate_kernel, halo is not None, part...  21 us
    pallas_call x2, Pallas kernels, sources(): pl.pallas_call(functools.partial(sources_kernel, count), grid_spec=pltpu....  17.5 us
    ppermute x17, waiting for transfers between devices, send(): return lax.ppermute(block, 'comp', [(i, i ^ s) for i in range(count)])  15.3 us
    pallas_call x3, Pallas kernels, unpack(): pl.pallas_call(functools.partial(unpack_kernel, partners, first_block, re...  14.2 us
    pallas_call x8, Pallas kernels, pack_points(): pl.pallas_call(functools.partial(pack_points_kernel, downwind, first_bloc...  9.14 us
    pmax x1, blocking collectives, on_device(): full = lax.pmax(most[0, 0], 'tile') > main * LANES  8.01 us
    pallas_call x1, Pallas kernels, pack_first(): pl.pallas_call(functools.partial(pack_first_kernel, first_block, count),...  4.76 us
  transfers between devices with their start and end apart: 19, of which 3 were waited for; matrix products, arithmetic and copies ran while one was open for 3% of the time, Pallas kernels for 49%

profile of v5, /device:TPU:8, one launch (start us, length us, event | category | flops | bytes accessed | tf_op | source)
XLA Modules:
  0.0 130.5 jit_solution(15423304202704083654)
XLA Ops:
  0.0 4.2 %pack_halo.1 = (bf16[49,8,1024]{2,1,0:T(8,128)(2,1)}, bf16[49,8,1024]{2,1,0:T(8,128)(2,1)}, s32[8,1024]{1,0:T(8,128)}) custom-call(bf16[192,8,1024]{2,1,0:T(8,128)(2,1)} %refs_0_.5, s32[8,1024]{1,0:T(8,128)} %sea.2, s32[8,1024]{1,0:T(8,128)} %depth.1), custom_call_target="tpu_custom_call" | custom-call | tf_op jit(solution)/shard_map/pack_halo/pallas_call | solution.py:54
  4.2 0.0 collective-permute-start
  4.2 2.6 %collective-permute-start.1 = (bf16[49,8,1024]{2,1,0:T(8,128)(2,1)}, bf16[49,8,1024]{2,1,0:T(8,128)(2,1)}, u32[]{:S(2)}, u32[]{:S(2)}) collective-permute-start(bf16[49,8,1024]{2,1,0:T(8,128)(2,1)} %get-tuple-element.113), channel_id=1, source_target_pairs={{4,0},{8,4},{12,8},{16,12},{20,16},{24,20},{28,24},{0,28},{5,1},{9... | collective-permute-start | bytes 2408456 | tf_op jit(solution)/shard_map/ppermute | solution.py:534
  6.9 0.1 constant_dynamic-slice_fusion
  6.9 0.1 copy.13
  7.0 0.1 broadcast_in_dim.7.refs_3_.refs_7_
  7.1 0.8 copy-done.2
  7.9 5.2 %propagate_downwind.2 = (bf16[4,96,256]{2,1,0:T(8,128)(2,1)}, bf16[4,96,256]{2,1,0:T(8,128)(2,1)S(1)}, bf16[4,96,256]{2,1,0:T(8,128)(2,1)S(1)}, bf16[4,96,256]{2,1,0:T(8,128)(2,1)S(1)}) custom-call(s32[1]{0:T(128)} %bitcast.25.pos, bf16[192,8,1024]{2,1,0:T(8,128)(2,1)S(1)} %copy-done.1, s32[8,1024]{1,0:T(8,128)S(1)} %copy-done.2, f32[8,1,128]{2,1,0:T(1,128)S(1)} %bitcast.55, ...), custom_call_target="tpu_custom_call" | custom-call | flops 23592960 | bytes 4718592 | tf_op jit(solution)/shard_map/propagate_downwind/pallas_call | solution.py:200
  13.1 0.7 copy-done.4
  13.7 0.7 copy-done.5
  14.4 2.0 %sea_ranks.1 = (s32[4,2,1,1024]{3,2,1,0:T(1,128)S(1)}, s32[8,128]{1,0:T(8,128)}) custom-call(s32[8,1024]{1,0:T(8,128)} %sea.2), custom_call_target="tpu_custom_call" | custom-call | flops 1 | bytes 1 | tf_op jit(solution)/shard_map/sea_ranks/pallas_call | solution.py:243
  16.4 3.0 %collective-permute-start.3 = (bf16[4,96,256]{2,1,0:T(8,128)(2,1)}, bf16[4,96,256]{2,1,0:T(8,128)(2,1)S(1)}, u32[]{:S(2)}, u32[]{:S(2)}) collective-permute-start(bf16[4,96,256]{2,1,0:T(8,128)(2,1)} %copy-done.4), channel_id=1, source_target_pairs={{0,2},{1,3},{2,0},{3,1},{4,6},{5,7},{6,4},{7,5},{8,10},{9,11},{10,... | collective-permute-start | bytes 589832 | tf_op jit(solution)/shard_map/ppermute | solution.py:502
  19.4 0.5 collective-permute-start.4
  19.9 4.6 %propagate_downwind.3 = (bf16[4,96,256]{2,1,0:T(8,128)(2,1)S(1)}, bf16[4,96,256]{2,1,0:T(8,128)(2,1)S(1)}, bf16[4,96,256]{2,1,0:T(8,128)(2,1)S(1)}, bf16[4,96,256]{2,1,0:T(8,128)(2,1)S(1)}) custom-call(s32[1]{0:T(128)} %bitcast.25.pos, bf16[192,8,1024]{2,1,0:T(8,128)(2,1)S(1)} %copy-done.1, s32[8,1024]{1,0:T(8,128)S(1)} %copy-done.3, ...), custom_call_target="tpu_custom_call" | custom-call | flops 23592960 | bytes 4718592 | tf_op jit(solution)/shard_map/propagate_downwind/pallas_call | solution.py:200
  24.5 1.1 pack_points.28
  25.6 0.0 collective-permute-done.refs_1_.refs_4_
  25.7 3.5 %collective-permute-start.6 = (bf16[6,96,128]{2,1,0:T(8,128)(2,1)S(1)}, bf16[6,96,128]{2,1,0:T(8,128)(2,1)S(1)}, u32[]{:S(2)}, u32[]{:S(2)}) collective-permute-start(bf16[6,96,128]{2,1,0:T(8,128)(2,1)S(1)} %pack_points.28), channel_id=1, source_target_pairs={{0,2},{1,3},{2,0},{3,1},{4,6},{5,7},{6,4},{7,5},{8,10},{9,11},{10,... | collective-permute-start | bytes 442376 | tf_op jit(solution)/shard_map/ppermute | solution.py:502
  29.2 1.1 pack_points.29
  30.3 0.0 copy-start.24
  30.3 0.0 copy-start.25
  30.4 0.0 collective-permute-done.1.refs_2_.refs_5_
  30.4 0.1 collective-permute-start.7
  30.4 11.2 %propagate_upwind.1 = (bf16[4,192,256]{2,1,0:T(8,128)(2,1)S(1)}, bf16[4,192,256]{2,1,0:T(8,128)(2,1)S(1)}, bf16[4,192,256]{2,1,0:T(8,128)(2,1)S(1)}, bf16[4,192,256]{2,1,0:T(8,128)(2,1)S(1)}) custom-call(s32[1]{0:T(128)} %bitcast.25.pos, bf16[192,8,1024]{2,1,0:T(8,128)(2,1)S(1)} %copy-done.1, bf16[49,8,1024]{2,1,0:T(8,128)(2,1)} %collective-permute-done.refs_1_.refs_4_, ...), custom_call_target="tpu_custom_call" | custom-call | flops 47185920 | bytes 9437184 | tf_op jit(solution)/shard_map/propagate_upwind/pallas_call | solution.py:200
  41.7 1.1 pack_points.27
  42.8 1.2 pack_points.25
  44.0 1.2 pack_points.30
  45.2 1.2 pack_points.31
  46.4 0.0 collective-permute-done.6.refs_3_
  46.4 2.4 %collective-permute-start.5 = (bf16[6,96,128]{2,1,0:T(8,128)(2,1)S(1)}, bf16[6,96,128]{2,1,0:T(8,128)(2,1)S(1)}, u32[]{:S(2)}, u32[]{:S(2)}) collective-permute-start(bf16[6,96,128]{2,1,0:T(8,128)(2,1)S(1)} %pack_points.27), channel_id=1, source_target_pairs={{0,1},{1,0},{2,3},{3,2},{4,5},{5,4},{6,7},{7,6},{8,9},{9,8},{10,11... | collective-permute-start | bytes 442376 | tf_op jit(solution)/shard_map/ppermute | solution.py:502
  48.8 0.0 collective-permute-done.2.refs_1_
  48.8 1.1 collective-permute-start.14
  49.9 0.0 collective-permute-done.3.refs_2_
  50.0 0.6 collective-permute-start.15
  50.6 2.8 %collective-permute-start.8 = (bf16[6,192,128]{2,1,0:T(8,128)(2,1)S(1)}, bf16[6,192,128]{2,1,0:T(8,128)(2,1)S(1)}, u32[]{:S(2)}, u32[]{:S(2)}) collective-permute-start(bf16[6,192,128]{2,1,0:T(8,128)(2,1)S(1)} %pack_points.25), channel_id=1, source_target_pairs={{0,1},{1,0},{2,3},{3,2},{4,5},{5,4},{6,7},{7,6},{8,9},{9,8},{10,11... | collective-permute-start | bytes 884744 | tf_op jit(solution)/shard_map/ppermute | solution.py:502
  53.3 4.8 %pack_first.3 = (bf16[6,384,128]{2,1,0:T(8,128)(2,1)S(1)}, f32[4,1,768]{2,1,0:T(1,128)S(1)}) custom-call(s32[1]{0:T(128)} %bitcast.25.pos, bf16[4,96,256]{2,1,0:T(8,128)(2,1)S(1)} %copy-done.20, bf16[4,96,256]{2,1,0:T(8,128)(2,1)S(1)} %collective-permute-done.2.refs_1_, bf16[4,96,256]{2,1,0:T(8,128)(2,1)S(1)} %collective-permute-done.3.refs_2_, ...), custom_call_target="tpu_custom_call" | custom-call | flops 5765000192 | bytes 1 | tf_op jit(solution)/shard_map/pack_first/pallas_call | solution.py:342
  58.2 1.2 pack_points.24
  59.4 1.1 pack_points.26.refs_1_
  60.5 0.0 collective-permute-done.7.refs_4_
  60.5 1.2 collective-permute-start.9
  61.7 0.0 collective-permute-done.5.refs_2_
  61.7 0.6 collective-permute-start.10
  62.3 0.0 collective-permute-done.14.refs_7_
  62.3 2.5 %collective-permute-done.15.refs_8_ = bf16[3,192,128]{2,1,0:T(8,128)(2,1)S(1)} collective-permute-done((bf16[3,192,128]{2,1,0:T(8,128)(2,1)S(1)}, bf16[3,192,128]{2,1,0:T(8,128)(2,1)S(1)}, u32[]{:S(2)}, u32[]{:S(2)}) %collective-permute-start.15) | collective-permute-done | bytes 147488 | tf_op jit(solution)/shard_map/ppermute | solution.py:502
  64.8 1.9 %collective-permute-done.8.refs_6_ = bf16[6,192,128]{2,1,0:T(8,128)(2,1)S(1)} collective-permute-done((bf16[6,192,128]{2,1,0:T(8,128)(2,1)S(1)}, bf16[6,192,128]{2,1,0:T(8,128)(2,1)S(1)}, u32[]{:S(2)}, u32[]{:S(2)}) %collective-permute-start.8) | collective-permute-done | bytes 294944 | tf_op jit(solution)/shard_map/ppermute | solution.py:502
  66.7 0.1 broadcast_in_dim.8.refs_11_
  66.8 8.4 %source_terms.5 = (bf16[2,3,192,128]{3,2,1,0:T(8,128)(2,1)S(1)}, bf16[2,3,192,128]{3,2,1,0:T(8,128)(2,1)S(1)}, bf16[2,3,192,128]{3,2,1,0:T(8,128)(2,1)S(1)}, bf16[2,3,192,128]{3,2,1,0:T(8,128)(2,1)S(1)}) custom-call(s32[1]{0:T(128)} %bitcast.25.pos, bf16[6,384,128]{2,1,0:T(8,128)(2,1)S(1)} %get-tuple-element.122.refs_0_, ...), custom_call_target="tpu_custom_call" | custom-call | flops 3623878656 | bytes 1 | tf_op jit(solution)/shard_map/source_terms/pallas_call | solution.py:405
  75.2 2.5 %collective-permute-start.16 = (bf16[2,3,192,128]{3,2,1,0:T(8,128)(2,1)S(1)}, bf16[2,3,192,128]{3,2,1,0:T(8,128)(2,1)S(1)}, u32[]{:S(2)}, u32[]{:S(2)}) collective-permute-start(bf16[2,3,192,128]{3,2,1,0:T(8,128)(2,1)S(1)} %get-tuple-element.144), channel_id=1, source_target_pairs={{0,1},{1,0},{2,3},{3,2},{4,5},{5,4},{6,7},{7,6},{8,9},{9,8},{10,11... | collective-permute-start | bytes 884744 | tf_op jit(solution)/shard_map/ppermute | solution.py:502
  77.7 0.4 collective-permute-start.17
  78.2 1.1 collective-permute-start.18
  79.3 9.1 %source_terms.4 = (bf16[2,3,192,128]{3,2,1,0:T(8,128)(2,1)S(1)}, bf16[2,3,192,128]{3,2,1,0:T(8,128)(2,1)}, bf16[2,3,192,128]{3,2,1,0:T(8,128)(2,1)}, bf16[2,3,192,128]{3,2,1,0:T(8,128)(2,1)S(1)}) custom-call(s32[1]{0:T(128)} %bitcast.25.pos, bf16[6,384,128]{2,1,0:T(8,128)(2,1)S(1)} %get-tuple-element.122.refs_0_, ...), custom_call_target="tpu_custom_call" | custom-call | flops 3623878656 | bytes 1 | tf_op jit(solution)/shard_map/source_terms/pallas_call | solution.py:405
  88.3 3.2 %collective-permute-start.11 = (bf16[2,3,192,128]{3,2,1,0:T(8,128)(2,1)}, bf16[2,3,192,128]{3,2,1,0:T(8,128)(2,1)S(1)}, u32[]{:S(2)}, u32[]{:S(2)}) collective-permute-start(bf16[2,3,192,128]{3,2,1,0:T(8,128)(2,1)} %get-tuple-element.138), channel_id=1, source_target_pairs={{0,2},{1,3},{2,0},{3,1},{4,6},{5,7},{6,4},{7,5},{8,10},{9,11},{10,... | collective-permute-start | bytes 884744 | tf_op jit(solution)/shard_map/ppermute | solution.py:502
  91.6 1.1 collective-permute-start.12
  92.7 1.2 slice.39
  93.8 8.0 %pmax.7 = s32[]{:T(128)} all-reduce(s32[]{:T(128)} %bitcast.28), channel_id=1, replica_groups=mesh['tile'=8,'comp'=4] {'tile'}, use_global_device_ids=true, to_apply=%region_0.1 | all-reduce | flops 1 | bytes 8 | tf_op jit(solution)/shard_map/pmax | solution.py:580
  102.5 2.9 %conditional.1 = (bf16[2,2,192,128]{3,2,1,0:T(8,128)(2,1)}, bf16[2,2,192,128]{3,2,1,0:T(8,128)(2,1)}, bf16[2,2,192,128]{3,2,1,0:T(8,128)(2,1)}, bf16[2,2,192,128]{3,2,1,0:T(8,128)(2,1)}) conditional(s32[]{:T(128)} %convert_element_type.6, () %tuple.25, (s32[1]{0:T(128)}, bf16[4,96,256]{2,1,0:T(8,128)(2,1)}, bf16[4,96,256]{2,1,0:T(8,128)(2,1)}, ...), branch_computations={%region_1.2_spmd, %region_2.3_spmd} | conditional | flops 8182984704 | bytes 15929658 | solution.py:582
  102.5 0.7 broadcast.29.clone.2
  103.2 0.7 broadcast.29.clone.1
  104.0 0.7 broadcast.29.clone
  104.7 0.7 broadcast.29
  105.4 0.1 pad_add_fusion.scalars
  105.5 10.8 %collective-permute-done.18.refs_3_ = bf16[2,3,192,128]{3,2,1,0:T(8,128)(2,1)S(1)} collective-permute-done((bf16[2,3,192,128]{3,2,1,0:T(8,128)(2,1)S(1)}, bf16[2,3,192,128]{3,2,1,0:T(8,128)(2,1)S(1)}, u32[]{:S(2)}, u32[]{:S(2)}) %collective-permute-start.18) | collective-permute-done | bytes 294944 | tf_op jit(solution)/shard_map/ppermute | solution.py:502
  116.3 5.8 %unpack.3.refs_3_ = bf16[192,8,1024]{2,1,0:T(8,128)(2,1)} custom-call(s32[2]{0:T(128)S(1)} %pad_add_fusion.scalars, bf16[2,3,192,128]{3,2,1,0:T(8,128)(2,1)S(1)} %get-tuple-element.143.refs_0_, bf16[2,3,192,128]{3,2,1,0:T(8,128)(2,1)S(1)} %collective-permute-done.16.refs_1_, bf16[2,3,192,128]{3,2,1,0:T(8,128)(2,1)S(1)} %collective-permute-done.17.refs_2_, ...), custom_call_target="tpu_custom_call" | custom-call | flops 1 | bytes 1 | tf_op jit(solution)/shard_map/unpack/pallas_call | solution.py:482
  122.1 4.2 %unpack.4.refs_3_ = bf16[192,8,1024]{2,1,0:T(8,128)(2,1)} custom-call(s32[2]{0:T(128)S(1)} %pad_add_fusion.scalars, bf16[2,3,192,128]{3,2,1,0:T(8,128)(2,1)S(1)} %get-tuple-element.136.refs_0_, bf16[2,3,192,128]{3,2,1,0:T(8,128)(2,1)S(1)} %collective-permute-done.13.refs_1_, ...), custom_call_target="tpu_custom_call", output_to_operand_aliasing={{}: (4, {})} | custom-call | flops 1 | bytes 1 | tf_op jit(solution)/shard_map/unpack/pallas_call | solution.py:482
  126.3 4.2 %unpack.5 = bf16[192,8,1024]{2,1,0:T(8,128)(2,1)} custom-call(s32[2]{0:T(128)S(1)} %pad_add_fusion.scalars, bf16[2,3,192,128]{3,2,1,0:T(8,128)(2,1)S(1)} %collective-permute-done.11.refs_0_, bf16[2,3,192,128]{3,2,1,0:T(8,128)(2,1)S(1)} %collective-permute-done.12.refs_1_, ...), custom_call_target="tpu_custom_call", output_to_operand_aliasing={{}: (4, {})} | custom-call | flops 1 | bytes 1 | tf_op jit(solution)/shard_map/unpack/pallas_call | solution.py:482
  (54 shorter events, 0.1 us)
Async XLA Ops:
  0.0 6.9 %copy-start = (f32[16,32]{1,0:T(8,128)S(1)}, f32[16,32]{1,0:T(8,128)}, u32[]{:S(2)}) copy-start(f32[16,32]{1,0:T(8,128)} %param.14) | copy-start | bytes 6148
  0.0 7.0 %copy-start.18 = (f32[2,24]{1,0:T(2,128)S(1)}, f32[2,24]{1,0:T(2,128)}, u32[]{:S(2)}) copy-start(f32[2,24]{1,0:T(2,128)} %constant.28.clone) | copy-start | bytes 580
  0.0 7.1 %copy-start.1 = (bf16[192,8,1024]{2,1,0:T(8,128)(2,1)S(1)}, bf16[192,8,1024]{2,1,0:T(8,128)(2,1)}, u32[]{:S(2)}) copy-start(bf16[192,8,1024]{2,1,0:T(8,128)(2,1)} %refs_0_.5) | copy-start | bytes 9437188
  4.2 15.7 %copy-start.3 = (s32[8,1024]{1,0:T(8,128)S(1)}, s32[8,1024]{1,0:T(8,128)}, u32[]{:S(2)}) copy-start(s32[8,1024]{1,0:T(8,128)} %get-tuple-element.108.refs_1_.refs_3_) | copy-start | bytes 98308
  4.2 21.4 %collective-permute-start = (bf16[49,8,1024]{2,1,0:T(8,128)(2,1)}, bf16[49,8,1024]{2,1,0:T(8,128)(2,1)}, u32[]{:S(2)}, u32[]{:S(2)}) collective-permute-start(bf16[49,8,1024]{2,1,0:T(8,128)(2,1)} %get-tuple-element.112), channel_id=1, source_target_pairs={{0,4},{4,8},{8,12},{12,16},{16,20},{20,24},{24,28},{28,0},{1,5},{5... | collective-permute-start | bytes 2408456 | tf_op jit(solution)/shard_map/ppermute | solution.py:534
  4.2 26.1 %collective-permute-start.1 = (bf16[49,8,1024]{2,1,0:T(8,128)(2,1)}, bf16[49,8,1024]{2,1,0:T(8,128)(2,1)}, u32[]{:S(2)}, u32[]{:S(2)}) collective-permute-start(bf16[49,8,1024]{2,1,0:T(8,128)(2,1)} %get-tuple-element.113), channel_id=1, source_target_pairs={{4,0},{8,4},{12,8},{16,12},{20,16},{24,20},{28,24},{0,28},{5,1},{9... | collective-permute-start | bytes 2408456 | tf_op jit(solution)/shard_map/ppermute | solution.py:534
  7.1 0.8 copy-start.2
  13.1 0.7 copy-start.4
  13.7 0.7 copy-start.5
  16.4 32.4 %collective-permute-start.2 = (bf16[4,96,256]{2,1,0:T(8,128)(2,1)}, bf16[4,96,256]{2,1,0:T(8,128)(2,1)S(1)}, u32[]{:S(2)}, u32[]{:S(2)}) collective-permute-start(bf16[4,96,256]{2,1,0:T(8,128)(2,1)} %copy-done.5), channel_id=1, source_target_pairs={{0,1},{1,0},{2,3},{3,2},{4,5},{5,4},{6,7},{7,6},{8,9},{9,8},{10,11... | collective-permute-start | bytes 589832 | tf_op jit(solution)/shard_map/ppermute | solution.py:502
  16.4 33.6 %collective-permute-start.3 = (bf16[4,96,256]{2,1,0:T(8,128)(2,1)}, bf16[4,96,256]{2,1,0:T(8,128)(2,1)S(1)}, u32[]{:S(2)}, u32[]{:S(2)}) collective-permute-start(bf16[4,96,256]{2,1,0:T(8,128)(2,1)} %copy-done.4), channel_id=1, source_target_pairs={{0,2},{1,3},{2,0},{3,1},{4,6},{5,7},{6,4},{7,5},{8,10},{9,11},{10,... | collective-permute-start | bytes 589832 | tf_op jit(solution)/shard_map/ppermute | solution.py:502
  19.4 31.1 %collective-permute-start.4 = (bf16[4,96,256]{2,1,0:T(8,128)(2,1)S(1)}, bf16[4,96,256]{2,1,0:T(8,128)(2,1)S(1)}, u32[]{:S(2)}, u32[]{:S(2)}) collective-permute-start(bf16[4,96,256]{2,1,0:T(8,128)(2,1)S(1)} %get-tuple-element.121), channel_id=1, source_target_pairs={{0,3},{1,2},{2,1},{3,0},{4,7},{5,6},{6,5},{7,4},{8,11},{9,10},{10,... | collective-permute-start | bytes 589832 | tf_op jit(solution)/shard_map/ppermute | solution.py:502
  24.5 5.8 %copy-start.16 = (bf16[4,96,256]{2,1,0:T(8,128)(2,1)}, bf16[4,96,256]{2,1,0:T(8,128)(2,1)S(1)}, u32[]{:S(2)}) copy-start(bf16[4,96,256]{2,1,0:T(8,128)(2,1)S(1)} %get-tuple-element.129.piece) | copy-start | bytes 589828
  24.5 5.8 %copy-start.15 = (bf16[4,96,256]{2,1,0:T(8,128)(2,1)}, bf16[4,96,256]{2,1,0:T(8,128)(2,1)S(1)}, u32[]{:S(2)}) copy-start(bf16[4,96,256]{2,1,0:T(8,128)(2,1)S(1)} %get-tuple-element.128.piece) | copy-start | bytes 589828
  24.5 17.1 %copy-start.14 = (bf16[4,96,256]{2,1,0:T(8,128)(2,1)}, bf16[4,96,256]{2,1,0:T(8,128)(2,1)S(1)}, u32[]{:S(2)}) copy-start(bf16[4,96,256]{2,1,0:T(8,128)(2,1)S(1)} %get-tuple-element.127.piece) | copy-start | bytes 589828
  24.5 34.8 %copy-start.12 = (bf16[4,96,256]{2,1,0:T(8,128)(2,1)}, bf16[4,96,256]{2,1,0:T(8,128)(2,1)S(1)}, u32[]{:S(2)}) copy-start(bf16[4,96,256]{2,1,0:T(8,128)(2,1)S(1)} %get-tuple-element.125.piece) | copy-start | bytes 589828
  25.7 20.7 %collective-permute-start.6 = (bf16[6,96,128]{2,1,0:T(8,128)(2,1)S(1)}, bf16[6,96,128]{2,1,0:T(8,128)(2,1)S(1)}, u32[]{:S(2)}, u32[]{:S(2)}) collective-permute-start(bf16[6,96,128]{2,1,0:T(8,128)(2,1)S(1)} %pack_points.28), channel_id=1, source_target_pairs={{0,2},{1,3},{2,0},{3,1},{4,6},{5,7},{6,4},{7,5},{8,10},{9,11},{10,... | collective-permute-start | bytes 442376 | tf_op jit(solution)/shard_map/ppermute | solution.py:502
  30.3 23.0 %copy-start.20 = (bf16[4,96,256]{2,1,0:T(8,128)(2,1)S(1)}, bf16[4,96,256]{2,1,0:T(8,128)(2,1)}, u32[]{:S(2)}) copy-start(bf16[4,96,256]{2,1,0:T(8,128)(2,1)} %get-tuple-element.109.refs_0_) | copy-start | bytes 589828
  30.3 23.0 %copy-start.24 = (f32[8,1024]{1,0:T(8,128)S(1)}, f32[8,1024]{1,0:T(8,128)}, u32[]{:S(2)}) copy-start(f32[8,1024]{1,0:T(8,128)} %refs_5_.1) | copy-start | bytes 98308
  30.3 23.0 %copy-start.25 = (f32[8,1024]{1,0:T(8,128)S(1)}, f32[8,1024]{1,0:T(8,128)}, u32[]{:S(2)}) copy-start(f32[8,1024]{1,0:T(8,128)} %refs_6_.1) | copy-start | bytes 98308
  30.4 30.1 %collective-permute-start.7 = (bf16[6,96,128]{2,1,0:T(8,128)(2,1)S(1)}, bf16[6,96,128]{2,1,0:T(8,128)(2,1)S(1)}, u32[]{:S(2)}, u32[]{:S(2)}) collective-permute-start(bf16[6,96,128]{2,1,0:T(8,128)(2,1)S(1)} %pack_points.29), channel_id=1, source_target_pairs={{0,3},{1,2},{2,1},{3,0},{4,7},{5,6},{6,5},{7,4},{8,11},{9,10},{10,... | collective-permute-start | bytes 442376 | tf_op jit(solution)/shard_map/ppermute | solution.py:502
  41.6 8.9 %copy-start.9 = (bf16[4,192,256]{2,1,0:T(8,128)(2,1)}, bf16[4,192,256]{2,1,0:T(8,128)(2,1)S(1)}, u32[]{:S(2)}) copy-start(bf16[4,192,256]{2,1,0:T(8,128)(2,1)S(1)} %get-tuple-element.124.piece) | copy-start | bytes 1179652
  41.6 16.5 %copy-start.8 = (bf16[4,192,256]{2,1,0:T(8,128)(2,1)}, bf16[4,192,256]{2,1,0:T(8,128)(2,1)S(1)}, u32[]{:S(2)}) copy-start(bf16[4,192,256]{2,1,0:T(8,128)(2,1)S(1)} %get-tuple-element.114.piece) | copy-start | bytes 1179652
  41.7 16.5 %copy-start.10 = (bf16[4,192,256]{2,1,0:T(8,128)(2,1)}, bf16[4,192,256]{2,1,0:T(8,128)(2,1)S(1)}, u32[]{:S(2)}) copy-start(bf16[4,192,256]{2,1,0:T(8,128)(2,1)S(1)} %get-tuple-element.131.piece) | copy-start | bytes 1179652
  41.7 16.5 %copy-start.11 = (bf16[4,192,256]{2,1,0:T(8,128)(2,1)}, bf16[4,192,256]{2,1,0:T(8,128)(2,1)S(1)}, u32[]{:S(2)}) copy-start(bf16[4,192,256]{2,1,0:T(8,128)(2,1)S(1)} %get-tuple-element.133.piece) | copy-start | bytes 1179652
  46.4 15.3 %collective-permute-start.5 = (bf16[6,96,128]{2,1,0:T(8,128)(2,1)S(1)}, bf16[6,96,128]{2,1,0:T(8,128)(2,1)S(1)}, u32[]{:S(2)}, u32[]{:S(2)}) collective-permute-start(bf16[6,96,128]{2,1,0:T(8,128)(2,1)S(1)} %pack_points.27), channel_id=1, source_target_pairs={{0,1},{1,0},{2,3},{3,2},{4,5},{5,4},{6,7},{7,6},{8,9},{9,8},{10,11... | collective-permute-start | bytes 442376 | tf_op jit(solution)/shard_map/ppermute | solution.py:502
  48.8 9.3 %copy-start.21 = (bf16[4,96,256]{2,1,0:T(8,128)(2,1)}, bf16[4,96,256]{2,1,0:T(8,128)(2,1)S(1)}, u32[]{:S(2)}) copy-start(bf16[4,96,256]{2,1,0:T(8,128)(2,1)S(1)} %collective-permute-done.2.refs_1_) | copy-start | bytes 589828
  48.8 13.5 %collective-permute-start.14 = (bf16[3,192,128]{2,1,0:T(8,128)(2,1)S(1)}, bf16[3,192,128]{2,1,0:T(8,128)(2,1)S(1)}, u32[]{:S(2)}, u32[]{:S(2)}) collective-permute-start(bf16[3,192,128]{2,1,0:T(8,128)(2,1)S(1)} %get-tuple-element.141), channel_id=1, source_target_pairs={{0,2},{1,3},{2,0},{3,1},{4,6},{5,7},{6,4},{7,5},{8,10},{9,11},{10,... | collective-permute-start | bytes 442376 | tf_op jit(solution)/shard_map/ppermute | solution.py:502
  50.0 8.2 %copy-start.22 = (bf16[4,96,256]{2,1,0:T(8,128)(2,1)}, bf16[4,96,256]{2,1,0:T(8,128)(2,1)S(1)}, u32[]{:S(2)}) copy-start(bf16[4,96,256]{2,1,0:T(8,128)(2,1)S(1)} %collective-permute-done.3.refs_2_) | copy-start | bytes 589828
  50.0 16.8 %copy-start.17 = (f32[2,24]{1,0:T(2,128)S(1)}, f32[2,24]{1,0:T(2,128)}, u32[]{:S(2)}) copy-start(f32[2,24]{1,0:T(2,128)} %constant.29.clone) | copy-start | bytes 580
  50.0 16.8 %copy-start.19 = (bf16[768,768]{1,0:T(8,128)(2,1)S(1)}, bf16[768,768]{1,0:T(8,128)(2,1)}, u32[]{:S(2)}) copy-start(bf16[768,768]{1,0:T(8,128)(2,1)} %refs_10_.3) | copy-start | bytes 3538948
  50.0 14.9 %collective-permute-start.15 = (bf16[3,192,128]{2,1,0:T(8,128)(2,1)S(1)}, bf16[3,192,128]{2,1,0:T(8,128)(2,1)S(1)}, u32[]{:S(2)}, u32[]{:S(2)}) collective-permute-start(bf16[3,192,128]{2,1,0:T(8,128)(2,1)S(1)} %get-tuple-element.142), channel_id=1, source_target_pairs={{0,3},{1,2},{2,1},{3,0},{4,7},{5,6},{6,5},{7,4},{8,11},{9,10},{10,... | collective-permute-start | bytes 442376 | tf_op jit(solution)/shard_map/ppermute | solution.py:502
  50.6 7.6 %copy-start.23 = (bf16[4,96,256]{2,1,0:T(8,128)(2,1)}, bf16[4,96,256]{2,1,0:T(8,128)(2,1)S(1)}, u32[]{:S(2)}) copy-start(bf16[4,96,256]{2,1,0:T(8,128)(2,1)S(1)} %collective-permute-done.4.refs_3_) | copy-start | bytes 589828
  50.6 16.1 %collective-permute-start.8 = (bf16[6,192,128]{2,1,0:T(8,128)(2,1)S(1)}, bf16[6,192,128]{2,1,0:T(8,128)(2,1)S(1)}, u32[]{:S(2)}, u32[]{:S(2)}) collective-permute-start(bf16[6,192,128]{2,1,0:T(8,128)(2,1)S(1)} %pack_points.25), channel_id=1, source_target_pairs={{0,1},{1,0},{2,3},{3,2},{4,5},{5,4},{6,7},{7,6},{8,9},{9,8},{10,11... | collective-permute-start | bytes 884744 | tf_op jit(solution)/shard_map/ppermute | solution.py:502
  60.5 18.8 %collective-permute-start.9 = (bf16[3,192,128]{2,1,0:T(8,128)(2,1)S(1)}, bf16[3,192,128]{2,1,0:T(8,128)(2,1)S(1)}, u32[]{:S(2)}, u32[]{:S(2)}) collective-permute-start(bf16[3,192,128]{2,1,0:T(8,128)(2,1)S(1)} %get-tuple-element.132), channel_id=1, source_target_pairs={{0,2},{1,3},{2,0},{3,1},{4,6},{5,7},{6,4},{7,5},{8,10},{9,11},{10,... | collective-permute-start | bytes 442376 | tf_op jit(solution)/shard_map/ppermute | solution.py:502
  61.7 17.6 %collective-permute-start.10 = (bf16[3,192,128]{2,1,0:T(8,128)(2,1)S(1)}, bf16[3,192,128]{2,1,0:T(8,128)(2,1)S(1)}, u32[]{:S(2)}, u32[]{:S(2)}) collective-permute-start(bf16[3,192,128]{2,1,0:T(8,128)(2,1)S(1)} %get-tuple-element.134), channel_id=1, source_target_pairs={{0,3},{1,2},{2,1},{3,0},{4,7},{5,6},{6,5},{7,4},{8,11},{9,10},{10,... | collective-permute-start | bytes 442376 | tf_op jit(solution)/shard_map/ppermute | solution.py:502
  75.2 16.4 %collective-permute-start.16 = (bf16[2,3,192,128]{3,2,1,0:T(8,128)(2,1)S(1)}, bf16[2,3,192,128]{3,2,1,0:T(8,128)(2,1)S(1)}, u32[]{:S(2)}, u32[]{:S(2)}) collective-permute-start(bf16[2,3,192,128]{3,2,1,0:T(8,128)(2,1)S(1)} %get-tuple-element.144), channel_id=1, source_target_pairs={{0,1},{1,0},{2,3},{3,2},{4,5},{5,4},{6,7},{7,6},{8,9},{9,8},{10,11... | collective-permute-start | bytes 884744 | tf_op jit(solution)/shard_map/ppermute | solution.py:502
  77.7 27.7 %collective-permute-start.17 = (bf16[2,3,192,128]{3,2,1,0:T(8,128)(2,1)S(1)}, bf16[2,3,192,128]{3,2,1,0:T(8,128)(2,1)S(1)}, u32[]{:S(2)}, u32[]{:S(2)}) collective-permute-start(bf16[2,3,192,128]{3,2,1,0:T(8,128)(2,1)S(1)} %get-tuple-element.145), channel_id=1, source_target_pairs={{0,2},{1,3},{2,0},{3,1},{4,6},{5,7},{6,4},{7,5},{8,10},{9,11},{10,... | collective-permute-start | bytes 884744 | tf_op jit(solution)/shard_map/ppermute | solution.py:502
  78.2 38.1 %collective-permute-start.18 = (bf16[2,3,192,128]{3,2,1,0:T(8,128)(2,1)S(1)}, bf16[2,3,192,128]{3,2,1,0:T(8,128)(2,1)S(1)}, u32[]{:S(2)}, u32[]{:S(2)}) collective-permute-start(bf16[2,3,192,128]{3,2,1,0:T(8,128)(2,1)S(1)} %get-tuple-element.146), channel_id=1, source_target_pairs={{0,3},{1,2},{2,1},{3,0},{4,7},{5,6},{6,5},{7,4},{8,11},{9,10},{10,... | collective-permute-start | bytes 884744 | tf_op jit(solution)/shard_map/ppermute | solution.py:502
  79.3 23.2 %copy-start.13 = (bf16[4,96,256]{2,1,0:T(8,128)(2,1)S(1)}, bf16[4,96,256]{2,1,0:T(8,128)(2,1)}, u32[]{:S(2)}) copy-start(bf16[4,96,256]{2,1,0:T(8,128)(2,1)} %copy-done.12) | copy-start | bytes 589828
  88.3 38.0 %collective-permute-start.11 = (bf16[2,3,192,128]{3,2,1,0:T(8,128)(2,1)}, bf16[2,3,192,128]{3,2,1,0:T(8,128)(2,1)S(1)}, u32[]{:S(2)}, u32[]{:S(2)}) collective-permute-start(bf16[2,3,192,128]{3,2,1,0:T(8,128)(2,1)} %get-tuple-element.138), channel_id=1, source_target_pairs={{0,2},{1,3},{2,0},{3,1},{4,6},{5,7},{6,4},{7,5},{8,10},{9,11},{10,... | collective-permute-start | bytes 884744 | tf_op jit(solution)/shard_map/ppermute | solution.py:502
  91.5 30.6 %collective-permute-start.13 = (bf16[2,3,192,128]{3,2,1,0:T(8,128)(2,1)}, bf16[2,3,192,128]{3,2,1,0:T(8,128)(2,1)S(1)}, u32[]{:S(2)}, u32[]{:S(2)}) collective-permute-start(bf16[2,3,192,128]{3,2,1,0:T(8,128)(2,1)} %get-tuple-element.140), channel_id=1, source_target_pairs={{0,1},{1,0},{2,3},{3,2},{4,5},{5,4},{6,7},{7,6},{8,9},{9,8},{10,11... | collective-permute-start | bytes 884744 | tf_op jit(solution)/shard_map/ppermute | solution.py:502
  91.6 34.8 %collective-permute-start.12 = (bf16[2,3,192,128]{3,2,1,0:T(8,128)(2,1)S(1)}, bf16[2,3,192,128]{3,2,1,0:T(8,128)(2,1)S(1)}, u32[]{:S(2)}, u32[]{:S(2)}) collective-permute-start(bf16[2,3,192,128]{3,2,1,0:T(8,128)(2,1)S(1)} %get-tuple-element.139), channel_id=1, source_target_pairs={{0,3},{1,2},{2,1},{3,0},{4,7},{5,6},{6,5},{7,4},{8,11},{9,10},{10,... | collective-permute-start | bytes 884744 | tf_op jit(solution)/shard_map/ppermute | solution.py:502
